TPU v7x, 32 devices: a whole 2x2x4 slice. The times are simulated.
32 devices in a mesh: groups: 2 (over x), ctx: 16 (over z, y, core).
Axes of the slice: x: 2, y: 2, z: 4, core: 2. Of those that a mesh axis runs over, the one named last changes fastest.
Arguments:
- queries: bfloat16 [128, 8192], P(('groups', 'ctx')), parts along dimension 0
- cache_keys: bfloat16 [49152, 512], P(('groups', 'ctx')), parts along dimension 0
- cached_value_rows: bfloat16 [49152, 512], P(('groups', 'ctx')), parts along dimension 0, may hold values from -5 to 5
- new_keys: bfloat16 [128, 512], P(('groups', 'ctx')), parts along dimension 0
- prompt_value_rows: bfloat16 [128, 512], P(('groups', 'ctx')), parts along dimension 0, may hold values from -5 to 5
- cache_len: int32 [32], P(('groups', 'ctx')), parts along dimension 0, may hold values from 1 to 1536, 15360 in all
- prompt_start: int32 [2], P('groups'), parts along dimension 0, may hold values from 7680 to 15360
Outputs:
- attended: bfloat16 [128, 8192], P(('groups', 'ctx')), parts along dimension 0
There are 2 independent parts, one for each index of `groups`. A program takes and returns all parts, laid end to end along the dimension named above; each array names one. Nothing has to cross between parts.
Inputs may be any that keep to these rules, and one draw needn't show every extreme that they name: cache_len sums to 15360; some shard is full.
All inputs are finite; a program needn't handle non-finite values.
Results may differ from a plain program's by a relative error of at most 0.0024.
Values may be sent and summed in bfloat16 or wider, within the bound.
No kernel may reach another device: no remote copies, remote signals or barrier semaphores. Data moves between devices by JAX's collectives and lax.ppermute only.
A program may use at most 64 MiB of HBM per device.

v0:
```python
import math

import jax
import jax.numpy as jnp
from jax import lax
from jax.sharding import PartitionSpec as P

KEY_VALUE_HEADS = 4


floor_score = -1e30


def prefix(value, axis, combine, identity):
    count, mine = (lax.axis_size(axis), lax.axis_index(axis))
    everything = lax.all_gather(value, axis)
    start = jnp.broadcast_to(jnp.asarray(identity, value.dtype), value.shape)

    def lap(k, before):
        reached = k < mine
        new = combine(before, everything[k])
        return jnp.where(reached, new, before)

    return lax.fori_loop(0, count, lap, start)


def add_lengths(earlier, later):
    return earlier + later


def shard_attention(queries, key_rows, value_rows, visible_mask, key_value_heads):
    count = queries.shape[0]
    length = key_rows.shape[0]
    head_dim = key_rows.shape[1] // key_value_heads
    heads = queries.shape[1] // head_dim
    group = heads // key_value_heads
    block_rows = min(count, max(1, 1024 // heads))
    blocks = count // block_rows
    grouped = queries.reshape(blocks, block_rows, key_value_heads, group, head_dim)
    key_heads = key_rows.reshape(length, key_value_heads, head_dim)
    value_heads = value_rows.reshape(length, key_value_heads, head_dim)
    masks = visible_mask.reshape(blocks, block_rows, length)
    scale = 1.0 / math.sqrt(head_dim)

    def one_block(inputs):
        query_block, mask_block = inputs
        scores = (
            jnp.einsum("qhgd,khd->qhgk", query_block, key_heads, preferred_element_type=jnp.float32)
            * scale
        )
        allowed = mask_block[:, None, None, :]
        top = jnp.max(jnp.where(allowed, scores, floor_score), axis=3)
        weights = jnp.where(allowed, jnp.exp(scores - top[..., None]), 0.0)
        total = jnp.sum(weights, axis=3)
        summed = jnp.einsum(
            "qhgk,khd->qhgd",
            weights.astype(jnp.bfloat16),
            value_heads,
            preferred_element_type=jnp.float32,
        )
        return (top, total, summed)

    top_scores, total_weights, sum_rows = lax.map(one_block, (grouped, masks))
    return (
        top_scores.reshape(count, heads),
        total_weights.reshape(count, heads),
        sum_rows.reshape(count, heads, head_dim),
    )


def combine(parts):
    top_parts, total_parts, sum_parts = parts
    best = jnp.max(top_parts, axis=0)
    factor = jnp.exp(top_parts - best)
    denom = jnp.sum(total_parts * factor, axis=0)
    numer = jnp.sum(sum_parts * factor[..., None], axis=0)
    return (numer / denom[..., None]).astype(jnp.bfloat16)


def per_device(
    queries, cache_keys, cached_value_rows, new_keys, prompt_value_rows, cache_len, prompt_start
):
    width = lax.axis_size("ctx")
    position = lax.axis_index("ctx")
    own_rows = queries.shape[0]
    slot_count = cache_keys.shape[0]
    before = prefix(cache_len, "ctx", add_lengths, jnp.zeros_like(cache_len))[0]
    slot_ids = jnp.arange(slot_count, dtype=jnp.int32)
    live_slots = (slot_ids < cache_len[0]) & (before + slot_ids < prompt_start[0])
    every_shard = lax.all_gather(queries, "ctx", axis=0, tiled=True)
    total_rows = every_shard.shape[0]
    row_ids = jnp.arange(total_rows, dtype=jnp.int32)
    fresh_ids = position * own_rows + jnp.arange(own_rows, dtype=jnp.int32)
    causal = fresh_ids[None, :] <= row_ids[:, None]
    visible_mask = jnp.concatenate(
        [jnp.broadcast_to(live_slots[None, :], (total_rows, slot_count)), causal], axis=1
    )
    key_rows = jnp.concatenate([cache_keys, new_keys], axis=0)
    value_rows = jnp.concatenate([cached_value_rows, prompt_value_rows], axis=0)
    top_scores, total_weights, sum_rows = shard_attention(
        every_shard, key_rows, value_rows, visible_mask, KEY_VALUE_HEADS
    )
    heads = top_scores.shape[1]
    head_dim = sum_rows.shape[2]
    merged = combine(
        (
            lax.all_to_all(
                top_scores.reshape(width, own_rows, heads),
                "ctx",
                split_axis=0,
                concat_axis=0,
                tiled=True,
            ),
            lax.all_to_all(
                total_weights.reshape(width, own_rows, heads),
                "ctx",
                split_axis=0,
                concat_axis=0,
                tiled=True,
            ),
            lax.all_to_all(
                sum_rows.reshape(width, own_rows, heads, head_dim),
                "ctx",
                split_axis=0,
                concat_axis=0,
                tiled=True,
            ),
        )
    )
    return merged.reshape(own_rows, heads * head_dim)


def solution(mesh):
    return jax.shard_map(
        per_device,
        mesh=mesh,
        in_specs=(
            P(("groups", "ctx"), None),
            P(("groups", "ctx"), None),
            P(("groups", "ctx"), None),
            P(("groups", "ctx"), None),
            P(("groups", "ctx"), None),
            P(("groups", "ctx")),
            P("groups"),
        ),
        out_specs=P(("groups", "ctx"), None),
        check_vma=False,
    )
```

profile of v0, /device:TPU:15, one launch (start us, length us, event | category | flops | bytes accessed | tf_op | source)
XLA Modules:
  0.0 159.7 jit_solution(15347070432678105187)
XLA Ops:
  6.5 0.7 all-gather.4.cloned.1.call-update
  7.9 1.3 dynamic-slice
  9.2 0.8 dynamic-update-slice
  10.0 7.9 %all-reduce = s32[16]{0:T(128)S(1)} all-reduce(s32[16]{0:T(128)S(1)} %dynamic-update-slice), channel_id=2, replica_groups=mesh['groups'=2,'ctx'=16] {'ctx'}, use_global_device_ids=true, to_apply=%add | all-reduce | flops 16 | bytes 128
  18.6 1.5 pad_maximum_fusion
  20.9 1.2 copy-done.1
  22.2 1.7 %reshape.58 = bf16[1540,4,128]{2,1,0:T(4,128)(2,1)} reshape(bf16[1540,512]{1,0:T(8,128)(2,1)S(1)} %pad_maximum_fusion.1) | data formatting | bytes 3153920 | tf_op jit(solution)/shard_map/reshape | solution.py:41
  24.0 2.8 %copy.17 = bf16[1540,4,128]{2,0,1:T(8,128)(2,1)} copy(bf16[1540,4,128]{2,1,0:T(4,128)(2,1)} %reshape.58) | data formatting | bytes 3153920 | tf_op jit(solution)/shard_map/while | solution.py:63
  26.7 21.2 %while.27 = (s32[]{:T(128)}, s32[1]{0:T(128)}, s32[]{:T(128)}, s32[16,1]{0,1:T(1,128)S(1)}, s32[]{:T(128)}) while((s32[]{:T(128)}, s32[1]{0:T(128)}, s32[]{:T(128)}, s32[16,1]{0,1:T(1,128)S(1)}, s32[]{:T(128)}) %tuple.59), condition=%wide.region_1.2_spmd, body=%wide.region_0.1_spmd.sunk | while | flops 5 | bytes 115 | solution.py:24
  28.0 0.7 constant_dynamic-slice_fusion.6
  30.7 0.7 constant_dynamic-slice_fusion.6
  32.0 0.7 constant_dynamic-slice_fusion.6
  33.3 0.7 constant_dynamic-slice_fusion.6
  34.7 0.7 constant_dynamic-slice_fusion.6
  36.0 0.7 constant_dynamic-slice_fusion.6
  37.3 0.7 constant_dynamic-slice_fusion.6
  38.6 0.7 constant_dynamic-slice_fusion.6
  40.0 0.7 constant_dynamic-slice_fusion.6
  41.3 0.7 constant_dynamic-slice_fusion.6
  42.6 0.7 constant_dynamic-slice_fusion.6
  48.1 2.1 %reshape.56 = bf16[4,16,4,16,128]{4,3,2,1,0:T(8,128)(2,1)S(1)} reshape(bf16[16,4,8192]{2,1,0:T(4,128)(2,1)} %all-gather.4.cloned.1.call-done) | data formatting | bytes 2097152 | tf_op jit(solution)/shard_map/reshape | solution.py:39
  50.2 25.2 %while.28 = (s32[]{:T(128)}, f32[4,16,4,16]{3,2,1,0:T(4,128)S(1)}, f32[4,16,4,16]{3,2,1,0:T(4,128)S(1)}, f32[4,16,4,16,128]{4,3,2,1,0:T(8,128)}, pred[4,16,1540]...) while((s32[]{:T(128)}, f32[4,16,4,16]{3,2,1,0:T(4,128)S(1)}, ...), condition=%wide.region_5.6_spmd, body=%wide.region_2.5_spmd.sunk | while | flops 824748032 | bytes 30497168 | solution.py:63
  50.3 1.5 fusion.27
  51.8 1.8 %fusion.28 = f32[16,4,16]{2,0,1:T(8,128)S(1)} fusion(f32[4,16,16,1540]{3,2,1,0:T(8,128)S(1)} %get-tuple-element.264, f32[16,4,16]{2,0,1:T(8,128)S(1)} %get-tuple-element.265, pred[16,1540]{1,0:T(8,128)(4,1)S(1)} %dynamic-slice_bitcast_fusion.2), kind=kLoop, calls=%fused_computation.7.clone.1 | loop fusion | flops 6306816 | bytes 6340672 | tf_op jit(solution)/shard_map/while/body/eval_jaxpr/reduce_sum | solution.py:54
  53.6 2.1 %fusion.29 = f32[1,16,4,16,128]{4,3,1,2,0:T(8,128)S(1)} fusion(bf16[1540,4,128]{2,0,1:T(8,128)(2,1)S(1)} %copy-done, f32[4,16,16,1540]{3,2,1,0:T(8,128)S(1)} %get-tuple-element.264, f32[16,4,16]{2,0,1:T(8,128)S(1)} %get-tuple-element.265, pred[16,1540]{1,0:T(8,128)(4,1)S(1)} %dynamic-slice_bitcast_fusion.2), kind=kOutput, calls=%fused_computation.13.clone.1 | convolution fusion | flops 410009600 | bytes 8437824 | tf_op jit(solution)/shard_map/while/body/eval_jaxpr/qhgk,khd->qhgd/dot_general | solution.py:55
  55.7 0.8 copy_dynamic-update-slice_fusion.6
  56.6 1.5 fusion.27
  58.0 1.8 %fusion.28 = f32[16,4,16]{2,0,1:T(8,128)S(1)} fusion(f32[4,16,16,1540]{3,2,1,0:T(8,128)S(1)} %get-tuple-element.264, f32[16,4,16]{2,0,1:T(8,128)S(1)} %get-tuple-element.265, pred[16,1540]{1,0:T(8,128)(4,1)S(1)} %dynamic-slice_bitcast_fusion.2), kind=kLoop, calls=%fused_computation.7.clone.1 | loop fusion | flops 6306816 | bytes 6340672 | tf_op jit(solution)/shard_map/while/body/eval_jaxpr/reduce_sum | solution.py:54
  59.9 2.1 %fusion.29 = f32[1,16,4,16,128]{4,3,1,2,0:T(8,128)S(1)} fusion(bf16[1540,4,128]{2,0,1:T(8,128)(2,1)S(1)} %copy-done, f32[4,16,16,1540]{3,2,1,0:T(8,128)S(1)} %get-tuple-element.264, f32[16,4,16]{2,0,1:T(8,128)S(1)} %get-tuple-element.265, pred[16,1540]{1,0:T(8,128)(4,1)S(1)} %dynamic-slice_bitcast_fusion.2), kind=kOutput, calls=%fused_computation.13.clone.1 | convolution fusion | flops 410009600 | bytes 8437824 | tf_op jit(solution)/shard_map/while/body/eval_jaxpr/qhgk,khd->qhgd/dot_general | solution.py:55
  62.0 0.9 copy_dynamic-update-slice_fusion.6
  62.8 1.5 fusion.27
  64.3 1.8 %fusion.28 = f32[16,4,16]{2,0,1:T(8,128)S(1)} fusion(f32[4,16,16,1540]{3,2,1,0:T(8,128)S(1)} %get-tuple-element.264, f32[16,4,16]{2,0,1:T(8,128)S(1)} %get-tuple-element.265, pred[16,1540]{1,0:T(8,128)(4,1)S(1)} %dynamic-slice_bitcast_fusion.2), kind=kLoop, calls=%fused_computation.7.clone.1 | loop fusion | flops 6306816 | bytes 6340672 | tf_op jit(solution)/shard_map/while/body/eval_jaxpr/reduce_sum | solution.py:54
  66.2 2.1 %fusion.29 = f32[1,16,4,16,128]{4,3,1,2,0:T(8,128)S(1)} fusion(bf16[1540,4,128]{2,0,1:T(8,128)(2,1)S(1)} %copy-done, f32[4,16,16,1540]{3,2,1,0:T(8,128)S(1)} %get-tuple-element.264, f32[16,4,16]{2,0,1:T(8,128)S(1)} %get-tuple-element.265, pred[16,1540]{1,0:T(8,128)(4,1)S(1)} %dynamic-slice_bitcast_fusion.2), kind=kOutput, calls=%fused_computation.13.clone.1 | convolution fusion | flops 410009600 | bytes 8437824 | tf_op jit(solution)/shard_map/while/body/eval_jaxpr/qhgk,khd->qhgd/dot_general | solution.py:55
  68.3 0.9 copy_dynamic-update-slice_fusion.6
  69.1 1.5 fusion.27
  70.6 1.8 %fusion.28 = f32[16,4,16]{2,0,1:T(8,128)S(1)} fusion(f32[4,16,16,1540]{3,2,1,0:T(8,128)S(1)} %get-tuple-element.264, f32[16,4,16]{2,0,1:T(8,128)S(1)} %get-tuple-element.265, pred[16,1540]{1,0:T(8,128)(4,1)S(1)} %dynamic-slice_bitcast_fusion.2), kind=kLoop, calls=%fused_computation.7.clone.1 | loop fusion | flops 6306816 | bytes 6340672 | tf_op jit(solution)/shard_map/while/body/eval_jaxpr/reduce_sum | solution.py:54
  72.5 2.1 %fusion.29 = f32[1,16,4,16,128]{4,3,1,2,0:T(8,128)S(1)} fusion(bf16[1540,4,128]{2,0,1:T(8,128)(2,1)S(1)} %copy-done, f32[4,16,16,1540]{3,2,1,0:T(8,128)S(1)} %get-tuple-element.264, f32[16,4,16]{2,0,1:T(8,128)S(1)} %get-tuple-element.265, pred[16,1540]{1,0:T(8,128)(4,1)S(1)} %dynamic-slice_bitcast_fusion.2), kind=kOutput, calls=%fused_computation.13.clone.1 | convolution fusion | flops 410009600 | bytes 8437824 | tf_op jit(solution)/shard_map/while/body/eval_jaxpr/qhgk,khd->qhgd/dot_general | solution.py:55
  74.6 0.9 copy_dynamic-update-slice_fusion.6
  75.6 0.7 reshape.73
  76.3 8.4 %all-to-all-start.2 = ((f32[16,1,256]{2,1,0:T(1,128)}), f32[16,1,256]{2,1,0:T(1,128)S(1)}, u32[]{:S(2)}, u32[]{:S(2)}) async-start(f32[16,1,256]{2,1,0:T(1,128)} %reshape.73), calls=%async_computation.2 | async-start | bytes 32768 | tf_op jit(solution)/shard_map/all_to_all | solution.py:114
  84.9 3.9 %all-to-all-done.2 = f32[16,1,256]{2,1,0:T(1,128)S(1)} async-done(((f32[16,1,256]{2,1,0:T(1,128)}), f32[16,1,256]{2,1,0:T(1,128)S(1)}, u32[]{:S(2)}, u32[]{:S(2)}) %all-to-all-start.2) | async-done | bytes 16416 | tf_op jit(solution)/shard_map/all_to_all | solution.py:114
  88.8 9.1 %all_to_all.15 = f32[16,1,256]{2,1,0:T(1,128)S(1)} all-to-all(f32[16,1,256]{2,1,0:T(1,128)S(1)} %reshape.71), channel_id=1, replica_groups=mesh['groups'=2,'ctx'=16] {'ctx'}, dimensions={0} | all-to-all | bytes 32768 | tf_op jit(solution)/shard_map/all_to_all | solution.py:107
  97.9 6.0 %all-to-all-start = ((f32[16,4,64,128]{3,2,1,0:T(8,128)}), f32[16,4,64,128]{3,2,1,0:T(8,128)S(1)}, u32[]{:S(2)}, u32[]{:S(2)}) async-start(f32[16,4,64,128]{3,2,1,0:T(8,128)} %bitcast.85), calls=%async_computation | async-start | bytes 4194304 | tf_op jit(solution)/shard_map/all_to_all | solution.py:121
  104.4 0.7 reduce
  105.2 0.7 reduce.1
  106.0 45.3 %all-to-all-done = f32[16,4,64,128]{3,2,1,0:T(8,128)S(1)} async-done(((f32[16,4,64,128]{3,2,1,0:T(8,128)}), f32[16,4,64,128]{3,2,1,0:T(8,128)S(1)}, u32[]{:S(2)}, u32[]{:S(2)}) %all-to-all-start) | async-done | bytes 2097184 | tf_op jit(solution)/shard_map/all_to_all | solution.py:121
  151.4 0.7 multiply_reduce_fusion
  152.2 0.7 copy.41
  (48 shorter events, 5.7 us)
Async XLA Ops:
  6.5 41.5 %all-gather.4.cloned.1.call-start = ((), (), s32[]{:S(2)}) async-start(), calls=%async_computation.3 | async-start | bytes 1114112 | tf_op jit(solution)/shard_map/all_gather | solution.py:90
  20.7 1.4 copy-start.1
  20.7 1.4 copy-start.2
  51.8 1.9 %copy-start = (bf16[1540,4,128]{2,0,1:T(8,128)(2,1)S(1)}, bf16[1540,4,128]{2,0,1:T(8,128)(2,1)}, u32[]{:S(2)}) copy-start(bf16[1540,4,128]{2,0,1:T(8,128)(2,1)} %get-tuple-element.308) | copy-start | bytes 4730884 | tf_op jit(solution)/shard_map/while
  58.0 1.9 %copy-start = (bf16[1540,4,128]{2,0,1:T(8,128)(2,1)S(1)}, bf16[1540,4,128]{2,0,1:T(8,128)(2,1)}, u32[]{:S(2)}) copy-start(bf16[1540,4,128]{2,0,1:T(8,128)(2,1)} %get-tuple-element.308) | copy-start | bytes 4730884 | tf_op jit(solution)/shard_map/while
  64.3 1.9 %copy-start = (bf16[1540,4,128]{2,0,1:T(8,128)(2,1)S(1)}, bf16[1540,4,128]{2,0,1:T(8,128)(2,1)}, u32[]{:S(2)}) copy-start(bf16[1540,4,128]{2,0,1:T(8,128)(2,1)} %get-tuple-element.308) | copy-start | bytes 4730884 | tf_op jit(solution)/shard_map/while
  70.6 1.9 %copy-start = (bf16[1540,4,128]{2,0,1:T(8,128)(2,1)S(1)}, bf16[1540,4,128]{2,0,1:T(8,128)(2,1)}, u32[]{:S(2)}) copy-start(bf16[1540,4,128]{2,0,1:T(8,128)(2,1)} %get-tuple-element.308) | copy-start | bytes 4730884 | tf_op jit(solution)/shard_map/while
  76.3 12.6 %all-to-all-start.2 = ((f32[16,1,256]{2,1,0:T(1,128)}), f32[16,1,256]{2,1,0:T(1,128)S(1)}, u32[]{:S(2)}, u32[]{:S(2)}) async-start(f32[16,1,256]{2,1,0:T(1,128)} %reshape.73), calls=%async_computation.2 | async-start | bytes 32768 | tf_op jit(solution)/shard_map/all_to_all | solution.py:114
  97.9 53.5 %all-to-all-start = ((f32[16,4,64,128]{3,2,1,0:T(8,128)}), f32[16,4,64,128]{3,2,1,0:T(8,128)S(1)}, u32[]{:S(2)}, u32[]{:S(2)}) async-start(f32[16,4,64,128]{3,2,1,0:T(8,128)} %bitcast.85), calls=%async_computation | async-start | bytes 4194304 | tf_op jit(solution)/shard_map/all_to_all | solution.py:121
Sparse Core Ops, SparseCore 0:
  9.5 38.1 all-gather.3
where the time goes:
time: 160 us
  waiting for transfers between devices  50 us (31%)
  local copies, waits for them, and re-layouts  27.2 us (17%)
  blocking collectives  16.9 us (11%)
  between operations  14.8 us (9%)
  starting transfers between devices  14.4 us (9%)
  matrix products  14.1 us (9%)
  other arithmetic  11.3 us (7%)
  loops' own time  10.9 us (7%)
    all_to_all x1, waiting for transfers between devices, per_device(): lax.all_to_all(sum_rows.reshape(width, own_rows, heads, head_dim), 'ctx',...  45.3 us
    another operation x1, loops' own time, prefix(): return lax.fori_loop(0, count, lap, start)  10.7 us
    dynamic_slice x16, local copies, waits for them, and re-layouts, lap(): new = combine(before, everything[k])  10.4 us
    all_to_all x1, blocking collectives, per_device(): lax.all_to_all(top_scores.reshape(width, own_rows, heads), 'ctx', split_a...  9.06 us
    all_to_all x1, starting transfers between devices, per_device(): lax.all_to_all(total_weights.reshape(width, own_rows, heads), 'ctx', spli...  8.41 us
    dot_general x4, matrix products, one_block(): jnp.einsum('qhgk,khd->qhgd', weights.astype(jnp.bfloat16), value_heads, p...  8.25 us
    unnamed x1, blocking collectives  7.88 us
    reduce_sum x4, other arithmetic, one_block(): total = jnp.sum(weights, axis=3)  7.24 us
  transfers between devices with their start and end apart: 3, of which 2 were waited for; matrix products, arithmetic and copies ran while one was open for 14% of the time, Pallas kernels for 0%

commit v1 on v0

v1 whole, which is shorter than its diff:
```python
import functools
import math

import jax
import jax.numpy as jnp
from jax import lax
from jax.experimental import pallas as pl
from jax.experimental.pallas import tpu as pltpu
from jax.sharding import PartitionSpec as P

KEY_VALUE_HEADS = 4
LANES = 128
CORES = 2
FLOOR = -1e30
KEY_TILE = 256
STEP = 2.0**15
F32 = jnp.float32
BF16 = jnp.bfloat16
I16 = jnp.int16
I32 = jnp.int32


def lane_ids(rows):
    return lax.broadcasted_iota(I32, (rows, LANES), 1)


def row_ids(rows):
    return lax.broadcasted_iota(I32, (rows, LANES), 0)


def encode_stats(top, total, exponent, heads):
    size = jnp.abs(top)
    level = jnp.zeros_like(top)
    scaled = top
    for i in range(1, 9):
        above = size >= STEP**i
        level = level + jnp.where(above, 1.0, 0.0)
        scaled = scaled * jnp.where(above, 1.0 / STEP, 1.0)
    a = jnp.floor(scaled)
    rest = (scaled - a) * STEP
    b = jnp.floor(rest)
    c = jnp.floor((rest - b) * STEP)
    scaled_log = jnp.log2(total) * 1024.0
    la = jnp.floor(scaled_log)
    lb = jnp.floor((scaled_log - la) * STEP)
    live = lane_ids(top.shape[0]) < heads

    def place(parts):
        out = None
        for i, part in enumerate(parts):
            part = jnp.where(live, part, 0.0)
            part = part if i == 0 else pltpu.roll(part, i * heads, 1)
            out = part if out is None else out + part
        return out.astype(I32).astype(I16)

    return place([level, a, b, c]), place([exponent, la, lb])


def decode_stats(first, second, heads):
    first = first.astype(I32).astype(F32)
    second = second.astype(I32).astype(F32)

    def part(plane, i):
        return plane if i == 0 else pltpu.roll(plane, LANES - i * heads, 1)

    level = part(first, 0)
    top = part(first, 1) + (part(first, 2) + part(first, 3) * (1.0 / STEP)) * (1.0 / STEP)
    for i in range(1, 9):
        top = top * jnp.where(level >= i, STEP, 1.0)
    total = jnp.exp2((part(second, 1) + part(second, 2) * (1.0 / STEP)) * (1.0 / 1024.0))
    return top, total, part(second, 0)


def exponent_of(peak):
    return jnp.clip(jnp.floor(jnp.log2(jnp.maximum(peak, 1e-30))) + 1.0, -100.0, 15.0)


def to_fixed(rows, exponent):
    return jnp.clip(jnp.floor(rows * jnp.exp2(15.0 - exponent) + 0.5), -32767.0, 32767.0).astype(I32).astype(I16)


def pack_kernel(info, length, queries, new_keys, new_values, mine, other):
    rows = queries.shape[0]
    half, half_kv = queries.shape[1] // CORES, new_keys.shape[1] // CORES
    core = info[0]
    lane = lane_ids(rows)
    count = jnp.full((rows, LANES), length[0], I32)
    coded = jnp.where(lane == 0, count // LANES, jnp.where(lane == 1, count % LANES, 0))
    coded = coded.astype(F32).astype(BF16)
    for out, side in ((mine, core), (other, 1 - core)):
        out[:, :half] = queries[:, pl.ds(pl.multiple_of(side * half, LANES), half)]
        out[:, half : half + LANES] = coded
        at = half + LANES
        out[:, at : at + half_kv] = new_keys[:, pl.ds(pl.multiple_of(side * half_kv, LANES), half_kv)]
        at = at + half_kv
        out[:, at : at + half_kv] = new_values[:, pl.ds(pl.multiple_of(side * half_kv, LANES), half_kv)]


def pack(info, length, queries, new_keys, new_values):
    rows = queries.shape[0]
    wide = queries.shape[1] // CORES + LANES + 2 * new_keys.shape[1] // CORES
    shape = jax.ShapeDtypeStruct((rows, wide), BF16)
    smem = pl.BlockSpec(memory_space=pltpu.SMEM)
    vmem = pl.BlockSpec(memory_space=pltpu.VMEM)
    return pl.pallas_call(
        pack_kernel,
        out_shape=(shape, shape),
        in_specs=[smem, smem, vmem, vmem, vmem],
        out_specs=(vmem, vmem),
    )(info, length, queries, new_keys, new_values)


def chip_offsets(info, block, stages):
    off = jnp.zeros_like(block)
    for i in range(stages):
        off = off ^ jnp.where((block >> i) & 1 == 1, info[4 + i], 0)
    return off


def attend_kernel(
    sizes, info, queries, extra_low, extra_high, fresh, keys_a, keys_b, values_a, values_b, out, top_plane,
    total_plane, scale_plane, scores, peak, mass, sums
):
    own_rows, stages, first_block, group, kv_heads, slots = sizes
    chip_rows = CORES * own_rows
    tokens = queries.shape[0]
    head = pl.program_id(1)
    core, chip, me, start = info[0], info[1], info[2], info[3]
    factor = math.log2(math.e) / math.sqrt(LANES)

    def token_parts(rows, base_row):
        row = row_ids(rows) + base_row
        place = chip ^ chip_offsets(info, row // chip_rows, stages)
        inside = row % chip_rows
        return place * CORES + (core ^ (inside // own_rows)), inside % own_rows

    all_low, all_high = extra_low.shape[0], extra_high.shape[0]
    before = [0.0, 0.0]
    length = [0.0, 0.0]
    for ref, rows, base in ((extra_low, all_low, 0), (extra_high, all_high, all_low)):
        shard, inner = token_parts(rows, base)
        coded = ref[...].astype(F32)
        lane = lane_ids(rows)
        counts = jnp.where(lane == 0, coded * float(LANES), jnp.where(lane == 1, coded, 0.0))
        counts = jnp.where(inner == 0, counts, 0.0)
        for s, holder in enumerate((me, me ^ 1)):
            before[s] = before[s] + jnp.sum(jnp.where(shard < holder, counts, 0.0))
            length[s] = length[s] + jnp.sum(jnp.where(shard == holder, counts, 0.0))
    limits = []
    for s in range(2):
        limit = jnp.minimum(length[s].astype(I32), start - before[s].astype(I32))
        limits.append(jnp.clip(limit, 0, slots))

    first = head * group
    wide = group * LANES
    q_rows = queries[:, pl.ds(pl.multiple_of(first * LANES, LANES), wide)]
    q = jnp.concatenate([q_rows[:, g * LANES : (g + 1) * LANES] for g in range(group)], axis=0)
    rows = group * tokens
    nt = (((1,), (1,)), ((), ()))

    pad = jnp.zeros((LANES - chip_rows, LANES), F32)
    half_kv = fresh.shape[1] // 2
    at = pl.multiple_of(head * LANES, LANES)
    fresh_keys = jnp.concatenate([fresh[:, pl.ds(at, LANES)].astype(F32), pad], 0).astype(BF16)
    fresh_values = jnp.concatenate(
        [fresh[:, pl.ds(pl.multiple_of(half_kv + head * LANES, LANES), LANES)].astype(F32), pad], 0
    ).astype(BF16)
    fresh_scores = lax.dot_general(q, fresh_keys, nt, preferred_element_type=F32)
    shard, inner = token_parts(tokens, first_block * chip_rows + pl.program_id(0) * tokens)
    token = shard * own_rows + inner
    lane = lane_ids(tokens)

    parts = []
    for s, (keys, values, holder) in enumerate(((keys_a, values_a, me), (keys_b, values_b, me ^ 1))):
        limit = limits[s]
        whole = limit // KEY_TILE
        tail = limit - whole * KEY_TILE
        in_shard = (lane >= s * own_rows) & (lane < (s + 1) * own_rows)
        seen = in_shard & (holder * own_rows + lane - s * own_rows <= token)
        seen = jnp.concatenate([seen.astype(F32)] * group, axis=0) > 0.5
        peak[...] = jnp.where(seen, fresh_scores, FLOOR)

        def score(j):
            at = pl.multiple_of(j * KEY_TILE, KEY_TILE)
            return lax.dot_general(q, keys[pl.ds(at, KEY_TILE), :], nt, preferred_element_type=F32)

        def raise_peak(tile):
            best = peak[...]
            for i in range(KEY_TILE // LANES):
                best = jnp.maximum(best, tile[:, i * LANES : (i + 1) * LANES])
            peak[...] = best

        def first_pass(j, carry):
            tile = score(j)
            scores[j] = tile
            raise_peak(tile)
            return carry

        lax.fori_loop(0, whole, first_pass, 0)
        slot = lax.broadcasted_iota(I32, (rows, KEY_TILE), 1)

        @pl.when(tail > 0)
        def _():
            tile = jnp.where(slot < tail, score(whole), FLOOR)
            scores[whole] = tile
            raise_peak(tile)

        top = jnp.max(peak[...], axis=1, keepdims=True)
        weight = jnp.where(seen, jnp.exp2((fresh_scores - top) * factor), 0.0)
        mass[...] = weight
        sums[s] = lax.dot_general(
            weight.astype(BF16), fresh_values, (((1,), (0,)), ((), ())), preferred_element_type=F32
        )

        def add(j, weight):
            more = mass[...]
            for i in range(KEY_TILE // LANES):
                more = more + weight[:, i * LANES : (i + 1) * LANES]
            mass[...] = more
            at = pl.multiple_of(j * KEY_TILE, KEY_TILE)
            sums[s] += lax.dot_general(
                weight.astype(BF16), values[pl.ds(at, KEY_TILE), :], (((1,), (0,)), ((), ())),
                preferred_element_type=F32,
            )

        def second_pass(j, carry):
            add(j, jnp.exp2((scores[j] - top) * factor))
            return carry

        lax.fori_loop(0, whole, second_pass, 0)

        @pl.when(tail > 0)
        def _():
            add(whole, jnp.where(slot < tail, jnp.exp2((scores[whole] - top) * factor), 0.0))

        parts.append((top, jnp.sum(mass[...], axis=1, keepdims=True)))

    (top_a, mass_a), (top_b, mass_b) = parts
    top = jnp.maximum(top_a, top_b)
    scale_a = jnp.exp2((top_a - top) * factor)
    scale_b = jnp.exp2((top_b - top) * factor)
    total = jnp.maximum(mass_a * scale_a + mass_b * scale_b, 1.0)
    merged = (sums[0] * scale_a + sums[1] * scale_b) / total
    exponent = exponent_of(jnp.max(jnp.abs(merged), axis=1, keepdims=True))
    fixed = to_fixed(merged, exponent)
    for g in range(group):
        at = pl.multiple_of((first + g) * LANES, LANES)
        out[:, pl.ds(at, LANES)] = fixed[g * tokens : (g + 1) * tokens]

    @pl.when(head == 0)
    def _():
        top_plane[...] = jnp.full(top_plane.shape, FLOOR, F32)
        total_plane[...] = jnp.ones(total_plane.shape, F32)
        scale_plane[...] = jnp.zeros(scale_plane.shape, F32)

    tops, totals, scales = top_plane[...], total_plane[...], scale_plane[...]
    for g in range(group):
        here = lane == first + g
        cut = slice(g * tokens, (g + 1) * tokens)
        tops = jnp.where(here, top[cut], tops)
        totals = jnp.where(here, total[cut], totals)
        scales = jnp.where(here, exponent[cut], scales)
    top_plane[...] = tops
    total_plane[...] = totals
    scale_plane[...] = scales

    @pl.when(head == kv_heads - 1)
    def _():
        heads = group * kv_heads
        left, right = encode_stats(tops, totals, scales, heads)
        out[:, heads * LANES : (heads + 1) * LANES] = left
        out[:, (heads + 1) * LANES :] = right


def attend(info, queries, low, high, fresh, keys_a, keys_b, values_a, values_b, *, own_rows, stages, first_block):
    count = queries.shape[0]
    tokens = min(count, 32)
    slots = keys_a.shape[0]
    kv_heads = keys_a.shape[1] // LANES // CORES
    heads = queries.shape[1] // LANES - 1
    group = heads // kv_heads
    tiles = -(-slots // KEY_TILE)
    sizes = (own_rows, stages, first_block, group, kv_heads, slots)
    half_kv = kv_heads * LANES
    kv = pl.BlockSpec((slots, LANES), lambda i, h, info: (0, info[0] * kv_heads + h))
    return pl.pallas_call(
        functools.partial(attend_kernel, sizes),
        out_shape=jax.ShapeDtypeStruct((count, (heads + 2) * LANES), I16),
        grid_spec=pltpu.PrefetchScalarGridSpec(
            num_scalar_prefetch=1,
            grid=(count // tokens, kv_heads),
            in_specs=[
                pl.BlockSpec((tokens, (heads + 1) * LANES), lambda i, h, info: (i, 0)),
                pl.BlockSpec((low.shape[0], LANES), lambda i, h, info: (0, heads)),
                pl.BlockSpec((high.shape[0], LANES), lambda i, h, info: (0, heads)),
                pl.BlockSpec((CORES * own_rows, 2 * half_kv), lambda i, h, info: (0, 0)),
                kv, kv, kv, kv,
            ],
            out_specs=pl.BlockSpec((tokens, (heads + 2) * LANES), lambda i, h, info: (i, 0)),
            scratch_shapes=[
                pltpu.VMEM((tokens, LANES), F32),
                pltpu.VMEM((tokens, LANES), F32),
                pltpu.VMEM((tokens, LANES), F32),
                pltpu.VMEM((tiles, group * tokens, KEY_TILE), F32),
                pltpu.VMEM((group * tokens, LANES), F32),
                pltpu.VMEM((group * tokens, LANES), F32),
                pltpu.VMEM((2, group * tokens, LANES), F32),
            ],
        ),
        compiler_params=pltpu.CompilerParams(vmem_limit_bytes=40 << 20),
    )(info, queries, low, high, fresh, keys_a, keys_b, values_a, values_b)


def merge_kernel(last, left, right, *outs):
    rows = left.shape[0]
    heads = left.shape[1] // LANES - 2
    factor = math.log2(math.e) / math.sqrt(LANES)

    def stats(ref):
        return decode_stats(ref[:, heads * LANES : (heads + 1) * LANES], ref[:, (heads + 1) * LANES :], heads)

    top_a, total_a, exp_a = stats(left)
    top_b, total_b, exp_b = stats(right)
    top = jnp.maximum(top_a, top_b)
    mass_a = total_a * jnp.exp2((top_a - top) * factor)
    mass_b = total_b * jnp.exp2((top_b - top) * factor)
    total = mass_a + mass_b
    part_a = mass_a / total * jnp.exp2(exp_a - 15.0)
    part_b = mass_b / total * jnp.exp2(exp_b - 15.0)
    lane = lane_ids(rows)
    scales = jnp.zeros((rows, LANES), F32)
    cut = rows // 2
    for h in range(heads):
        at = slice(h * LANES, (h + 1) * LANES)
        value = left[:, at].astype(I32).astype(F32) * part_a[:, h : h + 1]
        value = value + right[:, at].astype(I32).astype(F32) * part_b[:, h : h + 1]
        if last:
            outs[0][:, at] = value[:cut].astype(BF16)
            outs[1][:, at] = value[cut:].astype(BF16)
        else:
            exponent = exponent_of(jnp.max(jnp.abs(value), axis=1, keepdims=True))
            fixed = jnp.clip(jnp.floor(value * jnp.exp2(15.0 - exponent) + 0.5), -32767.0, 32767.0).astype(I32)
            outs[0][:, at] = fixed[:cut].astype(I16)
            outs[1][:, at] = fixed[cut:].astype(I16)
            scales = jnp.where(lane == h, exponent, scales)
    if not last:
        first, second = encode_stats(top, total, scales, heads)
        first, second = first.astype(I32), second.astype(I32)
        for out, part in ((outs[0], slice(0, cut)), (outs[1], slice(cut, rows))):
            out[:, heads * LANES : (heads + 1) * LANES] = first[part].astype(I16)
            out[:, (heads + 1) * LANES :] = second[part].astype(I16)


def merge(left, right, last):
    rows, wide = left.shape
    shape = (
        jax.ShapeDtypeStruct((rows // 2, wide - 2 * LANES), BF16)
        if last
        else jax.ShapeDtypeStruct((rows // 2, wide), I16)
    )
    vmem = pl.BlockSpec(memory_space=pltpu.VMEM)
    return pl.pallas_call(
        functools.partial(merge_kernel, last),
        out_shape=(shape, shape),
        in_specs=[vmem, vmem],
        out_specs=(vmem, vmem),
    )(left, right)


def per_device(
    queries, cache_keys, cached_value_rows, new_keys, prompt_value_rows, cache_len, prompt_start
):
    width = lax.axis_size("ctx")
    me = lax.axis_index("ctx")
    core = me % CORES
    own_rows = queries.shape[0]
    bits = [CORES << i for i in range((width // CORES).bit_length() - 1)][::-1]
    orders = [bits, bits[-1:] + bits[:-1]]
    stages = len(bits)

    def swap(x):
        return lax.ppermute(x, "ctx", [(i, i ^ 1) for i in range(width)])

    def exchange(x, stage):
        return lax.ppermute(x, "ctx", [(i, i ^ orders[i % CORES][stage]) for i in range(width)])

    steps = [jnp.where(core == 0, a // CORES, b // CORES) for a, b in zip(*orders)]
    info = jnp.stack([core, me // CORES, me, prompt_start[0]] + steps).astype(I32)

    mine, other = pack(info, cache_len, queries, new_keys, prompt_value_rows)
    both = jnp.concatenate([mine, swap(other)], axis=0)
    keys_b, values_b = swap(cache_keys), swap(cached_value_rows)
    wide = queries.shape[1] // CORES + LANES
    held, fresh = both[:, :wide], both[:, wide:]
    for stage in range(stages - 1):
        held = jnp.concatenate([held, exchange(held, stage)], axis=0)
    far = exchange(held, stages - 1)
    run = functools.partial(attend, own_rows=own_rows, stages=stages)
    blocks = width // CORES // 2
    rest = (held, far, fresh, cache_keys, keys_b, cached_value_rows, values_b)
    sent = run(info, far, *rest, first_block=blocks)
    kept = run(info, held, *rest, first_block=0)
    for stage in reversed(range(stages)):
        kept, sent = merge(kept, exchange(sent, stage), stage == 0)
    theirs = swap(sent)
    pair = jnp.concatenate([kept, theirs], axis=1)
    flipped = jnp.concatenate([theirs, kept], axis=1)
    return jnp.where(core == 0, pair, flipped)


def solution(mesh):
    return jax.shard_map(
        per_device,
        mesh=mesh,
        in_specs=(
            P(("groups", "ctx"), None),
            P(("groups", "ctx"), None),
            P(("groups", "ctx"), None),
            P(("groups", "ctx"), None),
            P(("groups", "ctx"), None),
            P(("groups", "ctx")),
            P("groups"),
        ),
        out_specs=P(("groups", "ctx"), None),
        check_vma=False,
    )
```

time: 160 us -> 85.7 us (0.54)
  the two profiles are of different devices: /device:TPU:15 before, /device:TPU:0 now
where the time goes in v1:
time: 85.7 us; the launch traced here: 84.2 us
  Pallas kernels  40.7 us (47%)
  waiting for transfers between devices  22.4 us (26%)
  starting transfers between devices  9.96 us (12%)
  local copies, waits for them, and re-layouts  6.81 us (8%)
  other arithmetic  3.04 us (4%)
  between operations  1.35 us (2%)
    pallas_call x2, Pallas kernels, attend(): pl.pallas_call(functools.partial(attend_kernel, sizes), out_shape=jax.Sha...  28.7 us
    ppermute x6, waiting for transfers between devices, exchange(): lax.ppermute(x, 'ctx', [(i, i ^ orders[i % CORES][stage]) for i in range(...  19.9 us
    pallas_call x3, Pallas kernels, merge(): pl.pallas_call(functools.partial(merge_kernel, last), out_shape=(shape, s...  10.5 us
    ppermute x6, starting transfers between devices, exchange(): lax.ppermute(x, 'ctx', [(i, i ^ orders[i % CORES][stage]) for i in range(...  9 us
    unnamed x14, local copies, waits for them, and re-layouts  6.14 us
    ppermute x4, waiting for transfers between devices, swap(): return lax.ppermute(x, 'ctx', [(i, i ^ 1) for i in range(width)])  2.5 us
  transfers between devices with their start and end apart: 10, of which 7 were waited for; matrix products, arithmetic and copies ran while one was open for 1% of the time, Pallas kernels for 17%

profile of v1, /device:TPU:0, one launch (start us, length us, event | category | flops | bytes accessed | tf_op | source)
XLA Modules:
  0.0 84.2 jit_solution(15000791195066981647)
XLA Ops:
  1.3 0.7 stack.27.info
  2.0 1.5 %shard_map.73 = (bf16[4,4736]{1,0:T(4,128)(2,1)}, bf16[4,4736]{1,0:T(4,128)(2,1)}) custom-call(s32[7]{0:T(128)} %stack.27.info, s32[1]{0:T(128)S(6)} %copy.8.length, bf16[4,8192]{1,0:T(4,128)(2,1)} %queries.1, bf16[4,512]{1,0:T(4,128)(2,1)} %new_keys.1, bf16[4,512]{1,0:T(4,128)(2,1)} %new_values.1), custom_call_target="tpu_custom_call" | custom-call | tf_op jit(solution)/shard_map/pallas_call | solution.py:105
  3.5 0.5 collective-permute-start
  3.9 1.1 %collective-permute-done = bf16[4,4736]{1,0:T(4,128)(2,1)S(1)} collective-permute-done((bf16[4,4736]{1,0:T(4,128)(2,1)}, bf16[4,4736]{1,0:T(4,128)(2,1)S(1)}, u32[]{:S(2)}, u32[]{:S(2)}) %collective-permute-start) | collective-permute-done | bytes 37920 | tf_op jit(solution)/shard_map/ppermute | solution.py:382
  5.0 0.8 fusion
  5.8 4.0 %collective-permute-start.1 = (bf16[8,4224]{1,0:T(8,128)(2,1)S(1)}, bf16[8,4224]{1,0:T(8,128)(2,1)S(1)}, u32[]{:S(2)}, u32[]{:S(2)}) collective-permute-start(bf16[8,4224]{1,0:T(8,128)(2,1)S(1)} %fusion), channel_id=1, source_target_pairs={{0,8},{1,3},{2,10},{3,1},{4,12},{5,7},{6,14},{7,5},{8,0},{9,11},{1... | collective-permute-start | bytes 202760 | tf_op jit(solution)/shard_map/ppermute | solution.py:385
  9.8 0.0 collective-permute-start.4
  9.8 0.5 collective-permute-start.5
  10.3 1.8 %collective-permute-done.1 = bf16[8,4224]{1,0:T(8,128)(2,1)S(1)} collective-permute-done((bf16[8,4224]{1,0:T(8,128)(2,1)S(1)}, bf16[8,4224]{1,0:T(8,128)(2,1)S(1)}, u32[]{:S(2)}, u32[]{:S(2)}) %collective-permute-start.1) | collective-permute-done | bytes 67616 | tf_op jit(solution)/shard_map/ppermute | solution.py:385
  12.1 2.0 %collective-permute-start.2 = (bf16[16,4224]{1,0:T(8,128)(2,1)S(1)}, bf16[16,4224]{1,0:T(8,128)(2,1)S(1)}, u32[]{:S(2)}, u32[]{:S(2)}) collective-permute-start(bf16[16,4224]{1,0:T(8,128)(2,1)S(1)} %pad_maximum_fusion.1), channel_id=1, source_target_pairs={{0,4},{1,9},{2,6},{3,11},{4,0},{5,13},{6,2},{7,15},{8,12},{9,1},{1... | collective-permute-start | bytes 405512 | tf_op jit(solution)/shard_map/ppermute | solution.py:385
  14.0 3.4 %collective-permute-done.2 = bf16[16,4224]{1,0:T(8,128)(2,1)S(1)} collective-permute-done((bf16[16,4224]{1,0:T(8,128)(2,1)S(1)}, bf16[16,4224]{1,0:T(8,128)(2,1)S(1)}, u32[]{:S(2)}, u32[]{:S(2)}) %collective-permute-start.2) | collective-permute-done | bytes 135200 | tf_op jit(solution)/shard_map/ppermute | solution.py:385
  17.5 2.0 %collective-permute-start.3 = (bf16[32,4224]{1,0:T(8,128)(2,1)S(1)}, bf16[32,4224]{1,0:T(8,128)(2,1)S(1)}, u32[]{:S(2)}, u32[]{:S(2)}) collective-permute-start(bf16[32,4224]{1,0:T(8,128)(2,1)S(1)} %pad_maximum_fusion.queries.extra_low), channel_id=1, source_target_pairs={{0,2},{1,5},{2,0},{3,7},{4,6},{5,1},{6,4},{7,3},{8,10},{9,13},{10,... | collective-permute-start | bytes 811016 | tf_op jit(solution)/shard_map/ppermute | solution.py:385
  19.4 0.7 pad_maximum_fusion.2.fresh
  20.1 3.9 %collective-permute-done.3.extra_high.queries = bf16[32,4224]{1,0:T(8,128)(2,1)S(1)} collective-permute-done((bf16[32,4224]{1,0:T(8,128)(2,1)S(1)}, bf16[32,4224]{1,0:T(8,128)(2,1)S(1)}, u32[]{:S(2)}, u32[]{:S(2)}) %collective-permute-start.3) | collective-permute-done | bytes 270368 | tf_op jit(solution)/shard_map/ppermute | solution.py:385
  24.0 0.0 collective-permute-done.4.keys_b
  24.0 0.0 collective-permute-done.5.values_b
  24.0 0.0 copy-start
  24.0 1.4 %copy-done = bf16[1536,512]{1,0:T(8,128)(2,1)S(1)} copy-done((bf16[1536,512]{1,0:T(8,128)(2,1)S(1)}, bf16[1536,512]{1,0:T(8,128)(2,1)}, u32[]{:S(2)}) %copy-start) | copy-done | bytes 1572888
  25.4 0.0 copy-start.1
  25.4 1.4 %copy-done.1 = bf16[1536,512]{1,0:T(8,128)(2,1)S(1)} copy-done((bf16[1536,512]{1,0:T(8,128)(2,1)S(1)}, bf16[1536,512]{1,0:T(8,128)(2,1)}, u32[]{:S(2)}) %copy-start.1) | copy-done | bytes 1572888
  26.8 0.0 copy-start.3
  26.8 0.7 copy-done.3
  27.5 14.3 %shard_map.75 = s16[32,4352]{1,0:T(8,128)(2,1)S(1)} custom-call(s32[7]{0:T(128)S(1)} %copy-done.3, bf16[32,4224]{1,0:T(8,128)(2,1)S(1)} %collective-permute-done.3.extra_high.queries, bf16[32,4224]{1,0:T(8,128)(2,1)S(1)} %pad_maximum_fusion.queries.extra_low, bf16[32,4224]{1,0:T(8,128)(2,1)S(1)} %collective-permute-done.3.extra_high.queries, ...), custom_call_target="tpu_custom_call" | custom-call | tf_op jit(solution)/shard_map/pallas_call | solution.py:286
  41.8 1.1 %collective-permute-start.6 = (s16[32,4352]{1,0:T(8,128)(2,1)S(1)}, s16[32,4352]{1,0:T(8,128)(2,1)S(1)}, u32[]{:S(2)}, u32[]{:S(2)}) collective-permute-start(s16[32,4352]{1,0:T(8,128)(2,1)S(1)} %shard_map.75), channel_id=1, source_target_pairs={{0,2},{1,5},{2,0},{3,7},{4,6},{5,1},{6,4},{7,3},{8,10},{9,13},{10,... | collective-permute-start | bytes 835592 | tf_op jit(solution)/shard_map/ppermute | solution.py:385
  42.9 14.3 %shard_map.74.left = s16[32,4352]{1,0:T(8,128)(2,1)S(1)} custom-call(s32[7]{0:T(128)S(1)} %copy-done.3, bf16[32,4224]{1,0:T(8,128)(2,1)S(1)} %pad_maximum_fusion.queries.extra_low, bf16[32,4224]{1,0:T(8,128)(2,1)S(1)} %pad_maximum_fusion.queries.extra_low, bf16[32,4224]{1,0:T(8,128)(2,1)S(1)} %collective-permute-done.3.extra_high.queries, ...), custom_call_target="tpu_custom_call" | custom-call | tf_op jit(solution)/shard_map/pallas_call | solution.py:286
  57.2 0.0 copy-start.2
  57.2 0.7 copy-done.2
  57.9 0.0 collective-permute-done.6.right
  57.9 0.0 copy-start.4
  57.9 0.7 copy-done.4
  58.6 4.7 %shard_map.76 = (s16[16,4352]{1,0:T(8,128)(2,1)}, s16[16,4352]{1,0:T(8,128)(2,1)}) custom-call(s16[32,4352]{1,0:T(8,128)(2,1)} %copy-done.2, s16[32,4352]{1,0:T(8,128)(2,1)} %copy-done.4), custom_call_target="tpu_custom_call" | custom-call | tf_op jit(solution)/shard_map/pallas_call | solution.py:362
  63.3 0.0 collective-permute-start.7
  63.3 5.3 %collective-permute-done.7.right = s16[16,4352]{1,0:T(8,128)(2,1)S(1)} collective-permute-done((s16[16,4352]{1,0:T(8,128)(2,1)}, s16[16,4352]{1,0:T(8,128)(2,1)S(1)}, u32[]{:S(2)}, u32[]{:S(2)}) %collective-permute-start.7) | collective-permute-done | bytes 139296 | tf_op jit(solution)/shard_map/ppermute | solution.py:385
  68.6 0.0 copy-start.5
  68.6 0.6 copy-done.5
  69.3 4.0 %shard_map.77 = (s16[8,4352]{1,0:T(8,128)(2,1)}, s16[8,4352]{1,0:T(8,128)(2,1)}) custom-call(s16[16,4352]{1,0:T(8,128)(2,1)} %get-tuple-element.15.left, s16[16,4352]{1,0:T(8,128)(2,1)} %copy-done.5), custom_call_target="tpu_custom_call" | custom-call | tf_op jit(solution)/shard_map/pallas_call | solution.py:362
  73.3 0.0 collective-permute-start.8
  73.3 5.5 %collective-permute-done.8.right = s16[8,4352]{1,0:T(8,128)(2,1)S(1)} collective-permute-done((s16[8,4352]{1,0:T(8,128)(2,1)}, s16[8,4352]{1,0:T(8,128)(2,1)S(1)}, u32[]{:S(2)}, u32[]{:S(2)}) %collective-permute-start.8) | collective-permute-done | bytes 69664 | tf_op jit(solution)/shard_map/ppermute | solution.py:385
  78.8 0.0 copy-start.6
  78.8 0.6 copy-done.6
  79.5 1.8 %shard_map.78 = (bf16[4,4096]{1,0:T(4,128)(2,1)}, bf16[4,4096]{1,0:T(4,128)(2,1)}) custom-call(s16[8,4352]{1,0:T(8,128)(2,1)} %get-tuple-element.17.left, s16[8,4352]{1,0:T(8,128)(2,1)} %copy-done.6), custom_call_target="tpu_custom_call" | custom-call | tf_op jit(solution)/shard_map/pallas_call | solution.py:362
  81.3 0.0 collective-permute-start.9
  81.3 1.4 %collective-permute-done.9 = bf16[4,4096]{1,0:T(4,128)(2,1)S(1)} collective-permute-done((bf16[4,4096]{1,0:T(4,128)(2,1)}, bf16[4,4096]{1,0:T(4,128)(2,1)S(1)}, u32[]{:S(2)}, u32[]{:S(2)}) %collective-permute-start.9) | collective-permute-done | bytes 32800 | tf_op jit(solution)/shard_map/ppermute | solution.py:382
  82.7 1.5 %maximum_select_fusion = bf16[4,8192]{1,0:T(4,128)(2,1)} fusion(bf16[4,4096]{1,0:T(4,128)(2,1)S(1)} %collective-permute-done.9, bf16[4,4096]{1,0:T(4,128)(2,1)} %get-tuple-element.19, pred[]{:T(512)S(6)} %eq.4), kind=kLoop, calls=%fused_computation.5 | loop fusion | flops 294912 | bytes 131073 | tf_op jit(solution)/shard_map/jit(_where)/select_n | solution.py:408
  (2 shorter events, 0.0 us)
Async XLA Ops:
  3.5 1.5 %collective-permute-start = (bf16[4,4736]{1,0:T(4,128)(2,1)}, bf16[4,4736]{1,0:T(4,128)(2,1)S(1)}, u32[]{:S(2)}, u32[]{:S(2)}) collective-permute-start(bf16[4,4736]{1,0:T(4,128)(2,1)} %get-tuple-element.14), channel_id=1, source_target_pairs={{0,1},{1,0},{2,3},{3,2},{4,5},{5,4},{6,7},{7,6},{8,9},{9,8},{10,11... | collective-permute-start | bytes 113672 | tf_op jit(solution)/shard_map/ppermute | solution.py:382
  5.8 6.3 %collective-permute-start.1 = (bf16[8,4224]{1,0:T(8,128)(2,1)S(1)}, bf16[8,4224]{1,0:T(8,128)(2,1)S(1)}, u32[]{:S(2)}, u32[]{:S(2)}) collective-permute-start(bf16[8,4224]{1,0:T(8,128)(2,1)S(1)} %fusion), channel_id=1, source_target_pairs={{0,8},{1,3},{2,10},{3,1},{4,12},{5,7},{6,14},{7,5},{8,0},{9,11},{1... | collective-permute-start | bytes 202760 | tf_op jit(solution)/shard_map/ppermute | solution.py:385
  9.8 14.2 %collective-permute-start.4 = (bf16[1536,512]{1,0:T(8,128)(2,1)}, bf16[1536,512]{1,0:T(8,128)(2,1)S(1)}, u32[]{:S(2)}, u32[]{:S(2)}) collective-permute-start(bf16[1536,512]{1,0:T(8,128)(2,1)} %keys_a.3), channel_id=1, source_target_pairs={{0,1},{1,0},{2,3},{3,2},{4,5},{5,4},{6,7},{7,6},{8,9},{9,8},{10,11... | collective-permute-start | bytes 4718600 | tf_op jit(solution)/shard_map/ppermute | solution.py:382
  9.8 14.2 %collective-permute-start.5 = (bf16[1536,512]{1,0:T(8,128)(2,1)}, bf16[1536,512]{1,0:T(8,128)(2,1)S(1)}, u32[]{:S(2)}, u32[]{:S(2)}) collective-permute-start(bf16[1536,512]{1,0:T(8,128)(2,1)} %values_a.3), channel_id=1, source_target_pairs={{0,1},{1,0},{2,3},{3,2},{4,5},{5,4},{6,7},{7,6},{8,9},{9,8},{10,11... | collective-permute-start | bytes 4718600 | tf_op jit(solution)/shard_map/ppermute | solution.py:382
  12.1 5.4 %collective-permute-start.2 = (bf16[16,4224]{1,0:T(8,128)(2,1)S(1)}, bf16[16,4224]{1,0:T(8,128)(2,1)S(1)}, u32[]{:S(2)}, u32[]{:S(2)}) collective-permute-start(bf16[16,4224]{1,0:T(8,128)(2,1)S(1)} %pad_maximum_fusion.1), channel_id=1, source_target_pairs={{0,4},{1,9},{2,6},{3,11},{4,0},{5,13},{6,2},{7,15},{8,12},{9,1},{1... | collective-permute-start | bytes 405512 | tf_op jit(solution)/shard_map/ppermute | solution.py:385
  17.5 6.5 %collective-permute-start.3 = (bf16[32,4224]{1,0:T(8,128)(2,1)S(1)}, bf16[32,4224]{1,0:T(8,128)(2,1)S(1)}, u32[]{:S(2)}, u32[]{:S(2)}) collective-permute-start(bf16[32,4224]{1,0:T(8,128)(2,1)S(1)} %pad_maximum_fusion.queries.extra_low), channel_id=1, source_target_pairs={{0,2},{1,5},{2,0},{3,7},{4,6},{5,1},{6,4},{7,3},{8,10},{9,13},{10,... | collective-permute-start | bytes 811016 | tf_op jit(solution)/shard_map/ppermute | solution.py:385
  24.0 1.4 %copy-start = (bf16[1536,512]{1,0:T(8,128)(2,1)S(1)}, bf16[1536,512]{1,0:T(8,128)(2,1)}, u32[]{:S(2)}) copy-start(bf16[1536,512]{1,0:T(8,128)(2,1)} %keys_a.3) | copy-start | bytes 4718596
  25.4 1.4 %copy-start.1 = (bf16[1536,512]{1,0:T(8,128)(2,1)S(1)}, bf16[1536,512]{1,0:T(8,128)(2,1)}, u32[]{:S(2)}) copy-start(bf16[1536,512]{1,0:T(8,128)(2,1)} %values_a.3) | copy-start | bytes 4718596
  26.8 0.7 copy-start.3
  41.8 16.1 %collective-permute-start.6 = (s16[32,4352]{1,0:T(8,128)(2,1)S(1)}, s16[32,4352]{1,0:T(8,128)(2,1)S(1)}, u32[]{:S(2)}, u32[]{:S(2)}) collective-permute-start(s16[32,4352]{1,0:T(8,128)(2,1)S(1)} %shard_map.75), channel_id=1, source_target_pairs={{0,2},{1,5},{2,0},{3,7},{4,6},{5,1},{6,4},{7,3},{8,10},{9,13},{10,... | collective-permute-start | bytes 835592 | tf_op jit(solution)/shard_map/ppermute | solution.py:385
  57.2 0.7 copy-start.2
  57.9 0.7 copy-start.4
  63.3 5.3 %collective-permute-start.7 = (s16[16,4352]{1,0:T(8,128)(2,1)}, s16[16,4352]{1,0:T(8,128)(2,1)S(1)}, u32[]{:S(2)}, u32[]{:S(2)}) collective-permute-start(s16[16,4352]{1,0:T(8,128)(2,1)} %get-tuple-element.16), channel_id=1, source_target_pairs={{0,4},{1,9},{2,6},{3,11},{4,0},{5,13},{6,2},{7,15},{8,12},{9,1},{1... | collective-permute-start | bytes 417800 | tf_op jit(solution)/shard_map/ppermute | solution.py:385
  68.6 0.6 copy-start.5
  73.3 5.5 %collective-permute-start.8 = (s16[8,4352]{1,0:T(8,128)(2,1)}, s16[8,4352]{1,0:T(8,128)(2,1)S(1)}, u32[]{:S(2)}, u32[]{:S(2)}) collective-permute-start(s16[8,4352]{1,0:T(8,128)(2,1)} %get-tuple-element.18), channel_id=1, source_target_pairs={{0,8},{1,3},{2,10},{3,1},{4,12},{5,7},{6,14},{7,5},{8,0},{9,11},{1... | collective-permute-start | bytes 208904 | tf_op jit(solution)/shard_map/ppermute | solution.py:385
  78.8 0.6 copy-start.6
  81.3 1.4 %collective-permute-start.9 = (bf16[4,4096]{1,0:T(4,128)(2,1)}, bf16[4,4096]{1,0:T(4,128)(2,1)S(1)}, u32[]{:S(2)}, u32[]{:S(2)}) collective-permute-start(bf16[4,4096]{1,0:T(4,128)(2,1)} %get-tuple-element.20), channel_id=1, source_target_pairs={{0,1},{1,0},{2,3},{3,2},{4,5},{5,4},{6,7},{7,6},{8,9},{9,8},{10,11... | collective-permute-start | bytes 98312 | tf_op jit(solution)/shard_map/ppermute | solution.py:382

commit v2 on v0

v2 whole, which is shorter than its diff:
```python
import functools
import math

import jax
import jax.numpy as jnp
from jax import lax
from jax.experimental import pallas as pl
from jax.experimental.pallas import tpu as pltpu
from jax.sharding import PartitionSpec as P

KEY_VALUE_HEADS = 4
LANES = 128
CORES = 2
FLOOR = -1e30
KEY_TILE = 256
STAT_ROWS = 16
CHUNK_BLOCKS = 4
STEP = 2.0**15
MARGIN = 0.9998
F32 = jnp.float32
BF16 = jnp.bfloat16
I16 = jnp.int16
I32 = jnp.int32
VMEM = pl.BlockSpec(memory_space=pltpu.VMEM)
SMEM = pl.BlockSpec(memory_space=pltpu.SMEM)
HBM = pl.BlockSpec(memory_space=pltpu.HBM)
SMALL = pltpu.CompilerParams(vmem_limit_bytes=8 << 20)


def encode(out, at, values, top, total):
    dims, width = values.shape
    largest = jnp.max(jnp.abs(values), axis=0, keepdims=True)
    exponent = jnp.floor(jnp.log2(jnp.maximum(largest, 1e-30))) + 1.0
    fixed = jnp.floor(values * (jnp.exp2(15.0 - exponent) * MARGIN) + 0.5)
    size = jnp.abs(top)
    level = jnp.zeros_like(top)
    scaled = top
    for i in range(1, 9):
        above = size >= STEP**i
        level = level + jnp.where(above, 1.0, 0.0)
        scaled = scaled * jnp.where(above, 1.0 / STEP, 1.0)
    a = jnp.floor(scaled)
    rest = (scaled - a) * STEP
    b = jnp.floor(rest)
    c = jnp.floor((rest - b) * STEP)
    logs = jnp.log2(total) * 1024.0
    la = jnp.floor(logs)
    lb = jnp.floor((logs - la) * STEP)
    row = lax.broadcasted_iota(I32, (STAT_ROWS, width), 0)
    stats = jnp.zeros((STAT_ROWS, width), F32)
    for i, part in enumerate((level, a, b, c, exponent, la, lb)):
        stats = jnp.where(row == i, part, stats)
    out[:dims, at : at + width] = fixed.astype(I32).astype(I16)
    out[dims:, at : at + width] = stats.astype(I32).astype(I16)


def decode_stats(ref, dims, at):
    stats = ref[dims:, at].astype(I32).astype(F32)

    def part(i):
        return stats[i : i + 1, :]

    top = part(1) + (part(2) + part(3) * (1.0 / STEP)) * (1.0 / STEP)
    for i in range(1, 9):
        top = top * jnp.where(part(0) >= i, STEP, 1.0)
    total = jnp.exp2((part(5) + part(6) * (1.0 / STEP)) * (1.0 / 1024.0))
    return top, total, jnp.exp2(part(4) - 15.0) * (1.0 / MARGIN)


def join_kernel(length, length_other, queries, queries_other, out):
    rows = queries.shape[0]
    half = queries.shape[1] // CORES
    core = lax.axis_index("ctx") % CORES
    at = pl.multiple_of(core * half, LANES)
    mine = queries[:, pl.ds(at, half)].astype(F32)
    other = queries_other[:, pl.ds(at, half)].astype(F32)
    out[:, :half] = jnp.concatenate([mine, other], axis=0).astype(BF16)
    lane = lax.broadcasted_iota(I32, (CORES * rows, LANES), 1)
    row = lax.broadcasted_iota(I32, (CORES * rows, LANES), 0)
    count = jnp.where(row < rows, length[0], length_other[0])
    coded = jnp.where(lane == 0, count // LANES, jnp.where(lane == 1, count % LANES, 0))
    out[:, half:] = coded.astype(F32).astype(BF16)


def join(length, length_other, queries, queries_other):
    rows, wide = queries.shape
    return pl.pallas_call(
        join_kernel,
        out_shape=jax.ShapeDtypeStruct((CORES * rows, wide // CORES + LANES), BF16),
        in_specs=[SMEM, SMEM, VMEM, VMEM],
        out_specs=VMEM,
        compiler_params=SMALL,
    )(length, length_other, queries, queries_other)


def attend_kernel(
    sizes, start, queries, low, high, fresh_keys_a, fresh_keys_b, fresh_values_a, fresh_values_b,
    keys_a, keys_b, values_a, values_b, out, query_t, scores, sums, kv, arrived
):
    own_rows, orders, first_block, group, kv_heads = sizes
    chip_rows = CORES * own_rows
    slots = keys_a.shape[0]
    tokens = queries.shape[0]
    blocks = tokens // chip_rows
    lanes = blocks * group * chip_rows
    me = lax.axis_index("ctx")
    core, chip = me % CORES, me // CORES
    factor = math.log2(math.e) / math.sqrt(LANES)
    chunk = pl.program_id(0)

    def copy(h, i):
        at = pl.multiple_of((core * kv_heads + h) * LANES, LANES)
        source = (keys_a, keys_b, values_a, values_b)[i]
        return pltpu.make_async_copy(source.at[:, pl.ds(at, LANES)], kv.at[h, i], arrived.at[h, i])

    @pl.when(chunk == 0)
    def _():
        for h in range(kv_heads):
            for i in range(4):
                copy(h, i).start()

    steps = [jnp.where(core == 0, a // CORES, b // CORES) for a, b in zip(*orders)]

    def origin(block):
        off = jnp.zeros_like(block)
        for i, step in enumerate(steps):
            off = off ^ jnp.where((block >> i) & 1 == 1, step, 0)
        return chip ^ off

    before, length = 0.0, [0.0, 0.0]
    base = 0
    for ref in (low, high):
        rows = ref.shape[0]
        lane = lax.broadcasted_iota(I32, (rows, LANES), 1)
        row = lax.broadcasted_iota(I32, (rows, LANES), 0)
        place = origin((row + base) // chip_rows)
        inside = row % chip_rows
        counts = jnp.where(lane == 0, float(LANES), 1.0) * ref[...].astype(F32)
        counts = jnp.where((inside % own_rows == 0) & (lane < 2), counts, 0.0)
        before = before + jnp.sum(jnp.where(place < chip, counts, 0.0))
        for s in range(2):
            length[s] = length[s] + jnp.sum(jnp.where((place == chip) & (inside // own_rows == s), counts, 0.0))
        base = base + rows
    length = [x.astype(I32) for x in length]
    before = before.astype(I32)
    begins = [
        before + jnp.where(core == 1, length[1], 0),
        before + jnp.where(core == 0, length[0], 0),
    ]
    limits = [jnp.clip(jnp.minimum(n, start[0] - at), 0, slots) for n, at in zip(length, begins)]

    key_row = lax.broadcasted_iota(I32, (chip_rows, lanes), 0)
    lane = lax.broadcasted_iota(I32, (chip_rows, lanes), 1)
    part = key_row // own_rows
    key_id = (chip * CORES + (core ^ part)) * own_rows + key_row % own_rows
    inside = lane % chip_rows
    block = lane // (group * chip_rows) + (first_block + chunk * blocks)
    token = (origin(block) * CORES + (core ^ (inside // own_rows))) * own_rows + inside % own_rows
    causal = key_id <= token
    key_slot = lax.broadcasted_iota(I32, (KEY_TILE, lanes), 0)
    nothing = jnp.zeros((16 - chip_rows % 16, LANES), F32)

    for h in range(kv_heads):
        first = h * group
        q = jnp.concatenate(
            [
                queries[b * chip_rows : (b + 1) * chip_rows, (first + g) * LANES : (first + g + 1) * LANES].astype(F32)
                for b in range(blocks)
                for g in range(group)
            ],
            axis=0,
        )
        query_t[...] = q.T.astype(BF16)
        at = pl.multiple_of((core * kv_heads + h) * LANES, LANES)

        def fresh(a, b):
            return jnp.concatenate([a[:, pl.ds(at, LANES)].astype(F32), b[:, pl.ds(at, LANES)].astype(F32), nothing], 0)

        new_keys = fresh(fresh_keys_a, fresh_keys_b).astype(BF16)
        new_values = fresh(fresh_values_a, fresh_values_b).astype(BF16)
        new_scores = jnp.dot(new_keys, query_t[...], preferred_element_type=F32)[:chip_rows] * factor

        @pl.when(chunk == 0)
        def _():
            for i in range(2):
                copy(h, i).wait()

        def fold(tile, combine):
            return combine(tile.reshape(KEY_TILE // 8, 8, lanes), axis=0)

        tops = []
        for s in range(2):
            limit = limits[s]
            whole = limit // KEY_TILE
            seen = causal & (part == s)
            peak = jnp.where(seen, new_scores, FLOOR)

            def score(j):
                at = pl.multiple_of(j * KEY_TILE, KEY_TILE)
                return jnp.dot(kv[h, s, pl.ds(at, KEY_TILE), :], query_t[...], preferred_element_type=F32) * factor

            def first_pass(j, peak):
                tile = score(j)
                scores[s, j] = tile
                return jnp.maximum(peak, fold(tile, jnp.max))

            peak = lax.fori_loop(0, whole, first_pass, peak)

            def last_tile(peak):
                tile = jnp.where(key_slot < limit - whole * KEY_TILE, score(whole), FLOOR)
                scores[s, whole] = tile
                return jnp.maximum(peak, fold(tile, jnp.max))

            peak = lax.cond(limit > whole * KEY_TILE, last_tile, lambda peak: peak, peak)
            tops.append(jnp.max(peak, axis=0, keepdims=True))

        @pl.when(chunk == 0)
        def _():
            for i in range(2, 4):
                copy(h, i).wait()

        masses = []
        for s in range(2):
            limit = limits[s]
            whole = limit // KEY_TILE
            seen = causal & (part == s)
            top = tops[s]
            weight = jnp.where(seen, jnp.exp2(new_scores - top), 0.0)
            padded = jnp.concatenate([weight, jnp.zeros((16 - chip_rows % 16, lanes), F32)], 0).astype(BF16)
            tn = (((0,), (0,)), ((), ()))
            sums[s] = lax.dot_general(new_values, padded, tn, preferred_element_type=F32)

            def add(j, weight):
                at = pl.multiple_of(j * KEY_TILE, KEY_TILE)
                sums[s] += lax.dot_general(
                    kv[h, 2 + s, pl.ds(at, KEY_TILE), :], weight.astype(BF16), tn, preferred_element_type=F32
                )

            def second_pass(j, mass):
                weight = jnp.exp2(scores[s, j] - top)
                add(j, weight)
                return mass + fold(weight, jnp.sum)

            mass = lax.fori_loop(0, whole, second_pass, weight)

            def last_tile(mass):
                weight = jnp.where(
                    key_slot < limit - whole * KEY_TILE, jnp.exp2(scores[s, whole] - top), 0.0
                )
                add(whole, weight)
                return mass + fold(weight, jnp.sum)

            mass = lax.cond(limit > whole * KEY_TILE, last_tile, lambda mass: mass, mass)
            masses.append(jnp.sum(mass, axis=0, keepdims=True))

        top = jnp.maximum(tops[0], tops[1])
        scale_a = jnp.exp2(tops[0] - top)
        scale_b = jnp.exp2(tops[1] - top)
        total = jnp.maximum(masses[0] * scale_a + masses[1] * scale_b, 1.0)
        merged = sums[0] * (scale_a / total) + sums[1] * (scale_b / total)
        width = group * chip_rows
        for b in range(blocks):
            cut = slice(b * width, (b + 1) * width)
            encode(out, (b * kv_heads + h) * width, merged[:, cut], top[:, cut], total[:, cut])


def attend(
    start, queries, low, high, fresh, cache, *, own_rows, orders, first_block
):
    count = queries.shape[0]
    chip_rows = CORES * own_rows
    tokens = min(count, CHUNK_BLOCKS * chip_rows)
    slots = cache[0].shape[0]
    kv_heads = cache[0].shape[1] // LANES // CORES
    heads = queries.shape[1] // LANES - 1
    group = heads // kv_heads
    lanes = tokens * group
    tiles = -(-slots // KEY_TILE)
    sizes = (own_rows, orders, first_block, group, kv_heads)
    return pl.pallas_call(
        functools.partial(attend_kernel, sizes),
        out_shape=jax.ShapeDtypeStruct((LANES + STAT_ROWS, count * heads), I16),
        grid=(count // tokens,),
        in_specs=[
            SMEM,
            pl.BlockSpec((tokens, heads * LANES), lambda i: (i, 0)),
            pl.BlockSpec((low.shape[0], LANES), lambda i: (0, heads)),
            pl.BlockSpec((high.shape[0], LANES), lambda i: (0, heads)),
            VMEM, VMEM, VMEM, VMEM,
            HBM, HBM, HBM, HBM,
        ],
        out_specs=pl.BlockSpec((LANES + STAT_ROWS, tokens * heads), lambda i: (0, i)),
        scratch_shapes=[
            pltpu.VMEM((LANES, lanes), BF16),
            pltpu.VMEM((2, tiles, KEY_TILE, lanes), F32),
            pltpu.VMEM((2, LANES, lanes), F32),
            pltpu.VMEM((kv_heads, 4, tiles * KEY_TILE, LANES), BF16),
            pltpu.SemaphoreType.DMA((kv_heads, 4)),
        ],
        compiler_params=pltpu.CompilerParams(vmem_limit_bytes=32 << 20),
    )(start, queries, low, high, *fresh, *cache)


def merged_part(left, right, dims, at):
    top_a, total_a, unit_a = decode_stats(left, dims, at)
    top_b, total_b, unit_b = decode_stats(right, dims, at)
    top = jnp.maximum(top_a, top_b)
    mass_a = total_a * jnp.exp2(top_a - top)
    mass_b = total_b * jnp.exp2(top_b - top)
    total = mass_a + mass_b
    values = left[:dims, at].astype(I32).astype(F32) * (mass_a / total * unit_a)
    values = values + right[:dims, at].astype(I32).astype(F32) * (mass_b / total * unit_b)
    return values, top, total


def merge_kernel(left, right, kept, sent):
    dims = left.shape[0] - STAT_ROWS
    half = kept.shape[1]
    step = min(half, 2 * LANES)
    for out, base in ((sent, half), (kept, 0)):
        for at in range(0, half, step):
            encode(out, at, *merged_part(left, right, dims, slice(base + at, base + at + step)))


def merge(left, right):
    rows, width = left.shape
    shape = jax.ShapeDtypeStruct((rows, width // 2), I16)
    return pl.pallas_call(
        merge_kernel,
        out_shape=(shape, shape),
        in_specs=[VMEM, VMEM],
        out_specs=(VMEM, VMEM),
        compiler_params=SMALL,
    )(left, right)


def finish_kernel(group, left, right, mine, other):
    dims = left.shape[0] - STAT_ROWS
    own_rows = mine.shape[0]
    chip_rows = CORES * own_rows
    width = group * chip_rows
    for h in range(left.shape[1] // width):
        values, _, _ = merged_part(left, right, dims, slice(h * width, (h + 1) * width))
        rows = values.T
        for g in range(group):
            at = (h * group + g) * dims
            tokens = rows[g * chip_rows : (g + 1) * chip_rows]
            mine[:, at : at + dims] = tokens[:own_rows].astype(BF16)
            other[:, at : at + dims] = tokens[own_rows:].astype(BF16)


def finish(left, right, own_rows, group):
    dims = left.shape[0] - STAT_ROWS
    shape = jax.ShapeDtypeStruct((own_rows, left.shape[1] // (CORES * own_rows) * dims), BF16)
    return pl.pallas_call(
        functools.partial(finish_kernel, group),
        out_shape=(shape, shape),
        in_specs=[VMEM, VMEM],
        out_specs=(VMEM, VMEM),
        compiler_params=SMALL,
    )(left, right)


def place_kernel(mine, theirs, out):
    half = mine.shape[1]
    core = lax.axis_index("ctx") % CORES
    out[:, pl.ds(pl.multiple_of(core * half, LANES), half)] = mine[...]
    out[:, pl.ds(pl.multiple_of((1 - core) * half, LANES), half)] = theirs[...]


def place(mine, theirs):
    rows, half = mine.shape
    return pl.pallas_call(
        place_kernel,
        out_shape=jax.ShapeDtypeStruct((rows, CORES * half), BF16),
        in_specs=[VMEM, VMEM],
        out_specs=VMEM,
        compiler_params=SMALL,
    )(mine, theirs)


def per_device(
    queries, cache_keys, cached_value_rows, new_keys, prompt_value_rows, cache_len, prompt_start
):
    width = lax.axis_size("ctx")
    own_rows = queries.shape[0]
    group = queries.shape[1] // cache_keys.shape[1]
    bits = [CORES << i for i in range((width // CORES).bit_length() - 1)][::-1]
    orders = (tuple(bits), tuple(bits[-1:] + bits[:-1]))
    stages = len(bits)

    def swap(x):
        return lax.ppermute(x, "ctx", [(i, i ^ 1) for i in range(width)])

    def exchange(x, stage):
        return lax.ppermute(x, "ctx", [(i, i ^ orders[i % CORES][stage]) for i in range(width)])

    held = join(cache_len, swap(cache_len), queries, swap(queries))
    fresh = (new_keys, swap(new_keys), prompt_value_rows, swap(prompt_value_rows))
    cache = (cache_keys, swap(cache_keys), cached_value_rows, swap(cached_value_rows))
    for stage in range(stages - 1):
        held = jnp.concatenate([held, exchange(held, stage)], axis=0)
    far = exchange(held, stages - 1)
    run = functools.partial(attend, own_rows=own_rows, orders=orders)
    sent = run(prompt_start, far, held, far, fresh, cache, first_block=width // CORES // 2)
    kept = run(prompt_start, held, held, far, fresh, cache, first_block=0)
    for stage in reversed(range(1, stages)):
        kept, sent = merge(kept, exchange(sent, stage))
    mine, other = finish(kept, exchange(sent, 0), own_rows, group)
    return place(mine, swap(other))


def solution(mesh):
    return jax.shard_map(
        per_device,
        mesh=mesh,
        in_specs=(
            P(("groups", "ctx"), None),
            P(("groups", "ctx"), None),
            P(("groups", "ctx"), None),
            P(("groups", "ctx"), None),
            P(("groups", "ctx"), None),
            P(("groups", "ctx")),
            P("groups"),
        ),
        out_specs=P(("groups", "ctx"), None),
        check_vma=False,
    )
```

time: 160 us -> 63.6 us (0.40)
  the two profiles are of different devices: /device:TPU:15 before, /device:TPU:3 now
where the time goes in v2:
time: 63.6 us; the launch traced here: 62.5 us
  Pallas kernels  26.2 us (41%)
  waiting for transfers between devices  16.2 us (25%)
  starting transfers between devices  13.7 us (22%)
  local copies, waits for them, and re-layouts  5.03 us (8%)
  between operations  1.4 us (2%)
    pallas_call x2, Pallas kernels, attend(): pl.pallas_call(functools.partial(attend_kernel, sizes), out_shape=jax.Sha...  24.1 us
    ppermute x6, waiting for transfers between devices, exchange(): lax.ppermute(x, 'ctx', [(i, i ^ orders[i % CORES][stage]) for i in range(...  13.8 us
    ppermute x7, starting transfers between devices, swap(): return lax.ppermute(x, 'ctx', [(i, i ^ 1) for i in range(width)])  9.15 us
    unnamed x10, local copies, waits for them, and re-layouts  5.03 us
    ppermute x6, starting transfers between devices, exchange(): lax.ppermute(x, 'ctx', [(i, i ^ orders[i % CORES][stage]) for i in range(...  4.53 us
    ppermute x7, waiting for transfers between devices, swap(): return lax.ppermute(x, 'ctx', [(i, i ^ 1) for i in range(width)])  2.32 us
  transfers between devices with their start and end apart: 13, of which 9 were waited for; matrix products, arithmetic and copies ran while one was open for 0% of the time, Pallas kernels for 19%

profile of v2, /device:TPU:3, one launch (start us, length us, event | category | flops | bytes accessed | tf_op | source)
XLA Modules:
  0.0 62.5 jit_solution(6470635500338650045)
XLA Ops:
  0.0 0.7 %collective-permute-start.1 = (bf16[4,8192]{1,0:T(4,128)(2,1)}, bf16[4,8192]{1,0:T(4,128)(2,1)S(1)}, u32[]{:S(2)}, u32[]{:S(2)}) collective-permute-start(bf16[4,8192]{1,0:T(4,128)(2,1)} %queries.1), channel_id=1, source_target_pairs={{0,1},{1,0},{2,3},{3,2},{4,5},{5,4},{6,7},{7,6},{8,9},{9,8},{10,11... | collective-permute-start | bytes 196616 | tf_op jit(solution)/shard_map/ppermute | solution.py:393
  0.7 0.0 collective-permute-start
  1.3 0.7 %collective-permute-done.length_other = s32[1]{0:T(128)} collective-permute-done((s32[1]{0:T(128)}, s32[1]{0:T(128)}, u32[]{:S(2)}, u32[]{:S(2)}) %collective-permute-start) | collective-permute-done | bytes 36 | tf_op jit(solution)/shard_map/ppermute | solution.py:393
  2.1 0.0 collective-permute-done.1.queries_other
  2.1 0.0 copy-start.2
  2.1 0.8 %copy-done.2 = bf16[4,8192]{1,0:T(4,128)(2,1)S(1)} copy-done((bf16[4,8192]{1,0:T(4,128)(2,1)S(1)}, bf16[4,8192]{1,0:T(4,128)(2,1)}, u32[]{:S(2)}) %copy-start.2) | copy-done | bytes 65560
  2.9 0.6 shard_map.73
  3.5 1.3 %collective-permute-start.2 = (bf16[8,4224]{1,0:T(8,128)(2,1)S(1)}, bf16[8,4224]{1,0:T(8,128)(2,1)S(1)}, u32[]{:S(2)}, u32[]{:S(2)}) collective-permute-start(bf16[8,4224]{1,0:T(8,128)(2,1)S(1)} %shard_map.73), channel_id=1, source_target_pairs={{0,8},{1,3},{2,10},{3,1},{4,12},{5,7},{6,14},{7,5},{8,0},{9,11},{1... | collective-permute-start | bytes 202760 | tf_op jit(solution)/shard_map/ppermute | solution.py:396
  4.8 1.6 %collective-permute-start.7 = (bf16[1536,512]{1,0:T(8,128)(2,1)}, bf16[1536,512]{1,0:T(8,128)(2,1)S(1)}, u32[]{:S(2)}, u32[]{:S(2)}) collective-permute-start(bf16[1536,512]{1,0:T(8,128)(2,1)} %keys_a.3), channel_id=1, source_target_pairs={{0,1},{1,0},{2,3},{3,2},{4,5},{5,4},{6,7},{7,6},{8,9},{9,8},{10,11... | collective-permute-start | bytes 4718600 | tf_op jit(solution)/shard_map/ppermute | solution.py:393
  6.4 0.0 collective-permute-start.8
  6.4 0.3 collective-permute-done.2
  6.7 2.4 %collective-permute-start.3 = (bf16[16,4224]{1,0:T(8,128)(2,1)S(1)}, bf16[16,4224]{1,0:T(8,128)(2,1)S(1)}, u32[]{:S(2)}, u32[]{:S(2)}) collective-permute-start(bf16[16,4224]{1,0:T(8,128)(2,1)S(1)} %pad_maximum_fusion.1), channel_id=1, source_target_pairs={{0,4},{1,9},{2,6},{3,11},{4,0},{5,13},{6,2},{7,15},{8,12},{9,1},{1... | collective-permute-start | bytes 405512 | tf_op jit(solution)/shard_map/ppermute | solution.py:396
  9.1 4.0 %collective-permute-done.3 = bf16[16,4224]{1,0:T(8,128)(2,1)S(1)} collective-permute-done((bf16[16,4224]{1,0:T(8,128)(2,1)S(1)}, bf16[16,4224]{1,0:T(8,128)(2,1)S(1)}, u32[]{:S(2)}, u32[]{:S(2)}) %collective-permute-start.3) | collective-permute-done | bytes 135200 | tf_op jit(solution)/shard_map/ppermute | solution.py:396
  13.1 0.6 %collective-permute-start.4 = (bf16[32,4224]{1,0:T(8,128)(2,1)S(1)}, bf16[32,4224]{1,0:T(8,128)(2,1)S(1)}, u32[]{:S(2)}, u32[]{:S(2)}) collective-permute-start(bf16[32,4224]{1,0:T(8,128)(2,1)S(1)} %pad_maximum_fusion.queries.low), channel_id=1, source_target_pairs={{0,2},{1,5},{2,0},{3,7},{4,6},{5,1},{6,4},{7,3},{8,10},{9,13},{10,... | collective-permute-start | bytes 811016 | tf_op jit(solution)/shard_map/ppermute | solution.py:396
  13.8 2.2 %collective-permute-start.5 = (bf16[4,512]{1,0:T(4,128)(2,1)}, bf16[4,512]{1,0:T(4,128)(2,1)S(1)}, u32[]{:S(2)}, u32[]{:S(2)}) collective-permute-start(bf16[4,512]{1,0:T(4,128)(2,1)} %fresh_keys_a.3), channel_id=1, source_target_pairs={{0,1},{1,0},{2,3},{3,2},{4,5},{5,4},{6,7},{7,6},{8,9},{9,8},{10,11... | collective-permute-start | bytes 12296 | tf_op jit(solution)/shard_map/ppermute | solution.py:393
  16.0 0.0 collective-permute-start.6
  16.7 0.4 collective-permute-done.5.fresh_keys_b
  17.0 0.3 collective-permute-done.6.fresh_values_b
  17.4 1.4 %collective-permute-done.4.high.queries = bf16[32,4224]{1,0:T(8,128)(2,1)S(1)} collective-permute-done((bf16[32,4224]{1,0:T(8,128)(2,1)S(1)}, bf16[32,4224]{1,0:T(8,128)(2,1)S(1)}, u32[]{:S(2)}, u32[]{:S(2)}) %collective-permute-start.4) | collective-permute-done | bytes 270368 | tf_op jit(solution)/shard_map/ppermute | solution.py:396
  18.8 0.0 collective-permute-done.7.keys_b
  18.8 0.0 collective-permute-done.8.values_b
  18.8 0.0 copy-start
  18.8 1.4 %copy-done = bf16[1536,512]{1,0:T(8,128)(2,1)S(1)} copy-done((bf16[1536,512]{1,0:T(8,128)(2,1)S(1)}, bf16[1536,512]{1,0:T(8,128)(2,1)}, u32[]{:S(2)}) %copy-start) | copy-done | bytes 1572888
  20.2 0.0 copy-start.1
  20.2 1.4 %copy-done.1 = bf16[1536,512]{1,0:T(8,128)(2,1)S(1)} copy-done((bf16[1536,512]{1,0:T(8,128)(2,1)S(1)}, bf16[1536,512]{1,0:T(8,128)(2,1)}, u32[]{:S(2)}) %copy-start.1) | copy-done | bytes 1572888
  21.6 0.0 copy-start.3
  21.6 0.7 %copy-done.3 = bf16[4,512]{1,0:T(4,128)(2,1)S(1)} copy-done((bf16[4,512]{1,0:T(4,128)(2,1)S(1)}, bf16[4,512]{1,0:T(4,128)(2,1)}, u32[]{:S(2)}) %copy-start.3) | copy-done | bytes 4120
  22.3 0.0 copy-start.4
  22.3 0.7 %copy-done.4 = bf16[4,512]{1,0:T(4,128)(2,1)S(1)} copy-done((bf16[4,512]{1,0:T(4,128)(2,1)S(1)}, bf16[4,512]{1,0:T(4,128)(2,1)}, u32[]{:S(2)}) %copy-start.4) | copy-done | bytes 4120
  23.0 12.1 %shard_map.75 = s16[144,1024]{1,0:T(8,128)(2,1)S(1)} custom-call(s32[1]{0:T(128)S(6)} %copy.9.start, bf16[32,4224]{1,0:T(8,128)(2,1)S(1)} %collective-permute-done.4.high.queries, bf16[32,4224]{1,0:T(8,128)(2,1)S(1)} %pad_maximum_fusion.queries.low, bf16[32,4224]{1,0:T(8,128)(2,1)S(1)} %collective-permute-done.4.high.queries, bf16[4,512]{1,0:T(4,128)(2,1)S(1)} %copy-done.3, ...), custom_call_target="tpu_custom_call" | custom-call | tf_op jit(solution)/shard_map/pallas_call | solution.py:280
  35.1 0.1 collective-permute-start.9
  35.2 12.1 %shard_map.74.left = s16[144,1024]{1,0:T(8,128)(2,1)S(1)} custom-call(s32[1]{0:T(128)S(6)} %copy.9.start, bf16[32,4224]{1,0:T(8,128)(2,1)S(1)} %pad_maximum_fusion.queries.low, bf16[32,4224]{1,0:T(8,128)(2,1)S(1)} %pad_maximum_fusion.queries.low, bf16[32,4224]{1,0:T(8,128)(2,1)S(1)} %collective-permute-done.4.high.queries, bf16[4,512]{1,0:T(4,128)(2,1)S(1)} %copy-done.3, ...), custom_call_target="tpu_custom_call" | custom-call | tf_op jit(solution)/shard_map/pallas_call | solution.py:280
  47.2 0.0 collective-permute-done.9.right
  47.2 0.4 shard_map.76
  47.7 0.1 collective-permute-start.10
  47.8 4.9 %collective-permute-done.10.right = s16[144,512]{1,0:T(8,128)(2,1)S(1)} collective-permute-done((s16[144,512]{1,0:T(8,128)(2,1)S(1)}, s16[144,512]{1,0:T(8,128)(2,1)S(1)}, u32[]{:S(2)}, u32[]{:S(2)}) %collective-permute-start.10) | collective-permute-done | bytes 147488 | tf_op jit(solution)/shard_map/ppermute | solution.py:396
  52.6 0.2 shard_map.77
  52.9 0.1 collective-permute-start.11
  52.9 3.2 %collective-permute-done.11.right = s16[144,256]{1,0:T(8,128)(2,1)S(1)} collective-permute-done((s16[144,256]{1,0:T(8,128)(2,1)S(1)}, s16[144,256]{1,0:T(8,128)(2,1)S(1)}, u32[]{:S(2)}, u32[]{:S(2)}) %collective-permute-start.11) | collective-permute-done | bytes 73760 | tf_op jit(solution)/shard_map/ppermute | solution.py:396
  56.1 0.2 shard_map.78
  56.3 4.7 %collective-permute-start.12 = (bf16[4,4096]{1,0:T(4,128)(2,1)S(1)}, bf16[4,4096]{1,0:T(4,128)(2,1)S(1)}, u32[]{:S(2)}, u32[]{:S(2)}) collective-permute-start(bf16[4,4096]{1,0:T(4,128)(2,1)S(1)} %get-tuple-element.16), channel_id=1, source_target_pairs={{0,1},{1,0},{2,3},{3,2},{4,5},{5,4},{6,7},{7,6},{8,9},{9,8},{10,11... | collective-permute-start | bytes 98312 | tf_op jit(solution)/shard_map/ppermute | solution.py:393
  61.0 0.9 %collective-permute-done.12.theirs = bf16[4,4096]{1,0:T(4,128)(2,1)S(1)} collective-permute-done((bf16[4,4096]{1,0:T(4,128)(2,1)S(1)}, bf16[4,4096]{1,0:T(4,128)(2,1)S(1)}, u32[]{:S(2)}, u32[]{:S(2)}) %collective-permute-start.12) | collective-permute-done | bytes 32800 | tf_op jit(solution)/shard_map/ppermute | solution.py:393
  61.8 0.6 %shard_map.79 = bf16[4,8192]{1,0:T(4,128)(2,1)} custom-call(bf16[4,4096]{1,0:T(4,128)(2,1)S(1)} %get-tuple-element.15.mine, bf16[4,4096]{1,0:T(4,128)(2,1)S(1)} %collective-permute-done.12.theirs), custom_call_target="tpu_custom_call" | custom-call | tf_op jit(solution)/shard_map/pallas_call | solution.py:373
  (2 shorter events, 0.0 us)
Async XLA Ops:
  0.0 2.1 %collective-permute-start.1 = (bf16[4,8192]{1,0:T(4,128)(2,1)}, bf16[4,8192]{1,0:T(4,128)(2,1)S(1)}, u32[]{:S(2)}, u32[]{:S(2)}) collective-permute-start(bf16[4,8192]{1,0:T(4,128)(2,1)} %queries.1), channel_id=1, source_target_pairs={{0,1},{1,0},{2,3},{3,2},{4,5},{5,4},{6,7},{7,6},{8,9},{9,8},{10,11... | collective-permute-start | bytes 196616 | tf_op jit(solution)/shard_map/ppermute | solution.py:393
  0.7 1.4 %collective-permute-start = (s32[1]{0:T(128)}, s32[1]{0:T(128)}, u32[]{:S(2)}, u32[]{:S(2)}) collective-permute-start(s32[1]{0:T(128)} %param.12), channel_id=1, source_target_pairs={{0,1},{1,0},{2,3},{3,2},{4,5},{5,4},{6,7},{7,6},{8,9},{9,8},{10,11... | collective-permute-start | bytes 20 | tf_op jit(solution)/shard_map/ppermute | solution.py:393
  2.1 0.8 %copy-start.2 = (bf16[4,8192]{1,0:T(4,128)(2,1)S(1)}, bf16[4,8192]{1,0:T(4,128)(2,1)}, u32[]{:S(2)}) copy-start(bf16[4,8192]{1,0:T(4,128)(2,1)} %queries.1) | copy-start | bytes 196612
  3.5 3.2 %collective-permute-start.2 = (bf16[8,4224]{1,0:T(8,128)(2,1)S(1)}, bf16[8,4224]{1,0:T(8,128)(2,1)S(1)}, u32[]{:S(2)}, u32[]{:S(2)}) collective-permute-start(bf16[8,4224]{1,0:T(8,128)(2,1)S(1)} %shard_map.73), channel_id=1, source_target_pairs={{0,8},{1,3},{2,10},{3,1},{4,12},{5,7},{6,14},{7,5},{8,0},{9,11},{1... | collective-permute-start | bytes 202760 | tf_op jit(solution)/shard_map/ppermute | solution.py:396
  4.8 14.0 %collective-permute-start.7 = (bf16[1536,512]{1,0:T(8,128)(2,1)}, bf16[1536,512]{1,0:T(8,128)(2,1)S(1)}, u32[]{:S(2)}, u32[]{:S(2)}) collective-permute-start(bf16[1536,512]{1,0:T(8,128)(2,1)} %keys_a.3), channel_id=1, source_target_pairs={{0,1},{1,0},{2,3},{3,2},{4,5},{5,4},{6,7},{7,6},{8,9},{9,8},{10,11... | collective-permute-start | bytes 4718600 | tf_op jit(solution)/shard_map/ppermute | solution.py:393
  6.4 12.4 %collective-permute-start.8 = (bf16[1536,512]{1,0:T(8,128)(2,1)}, bf16[1536,512]{1,0:T(8,128)(2,1)S(1)}, u32[]{:S(2)}, u32[]{:S(2)}) collective-permute-start(bf16[1536,512]{1,0:T(8,128)(2,1)} %values_a.3), channel_id=1, source_target_pairs={{0,1},{1,0},{2,3},{3,2},{4,5},{5,4},{6,7},{7,6},{8,9},{9,8},{10,11... | collective-permute-start | bytes 4718600 | tf_op jit(solution)/shard_map/ppermute | solution.py:393
  6.7 6.4 %collective-permute-start.3 = (bf16[16,4224]{1,0:T(8,128)(2,1)S(1)}, bf16[16,4224]{1,0:T(8,128)(2,1)S(1)}, u32[]{:S(2)}, u32[]{:S(2)}) collective-permute-start(bf16[16,4224]{1,0:T(8,128)(2,1)S(1)} %pad_maximum_fusion.1), channel_id=1, source_target_pairs={{0,4},{1,9},{2,6},{3,11},{4,0},{5,13},{6,2},{7,15},{8,12},{9,1},{1... | collective-permute-start | bytes 405512 | tf_op jit(solution)/shard_map/ppermute | solution.py:396
  13.1 5.7 %collective-permute-start.4 = (bf16[32,4224]{1,0:T(8,128)(2,1)S(1)}, bf16[32,4224]{1,0:T(8,128)(2,1)S(1)}, u32[]{:S(2)}, u32[]{:S(2)}) collective-permute-start(bf16[32,4224]{1,0:T(8,128)(2,1)S(1)} %pad_maximum_fusion.queries.low), channel_id=1, source_target_pairs={{0,2},{1,5},{2,0},{3,7},{4,6},{5,1},{6,4},{7,3},{8,10},{9,13},{10,... | collective-permute-start | bytes 811016 | tf_op jit(solution)/shard_map/ppermute | solution.py:396
  13.8 3.3 %collective-permute-start.5 = (bf16[4,512]{1,0:T(4,128)(2,1)}, bf16[4,512]{1,0:T(4,128)(2,1)S(1)}, u32[]{:S(2)}, u32[]{:S(2)}) collective-permute-start(bf16[4,512]{1,0:T(4,128)(2,1)} %fresh_keys_a.3), channel_id=1, source_target_pairs={{0,1},{1,0},{2,3},{3,2},{4,5},{5,4},{6,7},{7,6},{8,9},{9,8},{10,11... | collective-permute-start | bytes 12296 | tf_op jit(solution)/shard_map/ppermute | solution.py:393
  16.0 1.4 %collective-permute-start.6 = (bf16[4,512]{1,0:T(4,128)(2,1)}, bf16[4,512]{1,0:T(4,128)(2,1)S(1)}, u32[]{:S(2)}, u32[]{:S(2)}) collective-permute-start(bf16[4,512]{1,0:T(4,128)(2,1)} %fresh_values_a.3), channel_id=1, source_target_pairs={{0,1},{1,0},{2,3},{3,2},{4,5},{5,4},{6,7},{7,6},{8,9},{9,8},{10,11... | collective-permute-start | bytes 12296 | tf_op jit(solution)/shard_map/ppermute | solution.py:393
  18.8 1.4 %copy-start = (bf16[1536,512]{1,0:T(8,128)(2,1)S(1)}, bf16[1536,512]{1,0:T(8,128)(2,1)}, u32[]{:S(2)}) copy-start(bf16[1536,512]{1,0:T(8,128)(2,1)} %keys_a.3) | copy-start | bytes 4718596
  20.2 1.4 %copy-start.1 = (bf16[1536,512]{1,0:T(8,128)(2,1)S(1)}, bf16[1536,512]{1,0:T(8,128)(2,1)}, u32[]{:S(2)}) copy-start(bf16[1536,512]{1,0:T(8,128)(2,1)} %values_a.3) | copy-start | bytes 4718596
  21.6 0.7 %copy-start.3 = (bf16[4,512]{1,0:T(4,128)(2,1)S(1)}, bf16[4,512]{1,0:T(4,128)(2,1)}, u32[]{:S(2)}) copy-start(bf16[4,512]{1,0:T(4,128)(2,1)} %fresh_keys_a.3) | copy-start | bytes 12292
  22.3 0.7 %copy-start.4 = (bf16[4,512]{1,0:T(4,128)(2,1)S(1)}, bf16[4,512]{1,0:T(4,128)(2,1)}, u32[]{:S(2)}) copy-start(bf16[4,512]{1,0:T(4,128)(2,1)} %fresh_values_a.3) | copy-start | bytes 12292
  35.1 12.1 %collective-permute-start.9 = (s16[144,1024]{1,0:T(8,128)(2,1)S(1)}, s16[144,1024]{1,0:T(8,128)(2,1)S(1)}, u32[]{:S(2)}, u32[]{:S(2)}) collective-permute-start(s16[144,1024]{1,0:T(8,128)(2,1)S(1)} %shard_map.75), channel_id=1, source_target_pairs={{0,2},{1,5},{2,0},{3,7},{4,6},{5,1},{6,4},{7,3},{8,10},{9,13},{10,... | collective-permute-start | bytes 884744 | tf_op jit(solution)/shard_map/ppermute | solution.py:396
  47.7 5.0 %collective-permute-start.10 = (s16[144,512]{1,0:T(8,128)(2,1)S(1)}, s16[144,512]{1,0:T(8,128)(2,1)S(1)}, u32[]{:S(2)}, u32[]{:S(2)}) collective-permute-start(s16[144,512]{1,0:T(8,128)(2,1)S(1)} %get-tuple-element.12), channel_id=1, source_target_pairs={{0,4},{1,9},{2,6},{3,11},{4,0},{5,13},{6,2},{7,15},{8,12},{9,1},{1... | collective-permute-start | bytes 442376 | tf_op jit(solution)/shard_map/ppermute | solution.py:396
  52.9 3.3 %collective-permute-start.11 = (s16[144,256]{1,0:T(8,128)(2,1)S(1)}, s16[144,256]{1,0:T(8,128)(2,1)S(1)}, u32[]{:S(2)}, u32[]{:S(2)}) collective-permute-start(s16[144,256]{1,0:T(8,128)(2,1)S(1)} %get-tuple-element.14), channel_id=1, source_target_pairs={{0,8},{1,3},{2,10},{3,1},{4,12},{5,7},{6,14},{7,5},{8,0},{9,11},{1... | collective-permute-start | bytes 221192 | tf_op jit(solution)/shard_map/ppermute | solution.py:396
  56.3 5.5 %collective-permute-start.12 = (bf16[4,4096]{1,0:T(4,128)(2,1)S(1)}, bf16[4,4096]{1,0:T(4,128)(2,1)S(1)}, u32[]{:S(2)}, u32[]{:S(2)}) collective-permute-start(bf16[4,4096]{1,0:T(4,128)(2,1)S(1)} %get-tuple-element.16), channel_id=1, source_target_pairs={{0,1},{1,0},{2,3},{3,2},{4,5},{5,4},{6,7},{7,6},{8,9},{9,8},{10,11... | collective-permute-start | bytes 98312 | tf_op jit(solution)/shard_map/ppermute | solution.py:393

commit v3 on v2

--- a/solution.py
+++ b/solution.py
@@ -12,7 +12,8 @@
 LANES = 128
 CORES = 2
 FLOOR = -1e30
-KEY_TILE = 256
+TILES = (1024, 512)
+TAIL = 256
 STAT_ROWS = 16
 CHUNK_BLOCKS = 4
 STEP = 2.0**15
@@ -24,6 +25,7 @@
 VMEM = pl.BlockSpec(memory_space=pltpu.VMEM)
 SMEM = pl.BlockSpec(memory_space=pltpu.SMEM)
 HBM = pl.BlockSpec(memory_space=pltpu.HBM)
+ANY = pl.BlockSpec(memory_space=pl.ANY)
 SMALL = pltpu.CompilerParams(vmem_limit_bytes=8 << 20)
 
 
@@ -67,19 +69,24 @@
     return top, total, jnp.exp2(part(4) - 15.0) * (1.0 / MARGIN)
 
 
-def join_kernel(length, length_other, queries, queries_other, out):
-    rows = queries.shape[0]
-    half = queries.shape[1] // CORES
+def join_kernel(length, length_other, queries, queries_other, out, mine, other, arrived):
+    rows, half = mine.shape
     core = lax.axis_index("ctx") % CORES
     at = pl.multiple_of(core * half, LANES)
-    mine = queries[:, pl.ds(at, half)].astype(F32)
-    other = queries_other[:, pl.ds(at, half)].astype(F32)
-    out[:, :half] = jnp.concatenate([mine, other], axis=0).astype(BF16)
+    copies = [
+        pltpu.make_async_copy(source.at[:, pl.ds(at, half)], target, arrived.at[i])
+        for i, (source, target) in enumerate(((queries, mine), (queries_other, other)))
+    ]
+    for copy in copies:
+        copy.start()
     lane = lax.broadcasted_iota(I32, (CORES * rows, LANES), 1)
     row = lax.broadcasted_iota(I32, (CORES * rows, LANES), 0)
     count = jnp.where(row < rows, length[0], length_other[0])
     coded = jnp.where(lane == 0, count // LANES, jnp.where(lane == 1, count % LANES, 0))
     out[:, half:] = coded.astype(F32).astype(BF16)
+    for copy in copies:
+        copy.wait()
+    out[:, :half] = jnp.concatenate([mine[...].astype(F32), other[...].astype(F32)], axis=0).astype(BF16)
 
 
 def join(length, length_other, queries, queries_other):
@@ -87,15 +94,20 @@
     return pl.pallas_call(
         join_kernel,
         out_shape=jax.ShapeDtypeStruct((CORES * rows, wide // CORES + LANES), BF16),
-        in_specs=[SMEM, SMEM, VMEM, VMEM],
+        in_specs=[SMEM, SMEM, HBM, ANY],
         out_specs=VMEM,
+        scratch_shapes=[
+            pltpu.VMEM((rows, wide // CORES), BF16),
+            pltpu.VMEM((rows, wide // CORES), BF16),
+            pltpu.SemaphoreType.DMA((2,)),
+        ],
         compiler_params=SMALL,
     )(length, length_other, queries, queries_other)
 
 
 def attend_kernel(
-    sizes, start, queries, low, high, fresh_keys_a, fresh_keys_b, fresh_values_a, fresh_values_b,
-    keys_a, keys_b, values_a, values_b, out, query_t, scores, sums, kv, arrived
+    sizes, start, queries, low, high, new_keys_a, new_keys_b, new_values_a, new_values_b,
+    keys_a, keys_b, values_a, values_b, out, query_t, scores, sums, tops, totals, fresh, kv, fresh_arrived, arrived
 ):
     own_rows, orders, first_block, group, kv_heads = sizes
     chip_rows = CORES * own_rows
@@ -113,8 +125,15 @@
         source = (keys_a, keys_b, values_a, values_b)[i]
         return pltpu.make_async_copy(source.at[:, pl.ds(at, LANES)], kv.at[h, i], arrived.at[h, i])
 
+    fresh_copies = [
+        pltpu.make_async_copy(source, fresh.at[i], fresh_arrived.at[i])
+        for i, source in enumerate((new_keys_a, new_keys_b, new_values_a, new_values_b))
+    ]
+
     @pl.when(chunk == 0)
     def _():
+        for fresh_copy in fresh_copies:
+            fresh_copy.start()
         for h in range(kv_heads):
             for i in range(4):
                 copy(h, i).start()
@@ -157,10 +176,16 @@
     block = lane // (group * chip_rows) + (first_block + chunk * blocks)
     token = (origin(block) * CORES + (core ^ (inside // own_rows))) * own_rows + inside % own_rows
     causal = key_id <= token
-    key_slot = lax.broadcasted_iota(I32, (KEY_TILE, lanes), 0)
     nothing = jnp.zeros((16 - chip_rows % 16, LANES), F32)
-
-    for h in range(kv_heads):
+    heads = range(kv_heads)
+    fresh_scores, fresh_values = [], []
+
+    @pl.when(chunk == 0)
+    def _():
+        for fresh_copy in fresh_copies:
+            fresh_copy.wait()
+
+    for h in heads:
         first = h * group
         q = jnp.concatenate(
             [
@@ -170,94 +195,92 @@
             ],
             axis=0,
         )
-        query_t[...] = q.T.astype(BF16)
+        query_t[h] = q.T.astype(BF16)
         at = pl.multiple_of((core * kv_heads + h) * LANES, LANES)
 
-        def fresh(a, b):
-            return jnp.concatenate([a[:, pl.ds(at, LANES)].astype(F32), b[:, pl.ds(at, LANES)].astype(F32), nothing], 0)
-
-        new_keys = fresh(fresh_keys_a, fresh_keys_b).astype(BF16)
-        new_values = fresh(fresh_values_a, fresh_values_b).astype(BF16)
-        new_scores = jnp.dot(new_keys, query_t[...], preferred_element_type=F32)[:chip_rows] * factor
-
-        @pl.when(chunk == 0)
-        def _():
-            for i in range(2):
+        def both(i):
+            rows = [fresh[i + s, :, pl.ds(at, LANES)].astype(F32) for s in range(2)]
+            return jnp.concatenate(rows + [nothing], 0).astype(BF16)
+
+        new_keys = both(0)
+        fresh_values.append(both(2))
+        fresh_scores.append(jnp.dot(new_keys, query_t[h], preferred_element_type=F32)[:chip_rows] * factor)
+
+    @pl.when(chunk == 0)
+    def _():
+        for h in heads:
+            for i in range(4):
                 copy(h, i).wait()
 
-        def fold(tile, combine):
-            return combine(tile.reshape(KEY_TILE // 8, 8, lanes), axis=0)
-
-        tops = []
-        for s in range(2):
-            limit = limits[s]
-            whole = limit // KEY_TILE
-            seen = causal & (part == s)
-            peak = jnp.where(seen, new_scores, FLOOR)
-
-            def score(j):
-                at = pl.multiple_of(j * KEY_TILE, KEY_TILE)
-                return jnp.dot(kv[h, s, pl.ds(at, KEY_TILE), :], query_t[...], preferred_element_type=F32) * factor
-
-            def first_pass(j, peak):
-                tile = score(j)
-                scores[s, j] = tile
-                return jnp.maximum(peak, fold(tile, jnp.max))
-
-            peak = lax.fori_loop(0, whole, first_pass, peak)
-
-            def last_tile(peak):
-                tile = jnp.where(key_slot < limit - whole * KEY_TILE, score(whole), FLOOR)
-                scores[s, whole] = tile
-                return jnp.maximum(peak, fold(tile, jnp.max))
-
-            peak = lax.cond(limit > whole * KEY_TILE, last_tile, lambda peak: peak, peak)
-            tops.append(jnp.max(peak, axis=0, keepdims=True))
-
-        @pl.when(chunk == 0)
-        def _():
-            for i in range(2, 4):
-                copy(h, i).wait()
-
+    def fold(tile, combine):
+        return combine(tile.reshape(tile.shape[0] // 8, 8, lanes), axis=0)
+
+    def each_tile(limit, body, carry):
+        base, rest = 0, limit
+        for rows in TILES:
+            count = rest // rows
+
+            def whole(j, carry, rows=rows, base=base):
+                return body(pl.multiple_of(base + j * rows, TILES[-1]), rows, None, carry)
+
+            carry = lax.fori_loop(0, count, whole, carry)
+            base, rest = base + count * rows, rest - count * rows
+        base = pl.multiple_of(base, TILES[-1])
+        for rows, need in ((TAIL, (rest > 0) & (rest <= TAIL)), (TILES[-1], rest > TAIL)):
+            carry = lax.cond(need, lambda c, rows=rows: body(base, rows, rest, c), lambda c: c, carry)
+        return carry
+
+    tn = (((0,), (0,)), ((), ()))
+
+    def shard(s, carry):
+        limit = jnp.where(s == 0, limits[0], limits[1])
+        seen = causal & (part == s)
+
+        def first_pass(base, rows, filled, peaks):
+            higher = []
+            for h in heads:
+                tile = jnp.dot(kv[h, s, pl.ds(base, rows), :], query_t[h], preferred_element_type=F32) * factor
+                if filled is not None:
+                    tile = jnp.where(lax.broadcasted_iota(I32, (rows, lanes), 0) < filled, tile, FLOOR)
+                scores[h, pl.ds(base, rows), :] = tile
+                higher.append(jnp.maximum(peaks[h], fold(tile, jnp.max)))
+            return tuple(higher)
+
+        peaks = each_tile(limit, first_pass, tuple(jnp.where(seen, x, FLOOR) for x in fresh_scores))
+        top = [jnp.max(x, axis=0, keepdims=True) for x in peaks]
         masses = []
-        for s in range(2):
-            limit = limits[s]
-            whole = limit // KEY_TILE
-            seen = causal & (part == s)
-            top = tops[s]
-            weight = jnp.where(seen, jnp.exp2(new_scores - top), 0.0)
+        for h in heads:
+            weight = jnp.where(seen, jnp.exp2(fresh_scores[h] - top[h]), 0.0)
             padded = jnp.concatenate([weight, jnp.zeros((16 - chip_rows % 16, lanes), F32)], 0).astype(BF16)
-            tn = (((0,), (0,)), ((), ()))
-            sums[s] = lax.dot_general(new_values, padded, tn, preferred_element_type=F32)
-
-            def add(j, weight):
-                at = pl.multiple_of(j * KEY_TILE, KEY_TILE)
-                sums[s] += lax.dot_general(
-                    kv[h, 2 + s, pl.ds(at, KEY_TILE), :], weight.astype(BF16), tn, preferred_element_type=F32
+            sums[s, h] = lax.dot_general(fresh_values[h], padded, tn, preferred_element_type=F32)
+            masses.append(weight)
+
+        def second_pass(base, rows, filled, masses):
+            more = []
+            for h in heads:
+                weight = jnp.exp2(scores[h, pl.ds(base, rows), :] - top[h])
+                if filled is not None:
+                    weight = jnp.where(lax.broadcasted_iota(I32, (rows, lanes), 0) < filled, weight, 0.0)
+                sums[s, h] += lax.dot_general(
+                    kv[h, 2 + s, pl.ds(base, rows), :], weight.astype(BF16), tn, preferred_element_type=F32
                 )
-
-            def second_pass(j, mass):
-                weight = jnp.exp2(scores[s, j] - top)
-                add(j, weight)
-                return mass + fold(weight, jnp.sum)
-
-            mass = lax.fori_loop(0, whole, second_pass, weight)
-
-            def last_tile(mass):
-                weight = jnp.where(
-                    key_slot < limit - whole * KEY_TILE, jnp.exp2(scores[s, whole] - top), 0.0
-                )
-                add(whole, weight)
-                return mass + fold(weight, jnp.sum)
-
-            mass = lax.cond(limit > whole * KEY_TILE, last_tile, lambda mass: mass, mass)
-            masses.append(jnp.sum(mass, axis=0, keepdims=True))
-
-        top = jnp.maximum(tops[0], tops[1])
-        scale_a = jnp.exp2(tops[0] - top)
-        scale_b = jnp.exp2(tops[1] - top)
-        total = jnp.maximum(masses[0] * scale_a + masses[1] * scale_b, 1.0)
-        merged = sums[0] * (scale_a / total) + sums[1] * (scale_b / total)
+                more.append(masses[h] + fold(weight, jnp.sum))
+            return tuple(more)
+
+        masses = each_tile(limit, second_pass, tuple(masses))
+        for h in heads:
+            tops[s, h] = top[h]
+            totals[s, h] = jnp.sum(masses[h], axis=0, keepdims=True)
+        return carry
+
+    lax.fori_loop(0, 2, shard, 0)
+    for h in heads:
+        top_a, top_b = tops[0, h], tops[1, h]
+        top = jnp.maximum(top_a, top_b)
+        scale_a = jnp.exp2(top_a - top)
+        scale_b = jnp.exp2(top_b - top)
+        total = jnp.maximum(totals[0, h] * scale_a + totals[1, h] * scale_b, 1.0)
+        merged = sums[0, h] * (scale_a / total) + sums[1, h] * (scale_b / total)
         width = group * chip_rows
         for b in range(blocks):
             cut = slice(b * width, (b + 1) * width)
@@ -275,7 +298,7 @@
     heads = queries.shape[1] // LANES - 1
     group = heads // kv_heads
     lanes = tokens * group
-    tiles = -(-slots // KEY_TILE)
+    padded = -(-slots // TILES[-1]) * TILES[-1]
     sizes = (own_rows, orders, first_block, group, kv_heads)
     return pl.pallas_call(
         functools.partial(attend_kernel, sizes),
@@ -286,15 +309,19 @@
             pl.BlockSpec((tokens, heads * LANES), lambda i: (i, 0)),
             pl.BlockSpec((low.shape[0], LANES), lambda i: (0, heads)),
             pl.BlockSpec((high.shape[0], LANES), lambda i: (0, heads)),
-            VMEM, VMEM, VMEM, VMEM,
-            HBM, HBM, HBM, HBM,
+            HBM, ANY, HBM, ANY,
+            HBM, ANY, HBM, ANY,
         ],
         out_specs=pl.BlockSpec((LANES + STAT_ROWS, tokens * heads), lambda i: (0, i)),
         scratch_shapes=[
-            pltpu.VMEM((LANES, lanes), BF16),
-            pltpu.VMEM((2, tiles, KEY_TILE, lanes), F32),
-            pltpu.VMEM((2, LANES, lanes), F32),
-            pltpu.VMEM((kv_heads, 4, tiles * KEY_TILE, LANES), BF16),
+            pltpu.VMEM((kv_heads, LANES, lanes), BF16),
+            pltpu.VMEM((kv_heads, padded, lanes), F32),
+            pltpu.VMEM((2, kv_heads, LANES, lanes), F32),
+            pltpu.VMEM((2, kv_heads, 1, lanes), F32),
+            pltpu.VMEM((2, kv_heads, 1, lanes), F32),
+            pltpu.VMEM((4,) + fresh[0].shape, BF16),
+            pltpu.VMEM((kv_heads, 4, padded, LANES), BF16),
+            pltpu.SemaphoreType.DMA((4,)),
             pltpu.SemaphoreType.DMA((kv_heads, 4)),
         ],
         compiler_params=pltpu.CompilerParams(vmem_limit_bytes=32 << 20),

time: 63.6 us -> 53.6 us (0.84)
  the two profiles are of different devices: /device:TPU:3 before, /device:TPU:0 now
where the time goes in v3:
time: 53.6 us; the launch traced here: 53.3 us
  starting transfers between devices  18.6 us (35%)
  waiting for transfers between devices  16.9 us (32%)
  Pallas kernels  11.5 us (21%)
  local copies, waits for them, and re-layouts  5.03 us (9%)
  between operations  1.37 us (3%)
    ppermute x6, starting transfers between devices, exchange(): lax.ppermute(x, 'ctx', [(i, i ^ orders[i % CORES][stage]) for i in range(...  17 us
    ppermute x6, waiting for transfers between devices, exchange(): lax.ppermute(x, 'ctx', [(i, i ^ orders[i % CORES][stage]) for i in range(...  14.6 us
    pallas_call x2, Pallas kernels, attend(): pl.pallas_call(functools.partial(attend_kernel, sizes), out_shape=jax.Sha...  9.33 us
    unnamed x10, local copies, waits for them, and re-layouts  5.03 us
    ppermute x7, waiting for transfers between devices, swap(): return lax.ppermute(x, 'ctx', [(i, i ^ 1) for i in range(width)])  2.26 us
    ppermute x7, starting transfers between devices, swap(): return lax.ppermute(x, 'ctx', [(i, i ^ 1) for i in range(width)])  1.6 us
  transfers between devices with their start and end apart: 13, of which 9 were waited for; matrix products, arithmetic and copies ran while one was open for 0% of the time, Pallas kernels for 9%

profile of v3, /device:TPU:0, one launch (start us, length us, event | category | flops | bytes accessed | tf_op | source)
XLA Modules:
  0.0 53.3 jit_solution(1845338875358965068)
XLA Ops:
  0.0 0.5 collective-permute-start.1
  0.5 0.1 collective-permute-start
  1.2 0.7 %collective-permute-done.length_other = s32[1]{0:T(128)} collective-permute-done((s32[1]{0:T(128)}, s32[1]{0:T(128)}, u32[]{:S(2)}, u32[]{:S(2)}) %collective-permute-start) | collective-permute-done | bytes 36 | tf_op jit(solution)/shard_map/ppermute | solution.py:420
  1.8 0.0 collective-permute-done.1.queries_other
  1.8 0.0 copy-start.2
  1.8 0.8 %copy-done.2 = bf16[4,8192]{1,0:T(4,128)(2,1)S(1)} copy-done((bf16[4,8192]{1,0:T(4,128)(2,1)S(1)}, bf16[4,8192]{1,0:T(4,128)(2,1)}, u32[]{:S(2)}) %copy-start.2) | copy-done | bytes 65560
  2.7 0.7 %shard_map.73 = bf16[8,4224]{1,0:T(8,128)(2,1)S(1)} custom-call(s32[1]{0:T(128)S(6)} %copy.8.length, s32[1]{0:T(128)} %collective-permute-done.length_other, bf16[4,8192]{1,0:T(4,128)(2,1)S(1)} %copy-done.2, bf16[4,8192]{1,0:T(4,128)(2,1)S(1)} %collective-permute-done.1.queries_other), custom_call_target="tpu_custom_call" | custom-call | tf_op jit(solution)/shard_map/pallas_call | solution.py:94
  3.4 3.9 %collective-permute-start.2 = (bf16[8,4224]{1,0:T(8,128)(2,1)S(1)}, bf16[8,4224]{1,0:T(8,128)(2,1)S(1)}, u32[]{:S(2)}, u32[]{:S(2)}) collective-permute-start(bf16[8,4224]{1,0:T(8,128)(2,1)S(1)} %shard_map.73), channel_id=1, source_target_pairs={{0,8},{1,3},{2,10},{3,1},{4,12},{5,7},{6,14},{7,5},{8,0},{9,11},{1... | collective-permute-start | bytes 202760 | tf_op jit(solution)/shard_map/ppermute | solution.py:423
  7.3 0.0 collective-permute-start.7
  7.3 0.5 collective-permute-start.8
  7.8 1.8 %collective-permute-done.2 = bf16[8,4224]{1,0:T(8,128)(2,1)S(1)} collective-permute-done((bf16[8,4224]{1,0:T(8,128)(2,1)S(1)}, bf16[8,4224]{1,0:T(8,128)(2,1)S(1)}, u32[]{:S(2)}, u32[]{:S(2)}) %collective-permute-start.2) | collective-permute-done | bytes 67616 | tf_op jit(solution)/shard_map/ppermute | solution.py:423
  9.5 2.0 %collective-permute-start.3 = (bf16[16,4224]{1,0:T(8,128)(2,1)S(1)}, bf16[16,4224]{1,0:T(8,128)(2,1)S(1)}, u32[]{:S(2)}, u32[]{:S(2)}) collective-permute-start(bf16[16,4224]{1,0:T(8,128)(2,1)S(1)} %pad_maximum_fusion.1), channel_id=1, source_target_pairs={{0,4},{1,9},{2,6},{3,11},{4,0},{5,13},{6,2},{7,15},{8,12},{9,1},{1... | collective-permute-start | bytes 405512 | tf_op jit(solution)/shard_map/ppermute | solution.py:423
  11.5 3.4 %collective-permute-done.3 = bf16[16,4224]{1,0:T(8,128)(2,1)S(1)} collective-permute-done((bf16[16,4224]{1,0:T(8,128)(2,1)S(1)}, bf16[16,4224]{1,0:T(8,128)(2,1)S(1)}, u32[]{:S(2)}, u32[]{:S(2)}) %collective-permute-start.3) | collective-permute-done | bytes 135200 | tf_op jit(solution)/shard_map/ppermute | solution.py:423
  14.9 2.0 %collective-permute-start.4 = (bf16[32,4224]{1,0:T(8,128)(2,1)S(1)}, bf16[32,4224]{1,0:T(8,128)(2,1)S(1)}, u32[]{:S(2)}, u32[]{:S(2)}) collective-permute-start(bf16[32,4224]{1,0:T(8,128)(2,1)S(1)} %pad_maximum_fusion.queries.low), channel_id=1, source_target_pairs={{0,2},{1,5},{2,0},{3,7},{4,6},{5,1},{6,4},{7,3},{8,10},{9,13},{10,... | collective-permute-start | bytes 811016 | tf_op jit(solution)/shard_map/ppermute | solution.py:423
  16.9 0.0 collective-permute-start.5
  16.9 0.5 collective-permute-start.6
  18.1 0.2 collective-permute-done.5.new_keys_b
  18.3 0.2 collective-permute-done.6.new_values_b
  18.4 3.0 %collective-permute-done.4.high.queries = bf16[32,4224]{1,0:T(8,128)(2,1)S(1)} collective-permute-done((bf16[32,4224]{1,0:T(8,128)(2,1)S(1)}, bf16[32,4224]{1,0:T(8,128)(2,1)S(1)}, u32[]{:S(2)}, u32[]{:S(2)}) %collective-permute-start.4) | collective-permute-done | bytes 270368 | tf_op jit(solution)/shard_map/ppermute | solution.py:423
  21.5 0.0 collective-permute-done.7.keys_b
  21.5 0.0 collective-permute-done.8.values_b
  21.5 0.0 copy-start
  21.5 1.4 %copy-done = bf16[1536,512]{1,0:T(8,128)(2,1)S(1)} copy-done((bf16[1536,512]{1,0:T(8,128)(2,1)S(1)}, bf16[1536,512]{1,0:T(8,128)(2,1)}, u32[]{:S(2)}) %copy-start) | copy-done | bytes 1572888
  22.9 0.0 copy-start.1
  22.9 1.4 %copy-done.1 = bf16[1536,512]{1,0:T(8,128)(2,1)S(1)} copy-done((bf16[1536,512]{1,0:T(8,128)(2,1)S(1)}, bf16[1536,512]{1,0:T(8,128)(2,1)}, u32[]{:S(2)}) %copy-start.1) | copy-done | bytes 1572888
  24.3 0.0 copy-start.3
  24.3 0.7 %copy-done.3 = bf16[4,512]{1,0:T(4,128)(2,1)S(1)} copy-done((bf16[4,512]{1,0:T(4,128)(2,1)S(1)}, bf16[4,512]{1,0:T(4,128)(2,1)}, u32[]{:S(2)}) %copy-start.3) | copy-done | bytes 4120
  25.0 0.0 copy-start.4
  25.0 0.7 %copy-done.4 = bf16[4,512]{1,0:T(4,128)(2,1)S(1)} copy-done((bf16[4,512]{1,0:T(4,128)(2,1)S(1)}, bf16[4,512]{1,0:T(4,128)(2,1)}, u32[]{:S(2)}) %copy-start.4) | copy-done | bytes 4120
  25.7 4.7 %shard_map.75 = s16[144,1024]{1,0:T(8,128)(2,1)S(1)} custom-call(s32[1]{0:T(128)S(6)} %copy.9.start, bf16[32,4224]{1,0:T(8,128)(2,1)S(1)} %collective-permute-done.4.high.queries, bf16[32,4224]{1,0:T(8,128)(2,1)S(1)} %pad_maximum_fusion.queries.low, bf16[32,4224]{1,0:T(8,128)(2,1)S(1)} %collective-permute-done.4.high.queries, bf16[4,512]{1,0:T(4,128)(2,1)S(1)} %copy-done.3, ...), custom_call_target="tpu_custom_call" | custom-call | tf_op jit(solution)/shard_map/pallas_call | solution.py:303
  30.3 2.8 %collective-permute-start.9 = (s16[144,1024]{1,0:T(8,128)(2,1)S(1)}, s16[144,1024]{1,0:T(8,128)(2,1)S(1)}, u32[]{:S(2)}, u32[]{:S(2)}) collective-permute-start(s16[144,1024]{1,0:T(8,128)(2,1)S(1)} %shard_map.75), channel_id=1, source_target_pairs={{0,2},{1,5},{2,0},{3,7},{4,6},{5,1},{6,4},{7,3},{8,10},{9,13},{10,... | collective-permute-start | bytes 884744 | tf_op jit(solution)/shard_map/ppermute | solution.py:423
  33.2 4.7 %shard_map.74.left = s16[144,1024]{1,0:T(8,128)(2,1)S(1)} custom-call(s32[1]{0:T(128)S(6)} %copy.9.start, bf16[32,4224]{1,0:T(8,128)(2,1)S(1)} %pad_maximum_fusion.queries.low, bf16[32,4224]{1,0:T(8,128)(2,1)S(1)} %pad_maximum_fusion.queries.low, bf16[32,4224]{1,0:T(8,128)(2,1)S(1)} %collective-permute-done.4.high.queries, bf16[4,512]{1,0:T(4,128)(2,1)S(1)} %copy-done.3, ...), custom_call_target="tpu_custom_call" | custom-call | tf_op jit(solution)/shard_map/pallas_call | solution.py:303
  37.8 0.0 collective-permute-done.9.right
  37.9 0.4 shard_map.76
  38.3 3.4 %collective-permute-start.10 = (s16[144,512]{1,0:T(8,128)(2,1)S(1)}, s16[144,512]{1,0:T(8,128)(2,1)S(1)}, u32[]{:S(2)}, u32[]{:S(2)}) collective-permute-start(s16[144,512]{1,0:T(8,128)(2,1)S(1)} %get-tuple-element.12), channel_id=1, source_target_pairs={{0,4},{1,9},{2,6},{3,11},{4,0},{5,13},{6,2},{7,15},{8,12},{9,1},{1... | collective-permute-start | bytes 442376 | tf_op jit(solution)/shard_map/ppermute | solution.py:423
  41.7 4.0 %collective-permute-done.10.right = s16[144,512]{1,0:T(8,128)(2,1)S(1)} collective-permute-done((s16[144,512]{1,0:T(8,128)(2,1)S(1)}, s16[144,512]{1,0:T(8,128)(2,1)S(1)}, u32[]{:S(2)}, u32[]{:S(2)}) %collective-permute-start.10) | collective-permute-done | bytes 147488 | tf_op jit(solution)/shard_map/ppermute | solution.py:423
  45.7 0.2 shard_map.77
  46.0 2.9 %collective-permute-start.11 = (s16[144,256]{1,0:T(8,128)(2,1)S(1)}, s16[144,256]{1,0:T(8,128)(2,1)S(1)}, u32[]{:S(2)}, u32[]{:S(2)}) collective-permute-start(s16[144,256]{1,0:T(8,128)(2,1)S(1)} %get-tuple-element.14), channel_id=1, source_target_pairs={{0,8},{1,3},{2,10},{3,1},{4,12},{5,7},{6,14},{7,5},{8,0},{9,11},{1... | collective-permute-start | bytes 221192 | tf_op jit(solution)/shard_map/ppermute | solution.py:423
  48.9 2.4 %collective-permute-done.11.right = s16[144,256]{1,0:T(8,128)(2,1)S(1)} collective-permute-done((s16[144,256]{1,0:T(8,128)(2,1)S(1)}, s16[144,256]{1,0:T(8,128)(2,1)S(1)}, u32[]{:S(2)}, u32[]{:S(2)}) %collective-permute-start.11) | collective-permute-done | bytes 73760 | tf_op jit(solution)/shard_map/ppermute | solution.py:423
  51.3 0.2 shard_map.78
  51.4 0.1 collective-permute-start.12
  51.5 1.2 %collective-permute-done.12.theirs = bf16[4,4096]{1,0:T(4,128)(2,1)S(1)} collective-permute-done((bf16[4,4096]{1,0:T(4,128)(2,1)S(1)}, bf16[4,4096]{1,0:T(4,128)(2,1)S(1)}, u32[]{:S(2)}, u32[]{:S(2)}) %collective-permute-start.12) | collective-permute-done | bytes 32800 | tf_op jit(solution)/shard_map/ppermute | solution.py:420
  52.7 0.6 %shard_map.79 = bf16[4,8192]{1,0:T(4,128)(2,1)} custom-call(bf16[4,4096]{1,0:T(4,128)(2,1)S(1)} %get-tuple-element.15.mine, bf16[4,4096]{1,0:T(4,128)(2,1)S(1)} %collective-permute-done.12.theirs), custom_call_target="tpu_custom_call" | custom-call | tf_op jit(solution)/shard_map/pallas_call | solution.py:400
  (2 shorter events, 0.0 us)
Async XLA Ops:
  0.0 1.8 %collective-permute-start.1 = (bf16[4,8192]{1,0:T(4,128)(2,1)}, bf16[4,8192]{1,0:T(4,128)(2,1)S(1)}, u32[]{:S(2)}, u32[]{:S(2)}) collective-permute-start(bf16[4,8192]{1,0:T(4,128)(2,1)} %queries.1), channel_id=1, source_target_pairs={{0,1},{1,0},{2,3},{3,2},{4,5},{5,4},{6,7},{7,6},{8,9},{9,8},{10,11... | collective-permute-start | bytes 196616 | tf_op jit(solution)/shard_map/ppermute | solution.py:420
  0.5 1.4 %collective-permute-start = (s32[1]{0:T(128)}, s32[1]{0:T(128)}, u32[]{:S(2)}, u32[]{:S(2)}) collective-permute-start(s32[1]{0:T(128)} %param.12), channel_id=1, source_target_pairs={{0,1},{1,0},{2,3},{3,2},{4,5},{5,4},{6,7},{7,6},{8,9},{9,8},{10,11... | collective-permute-start | bytes 20 | tf_op jit(solution)/shard_map/ppermute | solution.py:420
  1.8 0.8 %copy-start.2 = (bf16[4,8192]{1,0:T(4,128)(2,1)S(1)}, bf16[4,8192]{1,0:T(4,128)(2,1)}, u32[]{:S(2)}) copy-start(bf16[4,8192]{1,0:T(4,128)(2,1)} %queries.1) | copy-start | bytes 196612
  3.4 6.1 %collective-permute-start.2 = (bf16[8,4224]{1,0:T(8,128)(2,1)S(1)}, bf16[8,4224]{1,0:T(8,128)(2,1)S(1)}, u32[]{:S(2)}, u32[]{:S(2)}) collective-permute-start(bf16[8,4224]{1,0:T(8,128)(2,1)S(1)} %shard_map.73), channel_id=1, source_target_pairs={{0,8},{1,3},{2,10},{3,1},{4,12},{5,7},{6,14},{7,5},{8,0},{9,11},{1... | collective-permute-start | bytes 202760 | tf_op jit(solution)/shard_map/ppermute | solution.py:423
  7.3 14.2 %collective-permute-start.7 = (bf16[1536,512]{1,0:T(8,128)(2,1)}, bf16[1536,512]{1,0:T(8,128)(2,1)S(1)}, u32[]{:S(2)}, u32[]{:S(2)}) collective-permute-start(bf16[1536,512]{1,0:T(8,128)(2,1)} %keys_a.3), channel_id=1, source_target_pairs={{0,1},{1,0},{2,3},{3,2},{4,5},{5,4},{6,7},{7,6},{8,9},{9,8},{10,11... | collective-permute-start | bytes 4718600 | tf_op jit(solution)/shard_map/ppermute | solution.py:420
  7.3 14.2 %collective-permute-start.8 = (bf16[1536,512]{1,0:T(8,128)(2,1)}, bf16[1536,512]{1,0:T(8,128)(2,1)S(1)}, u32[]{:S(2)}, u32[]{:S(2)}) collective-permute-start(bf16[1536,512]{1,0:T(8,128)(2,1)} %values_a.3), channel_id=1, source_target_pairs={{0,1},{1,0},{2,3},{3,2},{4,5},{5,4},{6,7},{7,6},{8,9},{9,8},{10,11... | collective-permute-start | bytes 4718600 | tf_op jit(solution)/shard_map/ppermute | solution.py:420
  9.5 5.4 %collective-permute-start.3 = (bf16[16,4224]{1,0:T(8,128)(2,1)S(1)}, bf16[16,4224]{1,0:T(8,128)(2,1)S(1)}, u32[]{:S(2)}, u32[]{:S(2)}) collective-permute-start(bf16[16,4224]{1,0:T(8,128)(2,1)S(1)} %pad_maximum_fusion.1), channel_id=1, source_target_pairs={{0,4},{1,9},{2,6},{3,11},{4,0},{5,13},{6,2},{7,15},{8,12},{9,1},{1... | collective-permute-start | bytes 405512 | tf_op jit(solution)/shard_map/ppermute | solution.py:423
  14.9 6.5 %collective-permute-start.4 = (bf16[32,4224]{1,0:T(8,128)(2,1)S(1)}, bf16[32,4224]{1,0:T(8,128)(2,1)S(1)}, u32[]{:S(2)}, u32[]{:S(2)}) collective-permute-start(bf16[32,4224]{1,0:T(8,128)(2,1)S(1)} %pad_maximum_fusion.queries.low), channel_id=1, source_target_pairs={{0,2},{1,5},{2,0},{3,7},{4,6},{5,1},{6,4},{7,3},{8,10},{9,13},{10,... | collective-permute-start | bytes 811016 | tf_op jit(solution)/shard_map/ppermute | solution.py:423
  16.9 1.4 %collective-permute-start.5 = (bf16[4,512]{1,0:T(4,128)(2,1)}, bf16[4,512]{1,0:T(4,128)(2,1)S(1)}, u32[]{:S(2)}, u32[]{:S(2)}) collective-permute-start(bf16[4,512]{1,0:T(4,128)(2,1)} %new_keys_a.3), channel_id=1, source_target_pairs={{0,1},{1,0},{2,3},{3,2},{4,5},{5,4},{6,7},{7,6},{8,9},{9,8},{10,11... | collective-permute-start | bytes 12296 | tf_op jit(solution)/shard_map/ppermute | solution.py:420
  16.9 1.5 %collective-permute-start.6 = (bf16[4,512]{1,0:T(4,128)(2,1)}, bf16[4,512]{1,0:T(4,128)(2,1)S(1)}, u32[]{:S(2)}, u32[]{:S(2)}) collective-permute-start(bf16[4,512]{1,0:T(4,128)(2,1)} %new_values_a.3), channel_id=1, source_target_pairs={{0,1},{1,0},{2,3},{3,2},{4,5},{5,4},{6,7},{7,6},{8,9},{9,8},{10,11... | collective-permute-start | bytes 12296 | tf_op jit(solution)/shard_map/ppermute | solution.py:420
  21.5 1.4 %copy-start = (bf16[1536,512]{1,0:T(8,128)(2,1)S(1)}, bf16[1536,512]{1,0:T(8,128)(2,1)}, u32[]{:S(2)}) copy-start(bf16[1536,512]{1,0:T(8,128)(2,1)} %keys_a.3) | copy-start | bytes 4718596
  22.9 1.4 %copy-start.1 = (bf16[1536,512]{1,0:T(8,128)(2,1)S(1)}, bf16[1536,512]{1,0:T(8,128)(2,1)}, u32[]{:S(2)}) copy-start(bf16[1536,512]{1,0:T(8,128)(2,1)} %values_a.3) | copy-start | bytes 4718596
  24.3 0.7 %copy-start.3 = (bf16[4,512]{1,0:T(4,128)(2,1)S(1)}, bf16[4,512]{1,0:T(4,128)(2,1)}, u32[]{:S(2)}) copy-start(bf16[4,512]{1,0:T(4,128)(2,1)} %new_keys_a.3) | copy-start | bytes 12292
  25.0 0.7 %copy-start.4 = (bf16[4,512]{1,0:T(4,128)(2,1)S(1)}, bf16[4,512]{1,0:T(4,128)(2,1)}, u32[]{:S(2)}) copy-start(bf16[4,512]{1,0:T(4,128)(2,1)} %new_values_a.3) | copy-start | bytes 12292
  30.3 7.5 %collective-permute-start.9 = (s16[144,1024]{1,0:T(8,128)(2,1)S(1)}, s16[144,1024]{1,0:T(8,128)(2,1)S(1)}, u32[]{:S(2)}, u32[]{:S(2)}) collective-permute-start(s16[144,1024]{1,0:T(8,128)(2,1)S(1)} %shard_map.75), channel_id=1, source_target_pairs={{0,2},{1,5},{2,0},{3,7},{4,6},{5,1},{6,4},{7,3},{8,10},{9,13},{10,... | collective-permute-start | bytes 884744 | tf_op jit(solution)/shard_map/ppermute | solution.py:423
  38.3 7.4 %collective-permute-start.10 = (s16[144,512]{1,0:T(8,128)(2,1)S(1)}, s16[144,512]{1,0:T(8,128)(2,1)S(1)}, u32[]{:S(2)}, u32[]{:S(2)}) collective-permute-start(s16[144,512]{1,0:T(8,128)(2,1)S(1)} %get-tuple-element.12), channel_id=1, source_target_pairs={{0,4},{1,9},{2,6},{3,11},{4,0},{5,13},{6,2},{7,15},{8,12},{9,1},{1... | collective-permute-start | bytes 442376 | tf_op jit(solution)/shard_map/ppermute | solution.py:423
  46.0 5.3 %collective-permute-start.11 = (s16[144,256]{1,0:T(8,128)(2,1)S(1)}, s16[144,256]{1,0:T(8,128)(2,1)S(1)}, u32[]{:S(2)}, u32[]{:S(2)}) collective-permute-start(s16[144,256]{1,0:T(8,128)(2,1)S(1)} %get-tuple-element.14), channel_id=1, source_target_pairs={{0,8},{1,3},{2,10},{3,1},{4,12},{5,7},{6,14},{7,5},{8,0},{9,11},{1... | collective-permute-start | bytes 221192 | tf_op jit(solution)/shard_map/ppermute | solution.py:423
  51.4 1.3 %collective-permute-start.12 = (bf16[4,4096]{1,0:T(4,128)(2,1)S(1)}, bf16[4,4096]{1,0:T(4,128)(2,1)S(1)}, u32[]{:S(2)}, u32[]{:S(2)}) collective-permute-start(bf16[4,4096]{1,0:T(4,128)(2,1)S(1)} %get-tuple-element.16), channel_id=1, source_target_pairs={{0,1},{1,0},{2,3},{3,2},{4,5},{5,4},{6,7},{7,6},{8,9},{9,8},{10,11... | collective-permute-start | bytes 98312 | tf_op jit(solution)/shard_map/ppermute | solution.py:420

commit v4 on v3

v4 whole, which is shorter than its diff:
```python
import functools
import math

import jax
import jax.numpy as jnp
from jax import lax
from jax.experimental import pallas as pl
from jax.experimental.pallas import tpu as pltpu
from jax.sharding import PartitionSpec as P

KEY_VALUE_HEADS = 4
LANES = 128
CORES = 2
FLOOR = -1e30
TILES = (512,)
TAIL = 256
ATTEND_BYTES = 32 << 20
STAT_ROWS = 16
CHUNK_BLOCKS = 2
STEP = 2.0**15
MARGIN = 0.9998
F32 = jnp.float32
BF16 = jnp.bfloat16
I16 = jnp.int16
I32 = jnp.int32
VMEM = pl.BlockSpec(memory_space=pltpu.VMEM)
SMEM = pl.BlockSpec(memory_space=pltpu.SMEM)
ANY = pl.BlockSpec(memory_space=pl.ANY)
SMALL = pltpu.CompilerParams(vmem_limit_bytes=8 << 20)


def encode(out, at, values, top, total):
    dims, width = values.shape
    largest = jnp.max(jnp.abs(values), axis=0, keepdims=True)
    exponent = jnp.floor(jnp.log2(jnp.maximum(largest, 1e-30))) + 1.0
    fixed = jnp.floor(values * (jnp.exp2(15.0 - exponent) * MARGIN) + 0.5)
    size = jnp.abs(top)
    level = jnp.zeros_like(top)
    scaled = top
    for i in range(1, 9):
        above = size >= STEP**i
        level = level + jnp.where(above, 1.0, 0.0)
        scaled = scaled * jnp.where(above, 1.0 / STEP, 1.0)
    a = jnp.floor(scaled)
    rest = (scaled - a) * STEP
    b = jnp.floor(rest)
    c = jnp.floor((rest - b) * STEP)
    logs = jnp.log2(total) * 1024.0
    la = jnp.floor(logs)
    lb = jnp.floor((logs - la) * STEP)
    row = lax.broadcasted_iota(I32, (STAT_ROWS, width), 0)
    stats = jnp.zeros((STAT_ROWS, width), F32)
    for i, part in enumerate((level, a, b, c, exponent, la, lb)):
        stats = jnp.where(row == i, part, stats)
    out[:dims, at : at + width] = fixed.astype(I32).astype(I16)
    out[dims:, at : at + width] = stats.astype(I32).astype(I16)


def decode_stats(ref, dims, at):
    stats = ref[dims:, at].astype(I32).astype(F32)

    def part(i):
        return stats[i : i + 1, :]

    top = part(1) + (part(2) + part(3) * (1.0 / STEP)) * (1.0 / STEP)
    for i in range(1, 9):
        top = top * jnp.where(part(0) >= i, STEP, 1.0)
    total = jnp.exp2((part(5) + part(6) * (1.0 / STEP)) * (1.0 / 1024.0))
    return top, total, jnp.exp2(part(4) - 15.0) * (1.0 / MARGIN)


def join_kernel(length, length_other, mine, queries_other, out):
    rows, half = mine.shape
    core = lax.axis_index("ctx") % CORES
    other = queries_other[:, pl.ds(pl.multiple_of(core * half, LANES), half)]
    out[:, :half] = jnp.concatenate([mine[...].astype(F32), other.astype(F32)], axis=0).astype(BF16)
    lane = lax.broadcasted_iota(I32, (CORES * rows, LANES), 1)
    row = lax.broadcasted_iota(I32, (CORES * rows, LANES), 0)
    count = jnp.where(row < rows, length[0], length_other[0])
    coded = jnp.where(lane == 0, count // LANES, jnp.where(lane == 1, count % LANES, 0))
    out[:, half:] = coded.astype(F32).astype(BF16)


def join(length, length_other, mine, queries_other):
    rows, half = mine.shape
    return pl.pallas_call(
        join_kernel,
        out_shape=jax.ShapeDtypeStruct((CORES * rows, half + LANES), BF16),
        in_specs=[SMEM, SMEM, VMEM, VMEM],
        out_specs=VMEM,
        compiler_params=SMALL,
    )(length, length_other, mine, queries_other)


def attend_kernel(sizes, *refs):
    own_rows, orders, group, kv_heads, sets = sizes
    start = refs[0]
    queries, extras = refs[1 : 1 + sets], refs[1 + sets : 1 + 2 * sets]
    rest = refs[1 + 2 * sets :]
    new_keys, new_values, keys_a, keys_b, values_a, values_b = rest[:6]
    outs = rest[6 : 6 + sets]
    query_t, scores, sums, tops, totals, kv, arrived = rest[6 + sets :]
    chip_rows = CORES * own_rows
    slots = keys_a.shape[0]
    tokens = queries[0].shape[0]
    blocks = tokens // chip_rows
    set_blocks = extras[0].shape[0] // chip_rows
    set_lanes = tokens * group
    lanes = sets * set_lanes
    me = lax.axis_index("ctx")
    core, chip = me % CORES, me // CORES
    factor = math.log2(math.e) / math.sqrt(LANES)
    chunk = pl.program_id(0)

    def copy(h, i):
        own = i % 2 == 0
        at = pl.multiple_of((0 if own else core * kv_heads * LANES) + h * LANES, LANES)
        source = (keys_a, keys_b, values_a, values_b)[i]
        return pltpu.make_async_copy(source.at[:, pl.ds(at, LANES)], kv.at[h, i], arrived.at[h, i])

    @pl.when(chunk == 0)
    def _():
        for h in range(kv_heads):
            for i in range(4):
                copy(h, i).start()

    steps = [jnp.where(core == 0, a // CORES, b // CORES) for a, b in zip(*orders)]

    def origin(block):
        off = jnp.zeros_like(block)
        for i, step in enumerate(steps):
            off = off ^ jnp.where((block >> i) & 1 == 1, step, 0)
        return chip ^ off

    found = [0.0, 0.0, 0.0]
    for i, ref in enumerate(extras):
        rows = ref.shape[0]
        lane = lax.broadcasted_iota(I32, (rows, LANES), 1)
        row = lax.broadcasted_iota(I32, (rows, LANES), 0)
        place = origin(row // chip_rows + i * set_blocks)
        inside = row % chip_rows
        counts = jnp.where(lane == 0, float(LANES), 1.0) * ref[...].astype(F32)
        counts = jnp.where((inside % own_rows == 0) & (lane < 2), counts, 0.0)
        here = place == chip
        second = inside >= own_rows
        for k, chosen in enumerate((place < chip, here & ~second, here & second)):
            found[k] = found[k] + jnp.sum(jnp.where(chosen, counts, 0.0), axis=0, keepdims=True)
    row = lax.broadcasted_iota(I32, (8, LANES), 0)
    found = jnp.where(row == 0, found[0], jnp.where(row == 1, found[1], found[2]))
    found = jnp.sum(found, axis=1, keepdims=True).astype(I32)
    before, length = found[0, 0], [found[1, 0], found[2, 0]]
    begins = [
        before + jnp.where(core == 1, length[1], 0),
        before + jnp.where(core == 0, length[0], 0),
    ]
    limits = [jnp.clip(jnp.minimum(n, start[0] - at), 0, slots) for n, at in zip(length, begins)]

    key_row = lax.broadcasted_iota(I32, (chip_rows, lanes), 0)
    lane = lax.broadcasted_iota(I32, (chip_rows, lanes), 1)
    part = key_row // own_rows
    key_id = (chip * CORES + (core ^ part)) * own_rows + key_row % own_rows
    inside = lane % chip_rows
    block = lane // set_lanes * set_blocks + lane % set_lanes // (group * chip_rows) + chunk * blocks
    token = (origin(block) * CORES + (core ^ (inside // own_rows))) * own_rows + inside % own_rows
    causal = key_id <= token
    nothing = jnp.zeros((16 - chip_rows % 16, LANES), F32)
    heads = range(kv_heads)
    fresh_scores, fresh_values = [], []

    for h in heads:
        first = h * group
        q = jnp.concatenate(
            [
                ref[b * chip_rows : (b + 1) * chip_rows, (first + g) * LANES : (first + g + 1) * LANES].astype(F32)
                for ref in queries
                for b in range(blocks)
                for g in range(group)
            ],
            axis=0,
        )
        query_t[h] = q.T.astype(BF16)
        at = pl.multiple_of((core * kv_heads + h) * LANES, LANES)

        def padded_rows(ref):
            return jnp.concatenate([ref[:, pl.ds(at, LANES)].astype(F32), nothing], 0).astype(BF16)

        fresh_values.append(padded_rows(new_values))
        fresh_scores.append(jnp.dot(padded_rows(new_keys), query_t[h], preferred_element_type=F32)[:chip_rows] * factor)

    @pl.when(chunk == 0)
    def _():
        for h in heads:
            for i in range(4):
                copy(h, i).wait()

    def fold(tile, combine):
        return combine(tile.reshape(tile.shape[0] // 8, 8, lanes), axis=0)

    def each_tile(limit, body, carry):
        base, rest = 0, limit
        for rows in TILES:
            count = rest // rows

            def whole(j, carry, rows=rows, base=base):
                return body(pl.multiple_of(base + j * rows, TILES[-1]), rows, None, carry)

            carry = lax.fori_loop(0, count, whole, carry)
            base, rest = base + count * rows, rest - count * rows
        base = pl.multiple_of(base, TILES[-1])
        for rows, need in ((TAIL, (rest > 0) & (rest <= TAIL)), (TILES[-1], rest > TAIL)):
            carry = lax.cond(need, lambda c, rows=rows: body(base, rows, rest, c), lambda c: c, carry)
        return carry

    tn = (((0,), (0,)), ((), ()))

    def shard(s, carry):
        limit = jnp.where(s == 0, limits[0], limits[1])
        seen = causal & (part == s)

        def first_pass(base, rows, filled, peaks):
            higher = []
            for h in heads:
                tile = jnp.dot(kv[h, s, pl.ds(base, rows), :], query_t[h], preferred_element_type=F32) * factor
                if filled is not None:
                    tile = jnp.where(lax.broadcasted_iota(I32, (rows, lanes), 0) < filled, tile, FLOOR)
                scores[h, pl.ds(base, rows), :] = tile
                higher.append(jnp.maximum(peaks[h], fold(tile, jnp.max)))
            return tuple(higher)

        peaks = each_tile(limit, first_pass, tuple(jnp.where(seen, x, FLOOR) for x in fresh_scores))
        top = [jnp.max(x, axis=0, keepdims=True) for x in peaks]
        masses = []
        for h in heads:
            weight = jnp.where(seen, jnp.exp2(fresh_scores[h] - top[h]), 0.0)
            padded = jnp.concatenate([weight, jnp.zeros((16 - chip_rows % 16, lanes), F32)], 0).astype(BF16)
            sums[s, h] = lax.dot_general(fresh_values[h], padded, tn, preferred_element_type=F32)
            masses.append(weight)

        def second_pass(base, rows, filled, masses):
            more = []
            for h in heads:
                weight = jnp.exp2(scores[h, pl.ds(base, rows), :] - top[h])
                if filled is not None:
                    weight = jnp.where(lax.broadcasted_iota(I32, (rows, lanes), 0) < filled, weight, 0.0)
                sums[s, h] += lax.dot_general(
                    kv[h, 2 + s, pl.ds(base, rows), :], weight.astype(BF16), tn, preferred_element_type=F32
                )
                more.append(masses[h] + fold(weight, jnp.sum))
            return tuple(more)

        masses = each_tile(limit, second_pass, tuple(masses))
        for h in heads:
            tops[s, h] = top[h]
            totals[s, h] = jnp.sum(masses[h], axis=0, keepdims=True)
        return carry

    lax.fori_loop(0, 2, shard, 0)
    for h in heads:
        top_a, top_b = tops[0, h], tops[1, h]
        top = jnp.maximum(top_a, top_b)
        scale_a = jnp.exp2(top_a - top)
        scale_b = jnp.exp2(top_b - top)
        total = jnp.maximum(totals[0, h] * scale_a + totals[1, h] * scale_b, 1.0)
        merged = sums[0, h] * (scale_a / total) + sums[1, h] * (scale_b / total)
        width = group * chip_rows
        for i, out in enumerate(outs):
            for b in range(blocks):
                at = i * set_lanes + b * width
                cut = slice(at, at + width)
                encode(out, (b * kv_heads + h) * width, merged[:, cut], top[:, cut], total[:, cut])


def attend(start, held, fresh, cache, *, own_rows, orders):
    sets = len(held)
    count = held[0].shape[0]
    chip_rows = CORES * own_rows
    tokens = min(count, CHUNK_BLOCKS * chip_rows)
    slots = cache[0].shape[0]
    kv_heads = cache[0].shape[1] // LANES
    heads = held[0].shape[1] // LANES - 1
    group = heads // kv_heads
    lanes = sets * tokens * group
    padded = -(-slots // TILES[-1]) * TILES[-1]
    sizes = (own_rows, orders, group, kv_heads, sets)
    shape = jax.ShapeDtypeStruct((LANES + STAT_ROWS, count * heads), I16)
    return pl.pallas_call(
        functools.partial(attend_kernel, sizes),
        out_shape=(shape,) * sets,
        grid=(count // tokens,),
        in_specs=[SMEM]
        + [pl.BlockSpec((tokens, heads * LANES), lambda i: (i, 0))] * sets
        + [pl.BlockSpec((count, LANES), lambda i: (0, heads))] * sets
        + [VMEM] * 2
        + [ANY] * 4,
        out_specs=(pl.BlockSpec((LANES + STAT_ROWS, tokens * heads), lambda i: (0, i)),) * sets,
        scratch_shapes=[
            pltpu.VMEM((kv_heads, LANES, lanes), BF16),
            pltpu.VMEM((kv_heads, padded, lanes), F32),
            pltpu.VMEM((2, kv_heads, LANES, lanes), F32),
            pltpu.VMEM((2, kv_heads, 1, lanes), F32),
            pltpu.VMEM((2, kv_heads, 1, lanes), F32),
            pltpu.VMEM((kv_heads, 4, padded, LANES), BF16),
            pltpu.SemaphoreType.DMA((kv_heads, 4)),
        ],
        compiler_params=pltpu.CompilerParams(vmem_limit_bytes=ATTEND_BYTES),
    )(start, *held, *held, *fresh, *cache)


def merged_part(refs, dims, at):
    stats = [decode_stats(ref, dims, at) for ref in refs]
    top = functools.reduce(jnp.maximum, [x[0] for x in stats])
    masses = [x[1] * jnp.exp2(x[0] - top) for x in stats]
    total = functools.reduce(jnp.add, masses)
    values = 0.0
    for ref, mass, (_, _, unit) in zip(refs, masses, stats):
        values = values + ref[:dims, at].astype(I32).astype(F32) * (mass / total * unit)
    return values, top, total


def merge_kernel(inputs, *refs):
    parts, outs = refs[:inputs], refs[inputs:]
    dims = parts[0].shape[0] - STAT_ROWS
    width = outs[0].shape[1]
    step = min(width, 2 * LANES)
    for i, out in reversed(list(enumerate(outs))):
        for at in range(0, width, step):
            encode(out, at, *merged_part(parts, dims, slice(i * width + at, i * width + at + step)))


def merge(parts, pieces):
    rows, width = parts[0].shape
    shape = jax.ShapeDtypeStruct((rows, width // pieces), I16)
    return pl.pallas_call(
        functools.partial(merge_kernel, len(parts)),
        out_shape=(shape,) * pieces,
        in_specs=[VMEM] * len(parts),
        out_specs=(VMEM,) * pieces,
        compiler_params=SMALL,
    )(*parts)


def finish_kernel(group, inputs, *refs):
    parts, (mine, other) = refs[:inputs], refs[inputs:]
    dims = parts[0].shape[0] - STAT_ROWS
    own_rows = mine.shape[0]
    chip_rows = CORES * own_rows
    width = group * chip_rows
    for h in range(parts[0].shape[1] // width):
        values, _, _ = merged_part(parts, dims, slice(h * width, (h + 1) * width))
        rows = values.T
        for g in range(group):
            at = (h * group + g) * dims
            tokens = rows[g * chip_rows : (g + 1) * chip_rows]
            mine[:, at : at + dims] = tokens[:own_rows].astype(BF16)
            other[:, at : at + dims] = tokens[own_rows:].astype(BF16)


def finish(parts, own_rows, group):
    rows, width = parts[0].shape
    shape = jax.ShapeDtypeStruct((own_rows, width // (CORES * own_rows) * (rows - STAT_ROWS)), BF16)
    return pl.pallas_call(
        functools.partial(finish_kernel, group, len(parts)),
        out_shape=(shape, shape),
        in_specs=[VMEM] * len(parts),
        out_specs=(VMEM, VMEM),
        compiler_params=SMALL,
    )(*parts)


def place_kernel(mine, theirs, out):
    half = mine.shape[1]
    core = lax.axis_index("ctx") % CORES
    out[:, pl.ds(pl.multiple_of(core * half, LANES), half)] = mine[...]
    out[:, pl.ds(pl.multiple_of((1 - core) * half, LANES), half)] = theirs[...]


def place(mine, theirs):
    rows, half = mine.shape
    return pl.pallas_call(
        place_kernel,
        out_shape=jax.ShapeDtypeStruct((rows, CORES * half), BF16),
        in_specs=[VMEM, VMEM],
        out_specs=VMEM,
        compiler_params=SMALL,
    )(mine, theirs)


def per_device(
    queries, cache_keys, cached_value_rows, new_keys, prompt_value_rows, cache_len, prompt_start
):
    width = lax.axis_size("ctx")
    own_rows = queries.shape[0]
    group = queries.shape[1] // cache_keys.shape[1]
    bits = [CORES << i for i in range((width // CORES).bit_length() - 1)]
    orders = (tuple(bits[-1:] + bits[:-1]), tuple(bits[-2:-1] + bits[:-2] + bits[-1:]))
    odd = len(bits) % 2
    stages = [(0,)] * odd + [(i, i + 1) for i in range(odd, len(bits), 2)]

    def swap(x):
        return lax.ppermute(x, "ctx", [(i, i ^ 1) for i in range(width)])

    def partners(stage):
        return [
            [sum(order[bit] for k, bit in enumerate(stage) if c >> k & 1) for order in orders]
            for c in range(1, 1 << len(stage))
        ]

    def exchange(x, distance):
        return lax.ppermute(x, "ctx", [(i, i ^ distance[i % CORES]) for i in range(width)])

    def own_half(x):
        half = x.shape[1] // CORES
        return lax.dynamic_slice_in_dim(x, core * half, half, 1)

    core = lax.axis_index("ctx") % CORES
    held = join(cache_len, swap(cache_len), own_half(queries), swap(queries))
    fresh = [jnp.concatenate([x, swap(x)], axis=0) for x in (new_keys, prompt_value_rows)]
    cache = [y for x in (cache_keys, cached_value_rows) for y in (own_half(x), swap(x))]
    for stage in stages:
        gathered = [held] + [exchange(held, distance) for distance in partners(stage)]
        if stage != stages[-1]:
            held = jnp.concatenate(gathered, axis=0)
    parts = attend(prompt_start, gathered, fresh, cache, own_rows=own_rows, orders=orders)
    for stage in reversed(stages):
        sent = [exchange(x, distance) for x, distance in zip(parts[1:], partners(stage))]
        parts = [parts[0]] + sent
        if stage != stages[0]:
            parts = merge(parts, 1 << len(stages[stages.index(stage) - 1]))
    mine, other = finish(parts, own_rows, group)
    return place(mine, swap(other))


def solution(mesh):
    return jax.shard_map(
        per_device,
        mesh=mesh,
        in_specs=(
            P(("groups", "ctx"), None),
            P(("groups", "ctx"), None),
            P(("groups", "ctx"), None),
            P(("groups", "ctx"), None),
            P(("groups", "ctx"), None),
            P(("groups", "ctx")),
            P("groups"),
        ),
        out_specs=P(("groups", "ctx"), None),
        check_vma=False,
    )
```

time: 53.6 us -> 52.2 us (0.974); the launches traced: 53.3 us -> 52.6 us
  waiting for transfers between devices: 16.9 us -> 22.7 us
  starting transfers between devices: 18.6 us -> 14.6 us
  local copies, waits for them, and re-layouts: 5.03 us -> 2.25 us
    unnamed x10 -> x4, local copies, waits for them, and re-layouts: 5.03 us -> 0.01 us
    ppermute x6 -> x8, starting transfers between devices: 17 us -> 12.8 us  [exchange(): lax.ppermute(x, 'ctx', [(i, i ^ distance[i % CORES]) for i in range(width)])]
    ppermute x6 -> x8, waiting for transfers between devices: 14.6 us -> 18.7 us  [exchange(): lax.ppermute(x, 'ctx', [(i, i ^ distance[i % CORES]) for i in range(width)])]
    dynamic_slice x0 -> x2, local copies, waits for them, and re-layouts: none -> 2.24 us  [own_half(): return lax.dynamic_slice_in_dim(x, core * half, half, 1)]
    ppermute x7, waiting for transfers between devices: 2.26 us -> 4.02 us  [swap(): return lax.ppermute(x, 'ctx', [(i, i ^ 1) for i in range(width)])]
    pallas_call x5 -> x3, Pallas kernels: 10.1 us -> 10.3 us  [the longest x1 9.83 us: attend(): pl.pallas_call(functools.partial(attend_kernel, sizes), out_shape=(shape,...]
  transfers between devices with their start and end apart: 13 -> 15, of which waited for: 9 -> 10; matrix products, arithmetic and copies ran while one was open for 0% -> 4% of each run, Pallas kernels for 9% -> 1%
where the time goes in v4:
time: 52.2 us; the launch traced here: 52.6 us
  waiting for transfers between devices  22.7 us (43%)
  starting transfers between devices  14.6 us (28%)
  Pallas kernels  11.6 us (22%)
  local copies, waits for them, and re-layouts  2.25 us (4%)
  between operations  1.41 us (3%)
    ppermute x8, waiting for transfers between devices, exchange(): lax.ppermute(x, 'ctx', [(i, i ^ distance[i % CORES]) for i in range(width)])  18.7 us
    ppermute x8, starting transfers between devices, exchange(): lax.ppermute(x, 'ctx', [(i, i ^ distance[i % CORES]) for i in range(width)])  12.8 us
    pallas_call x1, Pallas kernels, attend(): pl.pallas_call(functools.partial(attend_kernel, sizes), out_shape=(shape,...  9.83 us
    ppermute x7, waiting for transfers between devices, swap(): return lax.ppermute(x, 'ctx', [(i, i ^ 1) for i in range(width)])  4.02 us
    dynamic_slice x2, local copies, waits for them, and re-layouts, own_half(): return lax.dynamic_slice_in_dim(x, core * half, half, 1)  2.24 us
    ppermute x7, starting transfers between devices, swap(): return lax.ppermute(x, 'ctx', [(i, i ^ 1) for i in range(width)])  1.88 us
  transfers between devices with their start and end apart: 15, of which 10 were waited for; matrix products, arithmetic and copies ran while one was open for 4% of the time, Pallas kernels for 1%

profile of v4, /device:TPU:0, one launch (start us, length us, event | category | flops | bytes accessed | tf_op | source)
XLA Modules:
  0.0 52.6 jit_solution(8396182409511453203)
XLA Ops:
  0.0 0.5 collective-permute-start.8
  0.5 0.1 collective-permute-start.9
  0.5 0.5 collective-permute-start
  1.0 0.1 collective-permute-start.6
  1.0 0.5 collective-permute-start.1
  1.5 0.8 %constant_dynamic-slice_fusion.2.mine = bf16[4,4096]{1,0:T(4,128)(2,1)S(1)} fusion(bf16[4,8192]{1,0:T(4,128)(2,1)} %param.7, s32[]{:T(128)S(6)} %select_n.15), kind=kLoop, calls=%fused_computation.5 | loop fusion | bytes 65540 | tf_op jit(solution)/shard_map/dynamic_slice | solution.py:413
  2.9 0.9 %collective-permute-done.length_other = s32[1]{0:T(128)} collective-permute-done((s32[1]{0:T(128)}, s32[1]{0:T(128)}, u32[]{:S(2)}, u32[]{:S(2)}) %collective-permute-start) | collective-permute-done | bytes 36 | tf_op jit(solution)/shard_map/ppermute | solution.py:400
  3.8 0.3 collective-permute-start.7
  4.1 2.0 %collective-permute-done.1.queries_other = bf16[4,8192]{1,0:T(4,128)(2,1)S(1)} collective-permute-done((bf16[4,8192]{1,0:T(4,128)(2,1)}, bf16[4,8192]{1,0:T(4,128)(2,1)S(1)}, u32[]{:S(2)}, u32[]{:S(2)}) %collective-permute-start.1) | collective-permute-done | bytes 65568 | tf_op jit(solution)/shard_map/ppermute | solution.py:400
  6.1 0.6 %shard_map.73 = bf16[8,4224]{1,0:T(8,128)(2,1)S(1)} custom-call(s32[1]{0:T(128)S(6)} %copy.8.length, s32[1]{0:T(128)} %collective-permute-done.length_other, bf16[4,4096]{1,0:T(4,128)(2,1)S(1)} %constant_dynamic-slice_fusion.2.mine, bf16[4,8192]{1,0:T(4,128)(2,1)S(1)} %collective-permute-done.1.queries_other), custom_call_target="tpu_custom_call" | custom-call | tf_op jit(solution)/shard_map/pallas_call | solution.py:86
  6.6 0.0 copy-start
  6.7 0.0 copy-start.1
  6.7 4.0 %collective-permute-start.2 = (bf16[8,4224]{1,0:T(8,128)(2,1)S(1)}, bf16[8,4224]{1,0:T(8,128)(2,1)S(1)}, u32[]{:S(2)}, u32[]{:S(2)}) collective-permute-start(bf16[8,4224]{1,0:T(8,128)(2,1)S(1)} %shard_map.73), channel_id=1, source_target_pairs={{0,8},{1,5},{2,10},{3,7},{4,12},{5,1},{6,14},{7,3},{8,0},{9,13},{1... | collective-permute-start | bytes 202760 | tf_op jit(solution)/shard_map/ppermute | solution.py:409
  10.7 1.5 %constant_dynamic-slice_fusion = (bf16[1536,256]{1,0:T(8,128)(2,1)S(1)}, bf16[1536,256]{1,0:T(8,128)(2,1)S(1)}) fusion(bf16[1536,512]{1,0:T(8,128)(2,1)} %param.9, s32[]{:T(128)S(6)} %select_n.16, bf16[1536,512]{1,0:T(8,128)(2,1)} %param.8), kind=kLoop, calls=%fused_computation.3 | loop fusion | bytes 3145732 | tf_op jit(solution)/shard_map/dynamic_slice | solution.py:413
  12.8 0.1 collective-permute-done.2
  13.0 2.9 %collective-permute-start.5 = (bf16[16,4224]{1,0:T(8,128)(2,1)S(1)}, bf16[16,4224]{1,0:T(8,128)(2,1)S(1)}, u32[]{:S(2)}, u32[]{:S(2)}) collective-permute-start(bf16[16,4224]{1,0:T(8,128)(2,1)S(1)} %pad_maximum_fusion.refs_1_.refs_5_), channel_id=1, source_target_pairs={{0,6},{1,11},{2,4},{3,9},{4,2},{5,15},{6,0},{7,13},{8,14},{9,3},{1... | collective-permute-start | bytes 405512 | tf_op jit(solution)/shard_map/ppermute | solution.py:409
  15.9 0.0 collective-permute-done.6
  15.9 0.4 collective-permute-start.4
  16.4 0.0 collective-permute-done.7
  16.4 0.2 collective-permute-start.3
  16.6 0.0 copy-done
  16.6 0.0 copy-done.1
  16.6 3.2 %collective-permute-done.5.refs_4_.refs_8_ = bf16[16,4224]{1,0:T(8,128)(2,1)S(1)} collective-permute-done((bf16[16,4224]{1,0:T(8,128)(2,1)S(1)}, bf16[16,4224]{1,0:T(8,128)(2,1)S(1)}, u32[]{:S(2)}, u32[]{:S(2)}) %collective-permute-start.5) | collective-permute-done | bytes 135200 | tf_op jit(solution)/shard_map/ppermute | solution.py:409
  19.8 3.1 %collective-permute-done.4.refs_3_.refs_7_ = bf16[16,4224]{1,0:T(8,128)(2,1)S(1)} collective-permute-done((bf16[16,4224]{1,0:T(8,128)(2,1)S(1)}, bf16[16,4224]{1,0:T(8,128)(2,1)S(1)}, u32[]{:S(2)}, u32[]{:S(2)}) %collective-permute-start.4) | collective-permute-done | bytes 135200 | tf_op jit(solution)/shard_map/ppermute | solution.py:409
  22.9 0.0 collective-permute-done.3.refs_2_.refs_6_
  22.9 0.0 collective-permute-done.8.refs_12_
  22.9 0.0 collective-permute-done.9.refs_14_
  22.9 9.8 %shard_map.74 = (s16[144,512]{1,0:T(8,128)(2,1)S(1)}, s16[144,512]{1,0:T(8,128)(2,1)S(1)}, s16[144,512]{1,0:T(8,128)(2,1)S(1)}, s16[144,512]{1,0:T(8,128)(2,1)S(1)}) custom-call(s32[1]{0:T(128)S(6)} %copy.9.refs_0_, bf16[16,4224]{1,0:T(8,128)(2,1)S(1)} %pad_maximum_fusion.refs_1_.refs_5_, bf16[16,4224]{1,0:T(8,128)(2,1)S(1)} %collective-permute-done.3.refs_2_.refs_6_, ...), custom_call_target="tpu_custom_call" | custom-call | tf_op jit(solution)/shard_map/pallas_call | solution.py:286
  32.8 0.1 collective-permute-start.10
  32.8 0.9 %collective-permute-start.11 = (s16[144,512]{1,0:T(8,128)(2,1)S(1)}, s16[144,512]{1,0:T(8,128)(2,1)S(1)}, u32[]{:S(2)}, u32[]{:S(2)}) collective-permute-start(s16[144,512]{1,0:T(8,128)(2,1)S(1)} %get-tuple-element.15), channel_id=1, source_target_pairs={{0,4},{1,9},{2,6},{3,11},{4,0},{5,13},{6,2},{7,15},{8,12},{9,1},{1... | collective-permute-start | bytes 442376 | tf_op jit(solution)/shard_map/ppermute | solution.py:409
  33.7 2.6 %collective-permute-start.12 = (s16[144,512]{1,0:T(8,128)(2,1)S(1)}, s16[144,512]{1,0:T(8,128)(2,1)S(1)}, u32[]{:S(2)}, u32[]{:S(2)}) collective-permute-start(s16[144,512]{1,0:T(8,128)(2,1)S(1)} %get-tuple-element.16), channel_id=1, source_target_pairs={{0,6},{1,11},{2,4},{3,9},{4,2},{5,15},{6,0},{7,13},{8,14},{9,3},{1... | collective-permute-start | bytes 442376 | tf_op jit(solution)/shard_map/ppermute | solution.py:409
  36.3 1.7 %collective-permute-done.10.refs_1_ = s16[144,512]{1,0:T(8,128)(2,1)S(1)} collective-permute-done((s16[144,512]{1,0:T(8,128)(2,1)S(1)}, s16[144,512]{1,0:T(8,128)(2,1)S(1)}, u32[]{:S(2)}, u32[]{:S(2)}) %collective-permute-start.10) | collective-permute-done | bytes 147488 | tf_op jit(solution)/shard_map/ppermute | solution.py:409
  38.0 1.8 %collective-permute-done.11.refs_2_ = s16[144,512]{1,0:T(8,128)(2,1)S(1)} collective-permute-done((s16[144,512]{1,0:T(8,128)(2,1)S(1)}, s16[144,512]{1,0:T(8,128)(2,1)S(1)}, u32[]{:S(2)}, u32[]{:S(2)}) %collective-permute-start.11) | collective-permute-done | bytes 147488 | tf_op jit(solution)/shard_map/ppermute | solution.py:409
  39.8 4.3 %collective-permute-done.12.refs_3_ = s16[144,512]{1,0:T(8,128)(2,1)S(1)} collective-permute-done((s16[144,512]{1,0:T(8,128)(2,1)S(1)}, s16[144,512]{1,0:T(8,128)(2,1)S(1)}, u32[]{:S(2)}, u32[]{:S(2)}) %collective-permute-start.12) | collective-permute-done | bytes 147488 | tf_op jit(solution)/shard_map/ppermute | solution.py:409
  44.0 0.4 shard_map.75
  44.4 1.6 %collective-permute-start.13 = (s16[144,256]{1,0:T(8,128)(2,1)S(1)}, s16[144,256]{1,0:T(8,128)(2,1)S(1)}, u32[]{:S(2)}, u32[]{:S(2)}) collective-permute-start(s16[144,256]{1,0:T(8,128)(2,1)S(1)} %get-tuple-element.18), channel_id=1, source_target_pairs={{0,8},{1,5},{2,10},{3,7},{4,12},{5,1},{6,14},{7,3},{8,0},{9,13},{1... | collective-permute-start | bytes 221192 | tf_op jit(solution)/shard_map/ppermute | solution.py:409
  46.0 4.5 %collective-permute-done.13.refs_1_ = s16[144,256]{1,0:T(8,128)(2,1)S(1)} collective-permute-done((s16[144,256]{1,0:T(8,128)(2,1)S(1)}, s16[144,256]{1,0:T(8,128)(2,1)S(1)}, u32[]{:S(2)}, u32[]{:S(2)}) %collective-permute-start.13) | collective-permute-done | bytes 73760 | tf_op jit(solution)/shard_map/ppermute | solution.py:409
  50.5 0.2 shard_map.76
  50.7 0.1 collective-permute-start.14
  50.7 1.2 %collective-permute-done.14.theirs = bf16[4,4096]{1,0:T(4,128)(2,1)S(1)} collective-permute-done((bf16[4,4096]{1,0:T(4,128)(2,1)S(1)}, bf16[4,4096]{1,0:T(4,128)(2,1)S(1)}, u32[]{:S(2)}, u32[]{:S(2)}) %collective-permute-start.14) | collective-permute-done | bytes 32800 | tf_op jit(solution)/shard_map/ppermute | solution.py:400
  51.9 0.6 %shard_map.77 = bf16[4,8192]{1,0:T(4,128)(2,1)} custom-call(bf16[4,4096]{1,0:T(4,128)(2,1)S(1)} %get-tuple-element.19.mine, bf16[4,4096]{1,0:T(4,128)(2,1)S(1)} %collective-permute-done.14.theirs), custom_call_target="tpu_custom_call" | custom-call | tf_op jit(solution)/shard_map/pallas_call | solution.py:379
  (3 shorter events, 0.0 us)
Async XLA Ops:
  0.0 22.9 %collective-permute-start.8 = (bf16[1536,512]{1,0:T(8,128)(2,1)}, bf16[1536,512]{1,0:T(8,128)(2,1)S(1)}, u32[]{:S(2)}, u32[]{:S(2)}) collective-permute-start(bf16[1536,512]{1,0:T(8,128)(2,1)} %param.8), channel_id=1, source_target_pairs={{0,1},{1,0},{2,3},{3,2},{4,5},{5,4},{6,7},{7,6},{8,9},{9,8},{10,11... | collective-permute-start | bytes 4718600 | tf_op jit(solution)/shard_map/ppermute | solution.py:400
  0.5 22.5 %collective-permute-start.9 = (bf16[1536,512]{1,0:T(8,128)(2,1)}, bf16[1536,512]{1,0:T(8,128)(2,1)S(1)}, u32[]{:S(2)}, u32[]{:S(2)}) collective-permute-start(bf16[1536,512]{1,0:T(8,128)(2,1)} %param.9), channel_id=1, source_target_pairs={{0,1},{1,0},{2,3},{3,2},{4,5},{5,4},{6,7},{7,6},{8,9},{9,8},{10,11... | collective-permute-start | bytes 4718600 | tf_op jit(solution)/shard_map/ppermute | solution.py:400
  0.5 3.2 %collective-permute-start = (s32[1]{0:T(128)}, s32[1]{0:T(128)}, u32[]{:S(2)}, u32[]{:S(2)}) collective-permute-start(s32[1]{0:T(128)} %param.12), channel_id=1, source_target_pairs={{0,1},{1,0},{2,3},{3,2},{4,5},{5,4},{6,7},{7,6},{8,9},{9,8},{10,11... | collective-permute-start | bytes 20 | tf_op jit(solution)/shard_map/ppermute | solution.py:400
  1.0 14.9 %collective-permute-start.6 = (bf16[4,512]{1,0:T(4,128)(2,1)}, bf16[4,512]{1,0:T(4,128)(2,1)S(1)}, u32[]{:S(2)}, u32[]{:S(2)}) collective-permute-start(bf16[4,512]{1,0:T(4,128)(2,1)} %param.10), channel_id=1, source_target_pairs={{0,1},{1,0},{2,3},{3,2},{4,5},{5,4},{6,7},{7,6},{8,9},{9,8},{10,11... | collective-permute-start | bytes 12296 | tf_op jit(solution)/shard_map/ppermute | solution.py:400
  1.0 5.0 %collective-permute-start.1 = (bf16[4,8192]{1,0:T(4,128)(2,1)}, bf16[4,8192]{1,0:T(4,128)(2,1)S(1)}, u32[]{:S(2)}, u32[]{:S(2)}) collective-permute-start(bf16[4,8192]{1,0:T(4,128)(2,1)} %param.7), channel_id=1, source_target_pairs={{0,1},{1,0},{2,3},{3,2},{4,5},{5,4},{6,7},{7,6},{8,9},{9,8},{10,11... | collective-permute-start | bytes 196616 | tf_op jit(solution)/shard_map/ppermute | solution.py:400
  3.8 12.6 %collective-permute-start.7 = (bf16[4,512]{1,0:T(4,128)(2,1)}, bf16[4,512]{1,0:T(4,128)(2,1)S(1)}, u32[]{:S(2)}, u32[]{:S(2)}) collective-permute-start(bf16[4,512]{1,0:T(4,128)(2,1)} %param.11), channel_id=1, source_target_pairs={{0,1},{1,0},{2,3},{3,2},{4,5},{5,4},{6,7},{7,6},{8,9},{9,8},{10,11... | collective-permute-start | bytes 12296 | tf_op jit(solution)/shard_map/ppermute | solution.py:400
  6.6 9.9 %copy-start = (bf16[4,512]{1,0:T(4,128)(2,1)S(1)}, bf16[4,512]{1,0:T(4,128)(2,1)}, u32[]{:S(2)}) copy-start(bf16[4,512]{1,0:T(4,128)(2,1)} %param.10) | copy-start | bytes 12292
  6.7 9.9 %copy-start.1 = (bf16[4,512]{1,0:T(4,128)(2,1)S(1)}, bf16[4,512]{1,0:T(4,128)(2,1)}, u32[]{:S(2)}) copy-start(bf16[4,512]{1,0:T(4,128)(2,1)} %param.11) | copy-start | bytes 12292
  6.7 6.3 %collective-permute-start.2 = (bf16[8,4224]{1,0:T(8,128)(2,1)S(1)}, bf16[8,4224]{1,0:T(8,128)(2,1)S(1)}, u32[]{:S(2)}, u32[]{:S(2)}) collective-permute-start(bf16[8,4224]{1,0:T(8,128)(2,1)S(1)} %shard_map.73), channel_id=1, source_target_pairs={{0,8},{1,5},{2,10},{3,7},{4,12},{5,1},{6,14},{7,3},{8,0},{9,13},{1... | collective-permute-start | bytes 202760 | tf_op jit(solution)/shard_map/ppermute | solution.py:409
  13.0 6.9 %collective-permute-start.5 = (bf16[16,4224]{1,0:T(8,128)(2,1)S(1)}, bf16[16,4224]{1,0:T(8,128)(2,1)S(1)}, u32[]{:S(2)}, u32[]{:S(2)}) collective-permute-start(bf16[16,4224]{1,0:T(8,128)(2,1)S(1)} %pad_maximum_fusion.refs_1_.refs_5_), channel_id=1, source_target_pairs={{0,6},{1,11},{2,4},{3,9},{4,2},{5,15},{6,0},{7,13},{8,14},{9,3},{1... | collective-permute-start | bytes 405512 | tf_op jit(solution)/shard_map/ppermute | solution.py:409
  15.9 7.0 %collective-permute-start.4 = (bf16[16,4224]{1,0:T(8,128)(2,1)S(1)}, bf16[16,4224]{1,0:T(8,128)(2,1)S(1)}, u32[]{:S(2)}, u32[]{:S(2)}) collective-permute-start(bf16[16,4224]{1,0:T(8,128)(2,1)S(1)} %pad_maximum_fusion.refs_1_.refs_5_), channel_id=1, source_target_pairs={{0,4},{1,9},{2,6},{3,11},{4,0},{5,13},{6,2},{7,15},{8,12},{9,1},{1... | collective-permute-start | bytes 405512 | tf_op jit(solution)/shard_map/ppermute | solution.py:409
  16.4 6.6 %collective-permute-start.3 = (bf16[16,4224]{1,0:T(8,128)(2,1)S(1)}, bf16[16,4224]{1,0:T(8,128)(2,1)S(1)}, u32[]{:S(2)}, u32[]{:S(2)}) collective-permute-start(bf16[16,4224]{1,0:T(8,128)(2,1)S(1)} %pad_maximum_fusion.refs_1_.refs_5_), channel_id=1, source_target_pairs={{0,2},{1,3},{2,0},{3,1},{4,6},{5,7},{6,4},{7,5},{8,10},{9,11},{10,... | collective-permute-start | bytes 405512 | tf_op jit(solution)/shard_map/ppermute | solution.py:409
  32.8 5.2 %collective-permute-start.10 = (s16[144,512]{1,0:T(8,128)(2,1)S(1)}, s16[144,512]{1,0:T(8,128)(2,1)S(1)}, u32[]{:S(2)}, u32[]{:S(2)}) collective-permute-start(s16[144,512]{1,0:T(8,128)(2,1)S(1)} %get-tuple-element.14), channel_id=1, source_target_pairs={{0,2},{1,3},{2,0},{3,1},{4,6},{5,7},{6,4},{7,5},{8,10},{9,11},{10,... | collective-permute-start | bytes 442376 | tf_op jit(solution)/shard_map/ppermute | solution.py:409
  32.8 6.9 %collective-permute-start.11 = (s16[144,512]{1,0:T(8,128)(2,1)S(1)}, s16[144,512]{1,0:T(8,128)(2,1)S(1)}, u32[]{:S(2)}, u32[]{:S(2)}) collective-permute-start(s16[144,512]{1,0:T(8,128)(2,1)S(1)} %get-tuple-element.15), channel_id=1, source_target_pairs={{0,4},{1,9},{2,6},{3,11},{4,0},{5,13},{6,2},{7,15},{8,12},{9,1},{1... | collective-permute-start | bytes 442376 | tf_op jit(solution)/shard_map/ppermute | solution.py:409
  33.7 10.3 %collective-permute-start.12 = (s16[144,512]{1,0:T(8,128)(2,1)S(1)}, s16[144,512]{1,0:T(8,128)(2,1)S(1)}, u32[]{:S(2)}, u32[]{:S(2)}) collective-permute-start(s16[144,512]{1,0:T(8,128)(2,1)S(1)} %get-tuple-element.16), channel_id=1, source_target_pairs={{0,6},{1,11},{2,4},{3,9},{4,2},{5,15},{6,0},{7,13},{8,14},{9,3},{1... | collective-permute-start | bytes 442376 | tf_op jit(solution)/shard_map/ppermute | solution.py:409
  44.4 6.1 %collective-permute-start.13 = (s16[144,256]{1,0:T(8,128)(2,1)S(1)}, s16[144,256]{1,0:T(8,128)(2,1)S(1)}, u32[]{:S(2)}, u32[]{:S(2)}) collective-permute-start(s16[144,256]{1,0:T(8,128)(2,1)S(1)} %get-tuple-element.18), channel_id=1, source_target_pairs={{0,8},{1,5},{2,10},{3,7},{4,12},{5,1},{6,14},{7,3},{8,0},{9,13},{1... | collective-permute-start | bytes 221192 | tf_op jit(solution)/shard_map/ppermute | solution.py:409
  50.7 1.3 %collective-permute-start.14 = (bf16[4,4096]{1,0:T(4,128)(2,1)S(1)}, bf16[4,4096]{1,0:T(4,128)(2,1)S(1)}, u32[]{:S(2)}, u32[]{:S(2)}) collective-permute-start(bf16[4,4096]{1,0:T(4,128)(2,1)S(1)} %get-tuple-element.20), channel_id=1, source_target_pairs={{0,1},{1,0},{2,3},{3,2},{4,5},{5,4},{6,7},{7,6},{8,9},{9,8},{10,11... | collective-permute-start | bytes 98312 | tf_op jit(solution)/shard_map/ppermute | solution.py:400

commit v5 on v4

v5 whole, which is shorter than its diff:
```python
import functools
import math

import jax
import jax.numpy as jnp
from jax import lax
from jax.experimental import pallas as pl
from jax.experimental.pallas import tpu as pltpu
from jax.sharding import PartitionSpec as P

KEY_VALUE_HEADS = 4
LANES = 128
CORES = 2
FLOOR = -1e30
TILES = (1024, 512)
TAIL = 256
ATTEND_BYTES = 32 << 20
STAT_ROWS = 16
CHUNK_BLOCKS = 2
STEP = 2.0**15
MARGIN = 0.9998
F32 = jnp.float32
BF16 = jnp.bfloat16
I16 = jnp.int16
I32 = jnp.int32
VMEM = pl.BlockSpec(memory_space=pltpu.VMEM)
SMEM = pl.BlockSpec(memory_space=pltpu.SMEM)
SMALL = pltpu.CompilerParams(vmem_limit_bytes=8 << 20)


def encode(out, at, values, top, total):
    dims, width = values.shape
    largest = jnp.max(jnp.abs(values), axis=0, keepdims=True)
    exponent = jnp.floor(jnp.log2(jnp.maximum(largest, 1e-30))) + 1.0
    fixed = jnp.floor(values * (jnp.exp2(15.0 - exponent) * MARGIN) + 0.5)
    size = jnp.abs(top)
    level = jnp.zeros_like(top)
    scaled = top
    for i in range(1, 9):
        above = size >= STEP**i
        level = level + jnp.where(above, 1.0, 0.0)
        scaled = scaled * jnp.where(above, 1.0 / STEP, 1.0)
    a = jnp.floor(scaled)
    rest = (scaled - a) * STEP
    b = jnp.floor(rest)
    c = jnp.floor((rest - b) * STEP)
    logs = jnp.log2(total) * 1024.0
    la = jnp.floor(logs)
    lb = jnp.floor((logs - la) * STEP)
    row = lax.broadcasted_iota(I32, (STAT_ROWS, width), 0)
    stats = jnp.zeros((STAT_ROWS, width), F32)
    for i, part in enumerate((level, a, b, c, exponent, la, lb)):
        stats = jnp.where(row == i, part, stats)
    if not isinstance(at, int):
        at = pl.multiple_of(at, LANES)
    out[:dims, pl.ds(at, width)] = fixed.astype(I32).astype(I16)
    out[dims:, pl.ds(at, width)] = stats.astype(I32).astype(I16)


def decode_stats(ref, dims, at):
    stats = ref[dims:, at].astype(I32).astype(F32)

    def part(i):
        return stats[i : i + 1, :]

    top = part(1) + (part(2) + part(3) * (1.0 / STEP)) * (1.0 / STEP)
    for i in range(1, 9):
        top = top * jnp.where(part(0) >= i, STEP, 1.0)
    total = jnp.exp2((part(5) + part(6) * (1.0 / STEP)) * (1.0 / 1024.0))
    return top, total, jnp.exp2(part(4) - 15.0) * (1.0 / MARGIN)


def join_kernel(length, length_other, mine, queries_other, out):
    rows, half = mine.shape
    core = lax.axis_index("ctx") % CORES
    other = queries_other[:, pl.ds(pl.multiple_of(core * half, LANES), half)]
    out[:, :half] = jnp.concatenate([mine[...].astype(F32), other.astype(F32)], axis=0).astype(BF16)
    lane = lax.broadcasted_iota(I32, (CORES * rows, LANES), 1)
    row = lax.broadcasted_iota(I32, (CORES * rows, LANES), 0)
    count = jnp.where(row < rows, length[0], length_other[0])
    coded = jnp.where(lane == 0, count // LANES, jnp.where(lane == 1, count % LANES, 0))
    out[:, half:] = coded.astype(F32).astype(BF16)


def join(length, length_other, mine, queries_other):
    rows, half = mine.shape
    return pl.pallas_call(
        join_kernel,
        out_shape=jax.ShapeDtypeStruct((CORES * rows, half + LANES), BF16),
        in_specs=[SMEM, SMEM, VMEM, VMEM],
        out_specs=VMEM,
        compiler_params=SMALL,
    )(length, length_other, mine, queries_other)


def attend_kernel(sizes, *refs):
    own_rows, orders, group, kv_heads, sets, first, chosen = sizes
    start = refs[0]
    gathered = refs[1 : 1 + sets]
    new_keys, new_values, keys_a, keys_b, values_a, values_b = refs[1 + sets : 7 + sets]
    out, query_t, scores, sums, tops, totals = refs[7 + sets :]
    queries = gathered[first : first + chosen]
    chip_rows = CORES * own_rows
    slots = keys_a.shape[0]
    count = gathered[0].shape[0]
    tokens = min(count, CHUNK_BLOCKS * chip_rows)
    blocks = tokens // chip_rows
    set_blocks = count // chip_rows
    set_lanes = tokens * group
    lanes = chosen * set_lanes
    me = lax.axis_index("ctx")
    core, chip = me % CORES, me // CORES
    factor = math.log2(math.e) / math.sqrt(LANES)
    heads = range(kv_heads)

    steps = [jnp.where(core == 0, a // CORES, b // CORES) for a, b in zip(*orders)]

    def origin(block):
        off = jnp.zeros_like(block)
        for i, step in enumerate(steps):
            off = off ^ jnp.where((block >> i) & 1 == 1, step, 0)
        return chip ^ off

    found = [0.0, 0.0, 0.0]
    for i, ref in enumerate(gathered):
        rows = ref.shape[0]
        lane = lax.broadcasted_iota(I32, (rows, LANES), 1)
        row = lax.broadcasted_iota(I32, (rows, LANES), 0)
        place = origin(row // chip_rows + i * set_blocks)
        inside = row % chip_rows
        counts = jnp.where(lane == 0, float(LANES), 1.0) * ref[:, ref.shape[1] - LANES :].astype(F32)
        counts = jnp.where((inside % own_rows == 0) & (lane < 2), counts, 0.0)
        here = place == chip
        second = inside >= own_rows
        for k, wanted in enumerate((place < chip, here & ~second, here & second)):
            found[k] = found[k] + jnp.sum(jnp.where(wanted, counts, 0.0), axis=0, keepdims=True)
    row = lax.broadcasted_iota(I32, (8, LANES), 0)
    found = jnp.where(row == 0, found[0], jnp.where(row == 1, found[1], found[2]))
    found = jnp.sum(found, axis=1, keepdims=True).astype(I32)
    before, length = found[0, 0], [found[1, 0], found[2, 0]]
    begins = [
        before + jnp.where(core == 1, length[1], 0),
        before + jnp.where(core == 0, length[0], 0),
    ]
    limits = [jnp.clip(jnp.minimum(n, start[0] - at), 0, slots) for n, at in zip(length, begins)]

    def attend_chunk(chunk, carry):
        key_row = lax.broadcasted_iota(I32, (chip_rows, lanes), 0)
        lane = lax.broadcasted_iota(I32, (chip_rows, lanes), 1)
        part = key_row // own_rows
        key_id = (chip * CORES + (core ^ part)) * own_rows + key_row % own_rows
        inside = lane % chip_rows
        block = (lane // set_lanes + first) * set_blocks + lane % set_lanes // (group * chip_rows) + chunk * blocks
        token = (origin(block) * CORES + (core ^ (inside // own_rows))) * own_rows + inside % own_rows
        causal = key_id <= token
        nothing = jnp.zeros((16 - chip_rows % 16, LANES), F32)
        fresh_scores, fresh_values = [], []

        for h in heads:
            rows = pl.ds(pl.multiple_of(chunk * tokens, tokens), tokens)
            q = jnp.concatenate(
                [
                    ref[rows, (h * group + g) * LANES : (h * group + g + 1) * LANES].astype(F32)[b * chip_rows :][:chip_rows]
                    for ref in queries
                    for b in range(blocks)
                    for g in range(group)
                ],
                axis=0,
            )
            query_t[h] = q.T.astype(BF16)
            at = pl.multiple_of((core * kv_heads + h) * LANES, LANES)

            def padded_rows(ref):
                return jnp.concatenate([ref[:, pl.ds(at, LANES)].astype(F32), nothing], 0).astype(BF16)

            fresh_values.append(padded_rows(new_values))
            fresh_scores.append(jnp.dot(padded_rows(new_keys), query_t[h], preferred_element_type=F32)[:chip_rows] * factor)

        def fold(tile, combine):
            return combine(tile.reshape(tile.shape[0] // 8, 8, lanes), axis=0)

        def each_tile(limit, body, carry):
            base, rest = 0, limit
            for rows in TILES:
                count = rest // rows

                def whole(j, carry, rows=rows, base=base):
                    return body(pl.multiple_of(base + j * rows, TILES[-1]), rows, None, carry)

                carry = lax.fori_loop(0, count, whole, carry)
                base, rest = base + count * rows, rest - count * rows
            base = pl.multiple_of(base, TILES[-1])
            for rows, need in ((TAIL, (rest > 0) & (rest <= TAIL)), (TILES[-1], rest > TAIL)):
                carry = lax.cond(need, lambda c, rows=rows: body(base, rows, rest, c), lambda c: c, carry)
            return carry

        tn = (((0,), (0,)), ((), ()))

        for s, (keys, values) in enumerate(((keys_a, values_a), (keys_b, values_b))):
            limit = limits[s]
            seen = causal & (part == s)

            def columns(h, s=s):
                return pl.ds(pl.multiple_of((core * kv_heads * LANES if s else 0) + h * LANES, LANES), LANES)

            def first_pass(base, rows, filled, peaks, keys=keys, columns=columns):
                higher = []
                for h in heads:
                    tile = jnp.dot(keys[pl.ds(base, rows), columns(h)], query_t[h], preferred_element_type=F32) * factor
                    if filled is not None:
                        tile = jnp.where(lax.broadcasted_iota(I32, (rows, lanes), 0) < filled, tile, FLOOR)
                    scores[h, pl.ds(base, rows), :] = tile
                    higher.append(jnp.maximum(peaks[h], fold(tile, jnp.max)))
                return tuple(higher)

            peaks = each_tile(limit, first_pass, tuple(jnp.where(seen, x, FLOOR) for x in fresh_scores))
            top = [jnp.max(x, axis=0, keepdims=True) for x in peaks]
            masses = []
            for h in heads:
                weight = jnp.where(seen, jnp.exp2(fresh_scores[h] - top[h]), 0.0)
                padded = jnp.concatenate([weight, jnp.zeros((16 - chip_rows % 16, lanes), F32)], 0).astype(BF16)
                sums[s, h] = lax.dot_general(fresh_values[h], padded, tn, preferred_element_type=F32)
                masses.append(weight)

            def second_pass(base, rows, filled, masses, s=s, top=top, values=values, columns=columns):
                more = []
                for h in heads:
                    weight = jnp.exp2(scores[h, pl.ds(base, rows), :] - top[h])
                    if filled is not None:
                        weight = jnp.where(lax.broadcasted_iota(I32, (rows, lanes), 0) < filled, weight, 0.0)
                    sums[s, h] += lax.dot_general(
                        values[pl.ds(base, rows), columns(h)], weight.astype(BF16), tn, preferred_element_type=F32
                    )
                    more.append(masses[h] + fold(weight, jnp.sum))
                return tuple(more)

            masses = each_tile(limit, second_pass, tuple(masses))
            for h in heads:
                tops[s, h] = top[h]
                totals[s, h] = jnp.sum(masses[h], axis=0, keepdims=True)

        for h in heads:
            top_a, top_b = tops[0, h], tops[1, h]
            top = jnp.maximum(top_a, top_b)
            scale_a = jnp.exp2(top_a - top)
            scale_b = jnp.exp2(top_b - top)
            total = jnp.maximum(totals[0, h] * scale_a + totals[1, h] * scale_b, 1.0)
            merged = sums[0, h] * (scale_a / total) + sums[1, h] * (scale_b / total)
            width = group * chip_rows
            for i in range(chosen):
                for b in range(blocks):
                    at = i * set_lanes + b * width
                    cut = slice(at, at + width)
                    place = ((i * set_blocks + chunk * blocks + b) * kv_heads + h) * width
                    encode(out, place, merged[:, cut], top[:, cut], total[:, cut])
        return carry

    chunks = count // tokens
    if chunks == 1:
        attend_chunk(0, 0)
    else:
        lax.fori_loop(0, chunks, attend_chunk, 0)


def attend(start, gathered, chosen, fresh, cache, *, own_rows, orders):
    first, end = chosen
    count = gathered[0].shape[0]
    chip_rows = CORES * own_rows
    tokens = min(count, CHUNK_BLOCKS * chip_rows)
    slots = cache[0].shape[0]
    kv_heads = cache[0].shape[1] // LANES
    heads = gathered[0].shape[1] // LANES - 1
    group = heads // kv_heads
    lanes = (end - first) * tokens * group
    padded = -(-slots // TILES[-1]) * TILES[-1]
    sizes = (own_rows, orders, group, kv_heads, len(gathered), first, end - first)
    return pl.pallas_call(
        functools.partial(attend_kernel, sizes),
        out_shape=jax.ShapeDtypeStruct((LANES + STAT_ROWS, (end - first) * count * heads), I16),
        in_specs=[SMEM] + [VMEM] * (len(gathered) + 6),
        out_specs=VMEM,
        scratch_shapes=[
            pltpu.VMEM((kv_heads, LANES, lanes), BF16),
            pltpu.VMEM((kv_heads, padded, lanes), F32),
            pltpu.VMEM((2, kv_heads, LANES, lanes), F32),
            pltpu.VMEM((2, kv_heads, 1, lanes), F32),
            pltpu.VMEM((2, kv_heads, 1, lanes), F32),
        ],
        compiler_params=pltpu.CompilerParams(vmem_limit_bytes=ATTEND_BYTES),
    )(start, *gathered, *fresh, *cache)


def merged_part(refs, dims, at):
    stats = [decode_stats(ref, dims, at) for ref in refs]
    top = functools.reduce(jnp.maximum, [x[0] for x in stats])
    masses = [x[1] * jnp.exp2(x[0] - top) for x in stats]
    total = functools.reduce(jnp.add, masses)
    values = 0.0
    for ref, mass, (_, _, unit) in zip(refs, masses, stats):
        values = values + ref[:dims, at].astype(I32).astype(F32) * (mass / total * unit)
    return values, top, total


def merge_kernel(inputs, *refs):
    parts, outs = refs[:inputs], refs[inputs:]
    dims = parts[0].shape[0] - STAT_ROWS
    width = outs[0].shape[1]
    step = min(width, 2 * LANES)
    for i, out in reversed(list(enumerate(outs))):
        for at in range(0, width, step):
            encode(out, at, *merged_part(parts, dims, slice(i * width + at, i * width + at + step)))


def merge(parts, pieces):
    rows, width = parts[0].shape
    shape = jax.ShapeDtypeStruct((rows, width // pieces), I16)
    return pl.pallas_call(
        functools.partial(merge_kernel, len(parts)),
        out_shape=(shape,) * pieces,
        in_specs=[VMEM] * len(parts),
        out_specs=(VMEM,) * pieces,
        compiler_params=SMALL,
    )(*parts)


def finish_kernel(group, inputs, *refs):
    parts, (mine, other) = refs[:inputs], refs[inputs:]
    dims = parts[0].shape[0] - STAT_ROWS
    own_rows = mine.shape[0]
    chip_rows = CORES * own_rows
    width = group * chip_rows
    for h in range(parts[0].shape[1] // width):
        values, _, _ = merged_part(parts, dims, slice(h * width, (h + 1) * width))
        rows = values.T
        for g in range(group):
            at = (h * group + g) * dims
            tokens = rows[g * chip_rows : (g + 1) * chip_rows]
            mine[:, at : at + dims] = tokens[:own_rows].astype(BF16)
            other[:, at : at + dims] = tokens[own_rows:].astype(BF16)


def finish(parts, own_rows, group):
    rows, width = parts[0].shape
    shape = jax.ShapeDtypeStruct((own_rows, width // (CORES * own_rows) * (rows - STAT_ROWS)), BF16)
    return pl.pallas_call(
        functools.partial(finish_kernel, group, len(parts)),
        out_shape=(shape, shape),
        in_specs=[VMEM] * len(parts),
        out_specs=(VMEM, VMEM),
        compiler_params=SMALL,
    )(*parts)


def place_kernel(mine, theirs, out):
    half = mine.shape[1]
    core = lax.axis_index("ctx") % CORES
    out[:, pl.ds(pl.multiple_of(core * half, LANES), half)] = mine[...]
    out[:, pl.ds(pl.multiple_of((1 - core) * half, LANES), half)] = theirs[...]


def place(mine, theirs):
    rows, half = mine.shape
    return pl.pallas_call(
        place_kernel,
        out_shape=jax.ShapeDtypeStruct((rows, CORES * half), BF16),
        in_specs=[VMEM, VMEM],
        out_specs=VMEM,
        compiler_params=SMALL,
    )(mine, theirs)


def per_device(
    queries, cache_keys, cached_value_rows, new_keys, prompt_value_rows, cache_len, prompt_start
):
    width = lax.axis_size("ctx")
    own_rows = queries.shape[0]
    group = queries.shape[1] // cache_keys.shape[1]
    bits = [CORES << i for i in range((width // CORES).bit_length() - 1)]
    orders = (tuple(bits[-1:] + bits[:-1]), tuple(bits[-2:] + bits[:-2]))
    odd = len(bits) % 2
    stages = [(0,)] * odd + [(i, i + 1) for i in range(odd, len(bits), 2)]

    def swap(x):
        return lax.ppermute(x, "ctx", [(i, i ^ 1) for i in range(width)])

    def partners(stage):
        return [
            [sum(order[bit] for k, bit in enumerate(stage) if c >> k & 1) for order in orders]
            for c in range(1, 1 << len(stage))
        ]

    def exchange(x, distance):
        return lax.ppermute(x, "ctx", [(i, i ^ distance[i % CORES]) for i in range(width)])

    def own_half(x):
        half = x.shape[1] // CORES
        return lax.dynamic_slice_in_dim(x, core * half, half, 1)

    core = lax.axis_index("ctx") % CORES
    held = join(cache_len, swap(cache_len), own_half(queries), swap(queries))
    cache_keys, cached_value_rows, new_keys, prompt_value_rows, held = lax.optimization_barrier(
        (cache_keys, cached_value_rows, new_keys, prompt_value_rows, held)
    )
    fresh = [jnp.concatenate([x, swap(x)], axis=0) for x in (new_keys, prompt_value_rows)]
    cache = [y for x in (cache_keys, cached_value_rows) for y in (own_half(x), swap(x))]
    for stage in stages:
        gathered = [held] + [exchange(held, distance) for distance in partners(stage)]
        if stage != stages[-1]:
            held = jnp.concatenate(gathered, axis=0)
    half = len(gathered) // 2
    far, near = (
        attend(prompt_start, gathered, chosen, fresh, cache, own_rows=own_rows, orders=orders)
        for chosen in ((half, 2 * half), (0, half))
    )
    last = len(bits) - 1
    parts = [near, exchange(far, partners((last,))[0])]
    for stage in [(i - 1, i) if i else (i,) for i in range(last - 1, -1, -2)]:
        parts = merge(parts, 1 << len(stage))
        parts = [parts[0]] + [exchange(x, distance) for x, distance in zip(parts[1:], partners(stage))]
    mine, other = finish(parts, own_rows, group)
    return place(mine, swap(other))


def solution(mesh):
    return jax.shard_map(
        per_device,
        mesh=mesh,
        in_specs=(
            P(("groups", "ctx"), None),
            P(("groups", "ctx"), None),
            P(("groups", "ctx"), None),
            P(("groups", "ctx"), None),
            P(("groups", "ctx"), None),
            P(("groups", "ctx")),
            P("groups"),
        ),
        out_specs=P(("groups", "ctx"), None),
        check_vma=False,
    )
```

time: 52.2 us -> 45.3 us (0.87)
  waiting for transfers between devices: 22.7 us -> 14.7 us
  starting transfers between devices: 14.6 us -> 17 us
  Pallas kernels: 11.6 us -> 10.1 us
    ppermute x8, waiting for transfers between devices: 18.7 us -> 13.5 us  [exchange(): lax.ppermute(x, 'ctx', [(i, i ^ distance[i % CORES]) for i in range(width)])]
    ppermute x7, waiting for transfers between devices: 4.02 us -> 1.21 us  [swap(): return lax.ppermute(x, 'ctx', [(i, i ^ 1) for i in range(width)])]
    ppermute x8, starting transfers between devices: 12.8 us -> 15.3 us  [exchange(): lax.ppermute(x, 'ctx', [(i, i ^ distance[i % CORES]) for i in range(width)])]
    pallas_call x1 -> x2, Pallas kernels: 9.83 us -> 8.12 us  [attend(): pl.pallas_call(functools.partial(attend_kernel, sizes), out_shape=jax.Sha...]
  transfers between devices with their start and end apart: 15 -> 15, of which waited for: 10 -> 8; matrix products, arithmetic and copies ran while one was open for 4% -> 5% of each run, Pallas kernels for 1% -> 9%
where the time goes in v5:
time: 45.3 us; the launch traced here: 45.5 us
  starting transfers between devices  17 us (38%)
  waiting for transfers between devices  14.7 us (32%)
  Pallas kernels  10.1 us (22%)
  local copies, waits for them, and re-layouts  2.28 us (5%)
  between operations  1.41 us (3%)
    ppermute x8, starting transfers between devices, exchange(): lax.ppermute(x, 'ctx', [(i, i ^ distance[i % CORES]) for i in range(width)])  15.3 us
    ppermute x8, waiting for transfers between devices, exchange(): lax.ppermute(x, 'ctx', [(i, i ^ distance[i % CORES]) for i in range(width)])  13.5 us
    pallas_call x2, Pallas kernels, attend(): pl.pallas_call(functools.partial(attend_kernel, sizes), out_shape=jax.Sha...  8.12 us
    dynamic_slice x2, local copies, waits for them, and re-layouts, own_half(): return lax.dynamic_slice_in_dim(x, core * half, half, 1)  2.26 us
    ppermute x7, starting transfers between devices, swap(): return lax.ppermute(x, 'ctx', [(i, i ^ 1) for i in range(width)])  1.69 us
    ppermute x7, waiting for transfers between devices, swap(): return lax.ppermute(x, 'ctx', [(i, i ^ 1) for i in range(width)])  1.21 us
  transfers between devices with their start and end apart: 15, of which 8 were waited for; matrix products, arithmetic and copies ran while one was open for 5% of the time, Pallas kernels for 9%

profile of v5, /device:TPU:0, one launch (start us, length us, event | category | flops | bytes accessed | tf_op | source)
XLA Modules:
  0.0 45.5 jit_solution(17484877308710046122)
XLA Ops:
  0.0 0.5 collective-permute-start
  0.5 0.1 collective-permute-start.1
  0.5 0.8 %constant_dynamic-slice_fusion.2.mine = bf16[4,4096]{1,0:T(4,128)(2,1)S(1)} fusion(bf16[4,8192]{1,0:T(4,128)(2,1)} %param.7, s32[]{:T(128)S(6)} %select_n.15), kind=kLoop, calls=%fused_computation.6 | loop fusion | bytes 65540 | tf_op jit(solution)/shard_map/dynamic_slice | solution.py:397
  2.6 0.0 collective-permute-done.length_other
  2.6 0.0 collective-permute-done.1.queries_other
  2.6 0.7 %shard_map.73 = bf16[8,4224]{1,0:T(8,128)(2,1)S(1)} custom-call(s32[1]{0:T(128)S(6)} %copy.9.length, s32[1]{0:T(128)} %collective-permute-done.length_other, bf16[4,4096]{1,0:T(4,128)(2,1)S(1)} %constant_dynamic-slice_fusion.2.mine, bf16[4,8192]{1,0:T(4,128)(2,1)S(1)} %collective-permute-done.1.queries_other), custom_call_target="tpu_custom_call" | custom-call | tf_op jit(solution)/shard_map/pallas_call | solution.py:87
  3.3 0.5 %collective-permute-start.6 = (bf16[4,512]{1,0:T(4,128)(2,1)}, bf16[4,512]{1,0:T(4,128)(2,1)S(1)}, u32[]{:S(2)}, u32[]{:S(2)}) collective-permute-start(bf16[4,512]{1,0:T(4,128)(2,1)} %param.10), channel_id=1, source_target_pairs={{0,1},{1,0},{2,3},{3,2},{4,5},{5,4},{6,7},{7,6},{8,9},{9,8},{10,11... | collective-permute-start | bytes 12296 | tf_op jit(solution)/shard_map/ppermute | solution.py:384
  3.9 0.1 collective-permute-start.7
  3.9 4.0 %collective-permute-start.2 = (bf16[8,4224]{1,0:T(8,128)(2,1)S(1)}, bf16[8,4224]{1,0:T(8,128)(2,1)S(1)}, u32[]{:S(2)}, u32[]{:S(2)}) collective-permute-start(bf16[8,4224]{1,0:T(8,128)(2,1)S(1)} %shard_map.73), channel_id=1, source_target_pairs={{0,8},{1,5},{2,10},{3,7},{4,12},{5,1},{6,14},{7,3},{8,0},{9,13},{1... | collective-permute-start | bytes 202760 | tf_op jit(solution)/shard_map/ppermute | solution.py:393
  7.9 0.0 collective-permute-start.8
  8.0 0.5 %collective-permute-start.9 = (bf16[1536,512]{1,0:T(8,128)(2,1)}, bf16[1536,512]{1,0:T(8,128)(2,1)S(1)}, u32[]{:S(2)}, u32[]{:S(2)}) collective-permute-start(bf16[1536,512]{1,0:T(8,128)(2,1)} %param.9), channel_id=1, source_target_pairs={{0,1},{1,0},{2,3},{3,2},{4,5},{5,4},{6,7},{7,6},{8,9},{9,8},{10,11... | collective-permute-start | bytes 4718600 | tf_op jit(solution)/shard_map/ppermute | solution.py:384
  8.5 0.0 copy-start
  8.5 0.0 copy-start.1
  8.5 1.5 %constant_dynamic-slice_fusion = (bf16[1536,256]{1,0:T(8,128)(2,1)S(1)}, bf16[1536,256]{1,0:T(8,128)(2,1)S(1)}) fusion(bf16[1536,512]{1,0:T(8,128)(2,1)} %param.9, s32[]{:T(128)S(6)} %select_n.16, bf16[1536,512]{1,0:T(8,128)(2,1)} %param.8), kind=kLoop, calls=%fused_computation.4 | loop fusion | bytes 3145732 | tf_op jit(solution)/shard_map/dynamic_slice | solution.py:397
  10.0 0.2 collective-permute-done.2
  10.2 2.9 %collective-permute-start.5 = (bf16[16,4224]{1,0:T(8,128)(2,1)S(1)}, bf16[16,4224]{1,0:T(8,128)(2,1)S(1)}, u32[]{:S(2)}, u32[]{:S(2)}) collective-permute-start(bf16[16,4224]{1,0:T(8,128)(2,1)S(1)} %constant_dynamic-update-slice_fusion.refs_1_), channel_id=1, source_target_pairs={{0,6},{1,11},{2,4},{3,9},{4,2},{5,15},{6,0},{7,13},{8,14},{9,3},{1... | collective-permute-start | bytes 405512 | tf_op jit(solution)/shard_map/ppermute | solution.py:393
  13.1 0.0 collective-permute-done.6
  13.1 0.5 collective-permute-start.4
  13.6 0.0 collective-permute-done.7
  13.6 0.2 collective-permute-start.3
  13.8 0.0 copy-done
  13.8 0.0 copy-done.1
  13.8 3.8 %collective-permute-done.5.refs_4_ = bf16[16,4224]{1,0:T(8,128)(2,1)S(1)} collective-permute-done((bf16[16,4224]{1,0:T(8,128)(2,1)S(1)}, bf16[16,4224]{1,0:T(8,128)(2,1)S(1)}, u32[]{:S(2)}, u32[]{:S(2)}) %collective-permute-start.5) | collective-permute-done | bytes 135200 | tf_op jit(solution)/shard_map/ppermute | solution.py:393
  17.7 2.0 %collective-permute-done.4.refs_3_ = bf16[16,4224]{1,0:T(8,128)(2,1)S(1)} collective-permute-done((bf16[16,4224]{1,0:T(8,128)(2,1)S(1)}, bf16[16,4224]{1,0:T(8,128)(2,1)S(1)}, u32[]{:S(2)}, u32[]{:S(2)}) %collective-permute-start.4) | collective-permute-done | bytes 135200 | tf_op jit(solution)/shard_map/ppermute | solution.py:393
  19.7 0.5 %collective-permute-done.3.refs_2_ = bf16[16,4224]{1,0:T(8,128)(2,1)S(1)} collective-permute-done((bf16[16,4224]{1,0:T(8,128)(2,1)S(1)}, bf16[16,4224]{1,0:T(8,128)(2,1)S(1)}, u32[]{:S(2)}, u32[]{:S(2)}) %collective-permute-start.3) | collective-permute-done | bytes 135200 | tf_op jit(solution)/shard_map/ppermute | solution.py:393
  20.3 0.0 collective-permute-done.8.refs_8_
  20.3 0.0 collective-permute-done.9.refs_10_
  20.3 4.0 %shard_map.75 = s16[144,1024]{1,0:T(8,128)(2,1)S(1)} custom-call(s32[1]{0:T(128)S(6)} %copy.10.refs_0_, bf16[16,4224]{1,0:T(8,128)(2,1)S(1)} %constant_dynamic-update-slice_fusion.refs_1_, bf16[16,4224]{1,0:T(8,128)(2,1)S(1)} %collective-permute-done.3.refs_2_, bf16[16,4224]{1,0:T(8,128)(2,1)S(1)} %collective-permute-done.4.refs_3_, ...), custom_call_target="tpu_custom_call" | custom-call | tf_op jit(solution)/shard_map/pallas_call | solution.py:277
  24.2 3.2 %collective-permute-start.10 = (s16[144,1024]{1,0:T(8,128)(2,1)S(1)}, s16[144,1024]{1,0:T(8,128)(2,1)S(1)}, u32[]{:S(2)}, u32[]{:S(2)}) collective-permute-start(s16[144,1024]{1,0:T(8,128)(2,1)S(1)} %shard_map.75), channel_id=1, source_target_pairs={{0,4},{1,3},{2,6},{3,1},{4,0},{5,7},{6,2},{7,5},{8,12},{9,11},{10,... | collective-permute-start | bytes 884744 | tf_op jit(solution)/shard_map/ppermute | solution.py:393
  27.5 4.1 %shard_map.74.refs_0_ = s16[144,1024]{1,0:T(8,128)(2,1)S(1)} custom-call(s32[1]{0:T(128)S(6)} %copy.10.refs_0_, bf16[16,4224]{1,0:T(8,128)(2,1)S(1)} %constant_dynamic-update-slice_fusion.refs_1_, bf16[16,4224]{1,0:T(8,128)(2,1)S(1)} %collective-permute-done.3.refs_2_, bf16[16,4224]{1,0:T(8,128)(2,1)S(1)} %collective-permute-done.4.refs_3_, ...), custom_call_target="tpu_custom_call" | custom-call | tf_op jit(solution)/shard_map/pallas_call | solution.py:277
  31.6 0.5 %collective-permute-done.10.refs_1_ = s16[144,1024]{1,0:T(8,128)(2,1)S(1)} collective-permute-done((s16[144,1024]{1,0:T(8,128)(2,1)S(1)}, s16[144,1024]{1,0:T(8,128)(2,1)S(1)}, u32[]{:S(2)}, u32[]{:S(2)}) %collective-permute-start.10) | collective-permute-done | bytes 294944 | tf_op jit(solution)/shard_map/ppermute | solution.py:393
  32.2 0.4 shard_map.76
  32.6 3.0 %collective-permute-start.11 = (s16[144,256]{1,0:T(8,128)(2,1)S(1)}, s16[144,256]{1,0:T(8,128)(2,1)S(1)}, u32[]{:S(2)}, u32[]{:S(2)}) collective-permute-start(s16[144,256]{1,0:T(8,128)(2,1)S(1)} %get-tuple-element.22), channel_id=1, source_target_pairs={{0,8},{1,5},{2,10},{3,7},{4,12},{5,1},{6,14},{7,3},{8,0},{9,13},{1... | collective-permute-start | bytes 221192 | tf_op jit(solution)/shard_map/ppermute | solution.py:393
  35.6 0.0 collective-permute-start.12
  35.6 1.5 %collective-permute-start.13 = (s16[144,256]{1,0:T(8,128)(2,1)S(1)}, s16[144,256]{1,0:T(8,128)(2,1)S(1)}, u32[]{:S(2)}, u32[]{:S(2)}) collective-permute-start(s16[144,256]{1,0:T(8,128)(2,1)S(1)} %get-tuple-element.24), channel_id=1, source_target_pairs={{0,10},{1,13},{2,8},{3,15},{4,14},{5,9},{6,12},{7,11},{8,2},{9,5},... | collective-permute-start | bytes 221192 | tf_op jit(solution)/shard_map/ppermute | solution.py:393
  37.1 3.7 %collective-permute-done.11.refs_1_ = s16[144,256]{1,0:T(8,128)(2,1)S(1)} collective-permute-done((s16[144,256]{1,0:T(8,128)(2,1)S(1)}, s16[144,256]{1,0:T(8,128)(2,1)S(1)}, u32[]{:S(2)}, u32[]{:S(2)}) %collective-permute-start.11) | collective-permute-done | bytes 73760 | tf_op jit(solution)/shard_map/ppermute | solution.py:393
  40.8 0.0 collective-permute-done.12.refs_2_
  40.8 2.6 %collective-permute-done.13.refs_3_ = s16[144,256]{1,0:T(8,128)(2,1)S(1)} collective-permute-done((s16[144,256]{1,0:T(8,128)(2,1)S(1)}, s16[144,256]{1,0:T(8,128)(2,1)S(1)}, u32[]{:S(2)}, u32[]{:S(2)}) %collective-permute-start.13) | collective-permute-done | bytes 73760 | tf_op jit(solution)/shard_map/ppermute | solution.py:393
  43.4 0.2 shard_map.77
  43.6 0.1 collective-permute-start.14
  43.6 1.2 %collective-permute-done.14.theirs = bf16[4,4096]{1,0:T(4,128)(2,1)S(1)} collective-permute-done((bf16[4,4096]{1,0:T(4,128)(2,1)S(1)}, bf16[4,4096]{1,0:T(4,128)(2,1)S(1)}, u32[]{:S(2)}, u32[]{:S(2)}) %collective-permute-start.14) | collective-permute-done | bytes 32800 | tf_op jit(solution)/shard_map/ppermute | solution.py:384
  44.8 0.6 %shard_map.78 = bf16[4,8192]{1,0:T(4,128)(2,1)} custom-call(bf16[4,4096]{1,0:T(4,128)(2,1)S(1)} %get-tuple-element.25.mine, bf16[4,4096]{1,0:T(4,128)(2,1)S(1)} %collective-permute-done.14.theirs), custom_call_target="tpu_custom_call" | custom-call | tf_op jit(solution)/shard_map/pallas_call | solution.py:363
  (4 shorter events, 0.0 us)
Async XLA Ops:
  0.0 2.6 %collective-permute-start = (s32[1]{0:T(128)}, s32[1]{0:T(128)}, u32[]{:S(2)}, u32[]{:S(2)}) collective-permute-start(s32[1]{0:T(128)} %param.12), channel_id=1, source_target_pairs={{0,1},{1,0},{2,3},{3,2},{4,5},{5,4},{6,7},{7,6},{8,9},{9,8},{10,11... | collective-permute-start | bytes 20 | tf_op jit(solution)/shard_map/ppermute | solution.py:384
  0.5 2.1 %collective-permute-start.1 = (bf16[4,8192]{1,0:T(4,128)(2,1)}, bf16[4,8192]{1,0:T(4,128)(2,1)S(1)}, u32[]{:S(2)}, u32[]{:S(2)}) collective-permute-start(bf16[4,8192]{1,0:T(4,128)(2,1)} %param.7), channel_id=1, source_target_pairs={{0,1},{1,0},{2,3},{3,2},{4,5},{5,4},{6,7},{7,6},{8,9},{9,8},{10,11... | collective-permute-start | bytes 196616 | tf_op jit(solution)/shard_map/ppermute | solution.py:384
  3.3 9.8 %collective-permute-start.6 = (bf16[4,512]{1,0:T(4,128)(2,1)}, bf16[4,512]{1,0:T(4,128)(2,1)S(1)}, u32[]{:S(2)}, u32[]{:S(2)}) collective-permute-start(bf16[4,512]{1,0:T(4,128)(2,1)} %param.10), channel_id=1, source_target_pairs={{0,1},{1,0},{2,3},{3,2},{4,5},{5,4},{6,7},{7,6},{8,9},{9,8},{10,11... | collective-permute-start | bytes 12296 | tf_op jit(solution)/shard_map/ppermute | solution.py:384
  3.9 9.7 %collective-permute-start.7 = (bf16[4,512]{1,0:T(4,128)(2,1)}, bf16[4,512]{1,0:T(4,128)(2,1)S(1)}, u32[]{:S(2)}, u32[]{:S(2)}) collective-permute-start(bf16[4,512]{1,0:T(4,128)(2,1)} %param.11), channel_id=1, source_target_pairs={{0,1},{1,0},{2,3},{3,2},{4,5},{5,4},{6,7},{7,6},{8,9},{9,8},{10,11... | collective-permute-start | bytes 12296 | tf_op jit(solution)/shard_map/ppermute | solution.py:384
  3.9 6.3 %collective-permute-start.2 = (bf16[8,4224]{1,0:T(8,128)(2,1)S(1)}, bf16[8,4224]{1,0:T(8,128)(2,1)S(1)}, u32[]{:S(2)}, u32[]{:S(2)}) collective-permute-start(bf16[8,4224]{1,0:T(8,128)(2,1)S(1)} %shard_map.73), channel_id=1, source_target_pairs={{0,8},{1,5},{2,10},{3,7},{4,12},{5,1},{6,14},{7,3},{8,0},{9,13},{1... | collective-permute-start | bytes 202760 | tf_op jit(solution)/shard_map/ppermute | solution.py:393
  7.9 12.3 %collective-permute-start.8 = (bf16[1536,512]{1,0:T(8,128)(2,1)}, bf16[1536,512]{1,0:T(8,128)(2,1)S(1)}, u32[]{:S(2)}, u32[]{:S(2)}) collective-permute-start(bf16[1536,512]{1,0:T(8,128)(2,1)} %param.8), channel_id=1, source_target_pairs={{0,1},{1,0},{2,3},{3,2},{4,5},{5,4},{6,7},{7,6},{8,9},{9,8},{10,11... | collective-permute-start | bytes 4718600 | tf_op jit(solution)/shard_map/ppermute | solution.py:384
  8.0 12.3 %collective-permute-start.9 = (bf16[1536,512]{1,0:T(8,128)(2,1)}, bf16[1536,512]{1,0:T(8,128)(2,1)S(1)}, u32[]{:S(2)}, u32[]{:S(2)}) collective-permute-start(bf16[1536,512]{1,0:T(8,128)(2,1)} %param.9), channel_id=1, source_target_pairs={{0,1},{1,0},{2,3},{3,2},{4,5},{5,4},{6,7},{7,6},{8,9},{9,8},{10,11... | collective-permute-start | bytes 4718600 | tf_op jit(solution)/shard_map/ppermute | solution.py:384
  8.5 5.3 %copy-start = (bf16[4,512]{1,0:T(4,128)(2,1)S(1)}, bf16[4,512]{1,0:T(4,128)(2,1)}, u32[]{:S(2)}) copy-start(bf16[4,512]{1,0:T(4,128)(2,1)} %param.10) | copy-start | bytes 12292
  8.5 5.3 %copy-start.1 = (bf16[4,512]{1,0:T(4,128)(2,1)S(1)}, bf16[4,512]{1,0:T(4,128)(2,1)}, u32[]{:S(2)}) copy-start(bf16[4,512]{1,0:T(4,128)(2,1)} %param.11) | copy-start | bytes 12292
  10.2 7.5 %collective-permute-start.5 = (bf16[16,4224]{1,0:T(8,128)(2,1)S(1)}, bf16[16,4224]{1,0:T(8,128)(2,1)S(1)}, u32[]{:S(2)}, u32[]{:S(2)}) collective-permute-start(bf16[16,4224]{1,0:T(8,128)(2,1)S(1)} %constant_dynamic-update-slice_fusion.refs_1_), channel_id=1, source_target_pairs={{0,6},{1,11},{2,4},{3,9},{4,2},{5,15},{6,0},{7,13},{8,14},{9,3},{1... | collective-permute-start | bytes 405512 | tf_op jit(solution)/shard_map/ppermute | solution.py:393
  13.1 6.6 %collective-permute-start.4 = (bf16[16,4224]{1,0:T(8,128)(2,1)S(1)}, bf16[16,4224]{1,0:T(8,128)(2,1)S(1)}, u32[]{:S(2)}, u32[]{:S(2)}) collective-permute-start(bf16[16,4224]{1,0:T(8,128)(2,1)S(1)} %constant_dynamic-update-slice_fusion.refs_1_), channel_id=1, source_target_pairs={{0,4},{1,3},{2,6},{3,1},{4,0},{5,7},{6,2},{7,5},{8,12},{9,11},{10,... | collective-permute-start | bytes 405512 | tf_op jit(solution)/shard_map/ppermute | solution.py:393
  13.6 6.7 %collective-permute-start.3 = (bf16[16,4224]{1,0:T(8,128)(2,1)S(1)}, bf16[16,4224]{1,0:T(8,128)(2,1)S(1)}, u32[]{:S(2)}, u32[]{:S(2)}) collective-permute-start(bf16[16,4224]{1,0:T(8,128)(2,1)S(1)} %constant_dynamic-update-slice_fusion.refs_1_), channel_id=1, source_target_pairs={{0,2},{1,9},{2,0},{3,11},{4,6},{5,13},{6,4},{7,15},{8,10},{9,1},{1... | collective-permute-start | bytes 405512 | tf_op jit(solution)/shard_map/ppermute | solution.py:393
  24.2 7.9 %collective-permute-start.10 = (s16[144,1024]{1,0:T(8,128)(2,1)S(1)}, s16[144,1024]{1,0:T(8,128)(2,1)S(1)}, u32[]{:S(2)}, u32[]{:S(2)}) collective-permute-start(s16[144,1024]{1,0:T(8,128)(2,1)S(1)} %shard_map.75), channel_id=1, source_target_pairs={{0,4},{1,3},{2,6},{3,1},{4,0},{5,7},{6,2},{7,5},{8,12},{9,11},{10,... | collective-permute-start | bytes 884744 | tf_op jit(solution)/shard_map/ppermute | solution.py:393
  32.6 8.2 %collective-permute-start.11 = (s16[144,256]{1,0:T(8,128)(2,1)S(1)}, s16[144,256]{1,0:T(8,128)(2,1)S(1)}, u32[]{:S(2)}, u32[]{:S(2)}) collective-permute-start(s16[144,256]{1,0:T(8,128)(2,1)S(1)} %get-tuple-element.22), channel_id=1, source_target_pairs={{0,8},{1,5},{2,10},{3,7},{4,12},{5,1},{6,14},{7,3},{8,0},{9,13},{1... | collective-permute-start | bytes 221192 | tf_op jit(solution)/shard_map/ppermute | solution.py:393
  35.6 5.2 %collective-permute-start.12 = (s16[144,256]{1,0:T(8,128)(2,1)S(1)}, s16[144,256]{1,0:T(8,128)(2,1)S(1)}, u32[]{:S(2)}, u32[]{:S(2)}) collective-permute-start(s16[144,256]{1,0:T(8,128)(2,1)S(1)} %get-tuple-element.23), channel_id=1, source_target_pairs={{0,2},{1,9},{2,0},{3,11},{4,6},{5,13},{6,4},{7,15},{8,10},{9,1},{1... | collective-permute-start | bytes 221192 | tf_op jit(solution)/shard_map/ppermute | solution.py:393
  35.6 7.8 %collective-permute-start.13 = (s16[144,256]{1,0:T(8,128)(2,1)S(1)}, s16[144,256]{1,0:T(8,128)(2,1)S(1)}, u32[]{:S(2)}, u32[]{:S(2)}) collective-permute-start(s16[144,256]{1,0:T(8,128)(2,1)S(1)} %get-tuple-element.24), channel_id=1, source_target_pairs={{0,10},{1,13},{2,8},{3,15},{4,14},{5,9},{6,12},{7,11},{8,2},{9,5},... | collective-permute-start | bytes 221192 | tf_op jit(solution)/shard_map/ppermute | solution.py:393
  43.6 1.3 %collective-permute-start.14 = (bf16[4,4096]{1,0:T(4,128)(2,1)S(1)}, bf16[4,4096]{1,0:T(4,128)(2,1)S(1)}, u32[]{:S(2)}, u32[]{:S(2)}) collective-permute-start(bf16[4,4096]{1,0:T(4,128)(2,1)S(1)} %get-tuple-element.26), channel_id=1, source_target_pairs={{0,1},{1,0},{2,3},{3,2},{4,5},{5,4},{6,7},{7,6},{8,9},{9,8},{10,11... | collective-permute-start | bytes 98312 | tf_op jit(solution)/shard_map/ppermute | solution.py:384
